TPU v7x, 32 devices: a whole 2x2x4 slice. The times are simulated.
32 devices in a mesh: dp: 2 (over y), ctx: 4 (over x, core), tp: 4 (over z).
Axes of the slice: x: 2, y: 2, z: 4, core: 2. Of those that a mesh axis runs over, the one named last changes fastest.
Arguments:
- queries: bfloat16 [1024, 4096], P(('dp', 'ctx'), 'tp'), parts along dimension 0, may hold values from -6.5 to 6.5
- keys: bfloat16 [1024, 512], P(('dp', 'ctx'), 'tp'), parts along dimension 0, may hold values from -6.5 to 6.5
- values: bfloat16 [1024, 512], P(('dp', 'ctx'), 'tp'), parts along dimension 0, may hold values from -6 to 6
- out_weight: bfloat16 [4096, 2048], P('tp'), may hold values from -0.375 to 0.375
- norm_gain: float32 [2048], replicated, may hold values from 0.5 to 1.5
- expert_gate: bfloat16 [16, 2048, 384], P(('ctx', 'tp')), may hold values from -0.125 to 0.125
- expert_up: bfloat16 [16, 2048, 384], P(('ctx', 'tp')), may hold values from -0.125 to 0.125
- expert_down: bfloat16 [16, 384, 2048], P(('ctx', 'tp')), may hold values from -0.3125 to 0.3125
- expert_ids: int32 [1024, 8], P(('dp', 'ctx')), parts along dimension 0, may hold values from 0 to 15, as said below
- route_weights: float32 [1024, 8], P(('dp', 'ctx')), parts along dimension 0, may hold values from 0.05 to 1
Outputs:
- attended: bfloat16 [1024, 4096], P(('dp', 'ctx'), 'tp'), parts along dimension 0
- layer_out: bfloat16 [1024, 2048], P(('dp', 'ctx', 'tp')), parts along dimension 0
There are 2 independent parts, one for each index of `dp`. A program takes and returns all parts, laid end to end along the dimension named above; an argument that names none is the same for every part. Nothing has to cross between parts.
Inputs may be any that keep to these rules, and one draw needn't show every extreme that they name: `expert_ids`: each row names 8 different experts. In each aligned block of 128 rows (the rows of one ctx index) every expert is named by at least 32 and at most 96 rows, and one expert is named by exactly 96 rows in every block.
All inputs are finite; a program needn't handle non-finite values.
Results may differ from a plain program's by a relative error of at most 0.02.
Values may be sent and summed in bfloat16 or wider, within the bound.
No kernel may reach another device: no remote copies, remote signals or barrier semaphores. Data moves between devices by JAX's collectives and lax.ppermute only.
A program may use at most 64 MiB of HBM per device.

v0:
```python
import math

import jax
import jax.numpy as jnp
from jax import lax
from jax.sharding import PartitionSpec as P

HEAD = 128


def rms_scale(proj_rows, norm_gain):
    inverse = lax.rsqrt(jnp.mean(proj_rows * proj_rows, axis=1, keepdims=True) + 1e-06)
    return (proj_rows * inverse * norm_gain).astype(jnp.bfloat16)


def per_device(
    queries,
    keys,
    values,
    out_weight,
    norm_gain,
    expert_gate,
    expert_up,
    expert_down,
    expert_ids,
    route_weights,
):
    ctx_count = lax.axis_size("ctx")
    tp_count = lax.axis_size("tp")
    ctx_index = lax.axis_index("ctx")
    tp_index = lax.axis_index("tp")
    block_rows = queries.shape[0]
    local_heads = queries.shape[1] // HEAD
    kv_local = keys.shape[1] // HEAD
    group_size = local_heads // kv_local
    query_grid = queries.reshape(block_rows, kv_local, group_size, HEAD)
    query_pos = ctx_index * block_rows + jnp.arange(block_rows, dtype=jnp.int32)
    last_query = ctx_index * block_rows + block_rows - 1
    score_scale = HEAD ** (-0.5)

    def key_step(state_now, key_part, value_part, first_key):
        running_max, row_total, accum = state_now
        key_count = key_part.shape[0]
        key_grid = key_part.reshape(key_count, kv_local, HEAD)
        value_grid = value_part.reshape(key_count, kv_local, HEAD)
        scores = (
            jnp.einsum("tkgd,ukd->kgtu", query_grid, key_grid, preferred_element_type=jnp.float32)
            * score_scale
        )
        key_pos = first_key + jnp.arange(key_count, dtype=jnp.int32)
        allowed = key_pos[None, :] <= query_pos[:, None]
        new_max = jnp.maximum(running_max, jnp.max(jnp.where(allowed, scores, -1e30), axis=3))
        key_weights = jnp.where(allowed, jnp.exp(scores - new_max[..., None]), 0.0)
        rescale = jnp.exp(running_max - new_max)
        row_total = row_total * rescale + jnp.sum(key_weights, axis=3)
        update = jnp.einsum(
            "kgtu,ukd->kgtd",
            key_weights.astype(jnp.bfloat16),
            value_grid,
            preferred_element_type=jnp.float32,
        )
        accum = accum * rescale[..., None] + update
        return (new_max, row_total, accum)

    initial = (
        jnp.full((kv_local, group_size, block_rows), -1e30, jnp.float32),
        jnp.zeros((kv_local, group_size, block_rows), jnp.float32),
        jnp.zeros((kv_local, group_size, block_rows, HEAD), jnp.float32),
    )
    running_state = initial
    key_rows = lax.all_gather(keys, "ctx", axis=0, tiled=True)
    value_rows = lax.all_gather(values, "ctx", axis=0, tiled=True)
    key_count = key_rows.shape[0]
    sub_rows = math.gcd(key_count, 512)

    def sub_step(partial_value, sub_index):
        offset = sub_index * sub_rows
        key_part = lax.dynamic_slice_in_dim(key_rows, offset, sub_rows, 0)
        value_part = lax.dynamic_slice_in_dim(value_rows, offset, sub_rows, 0)
        updated = lax.cond(
            offset <= last_query,
            lambda state_now: key_step(state_now, key_part, value_part, offset),
            lambda state_now: state_now,
            partial_value,
        )
        return (updated, None)

    running_state, unused = lax.scan(
        sub_step, running_state, jnp.arange(key_count // sub_rows, dtype=jnp.int32)
    )
    final_max, row_total, accum = running_state
    attended = (
        (accum / row_total[..., None])
        .transpose(2, 0, 1, 3)
        .reshape(block_rows, local_heads * HEAD)
        .astype(jnp.bfloat16)
    )
    own_proj = lax.psum_scatter(
        jnp.dot(attended, out_weight, preferred_element_type=jnp.float32).astype(jnp.bfloat16),
        "tp",
        scatter_dimension=0,
        tiled=True,
    ).astype(jnp.float32)
    normed = lax.all_gather(rms_scale(own_proj, norm_gain), "tp", axis=0, tiled=True)
    top_count = expert_ids.shape[1]
    capacity = block_rows * top_count // (ctx_count * tp_count) * 3 // 2
    slot_total = ctx_count * capacity
    is_mine = expert_ids % tp_count == tp_index
    target_ctx = expert_ids // tp_count
    flat_target = target_ctx.reshape(-1)
    flat_mine = is_mine.reshape(-1)
    to_target = (
        flat_target[:, None] == jnp.arange(ctx_count, dtype=jnp.int32)[None, :]
    ) & flat_mine[:, None]
    running = jnp.cumsum(to_target.astype(jnp.int32), axis=0) - 1
    position = jnp.sum(jnp.where(to_target, running, 0), axis=1)
    slot_id = jnp.where(flat_mine, flat_target * capacity + position, -1).reshape(
        block_rows, top_count
    )
    slot_match = slot_id[:, :, None] == jnp.arange(slot_total, dtype=jnp.int32)[None, None, :]
    dispatch_map = jnp.any(slot_match, axis=1).astype(jnp.bfloat16)
    outgoing = jnp.einsum(
        "ts,td->sd", dispatch_map, normed, preferred_element_type=jnp.float32
    ).astype(jnp.bfloat16)
    outgoing = outgoing.reshape(ctx_count, capacity, normed.shape[1])
    route_share = route_weights / jnp.sum(route_weights, axis=1, keepdims=True)
    mix_weights = jnp.sum(jnp.where(slot_match, route_share[:, :, None], 0.0), axis=1)
    mix_high = mix_weights.astype(jnp.bfloat16)
    mix_low = (mix_weights - mix_high.astype(jnp.float32)).astype(jnp.bfloat16)
    arrived = lax.all_to_all(outgoing, "ctx", split_axis=0, concat_axis=0, tiled=True)
    source_count, item_count, features = arrived.shape
    flattened = arrived.reshape(source_count * item_count, features)
    gate_proj = jnp.dot(flattened, expert_gate[0], preferred_element_type=jnp.float32)
    up_proj = jnp.dot(flattened, expert_up[0], preferred_element_type=jnp.float32)
    activated = (jax.nn.silu(gate_proj) * up_proj).astype(jnp.bfloat16)
    expert_out = jnp.dot(activated, expert_down[0], preferred_element_type=jnp.float32).astype(
        jnp.bfloat16
    )
    expert_out = expert_out.reshape(source_count, item_count, features)
    returned = lax.all_to_all(expert_out, "ctx", split_axis=0, concat_axis=0, tiled=True)
    returned_flat = returned.reshape(slot_total, returned.shape[2])
    high_part = jnp.dot(mix_high, returned_flat, preferred_element_type=jnp.float32)
    expert_mix = lax.psum_scatter(
        (high_part + jnp.dot(mix_low, returned_flat, preferred_element_type=jnp.float32)).astype(
            jnp.bfloat16
        ),
        "tp",
        scatter_dimension=0,
        tiled=True,
    ).astype(jnp.float32)
    layer_out = (own_proj + expert_mix).astype(jnp.bfloat16)
    return (attended, layer_out)


def solution(mesh):
    in_specs = (
        P(("dp", "ctx"), "tp"),
        P(("dp", "ctx"), "tp"),
        P(("dp", "ctx"), "tp"),
        P("tp", None),
        P(),
        P(("ctx", "tp"), None, None),
        P(("ctx", "tp"), None, None),
        P(("ctx", "tp"), None, None),
        P(("dp", "ctx"), None),
        P(("dp", "ctx"), None),
    )
    out_specs = (P(("dp", "ctx"), "tp"), P(("dp", "ctx", "tp"), None))
    return jax.shard_map(
        per_device, mesh=mesh, in_specs=in_specs, out_specs=out_specs, check_vma=False
    )
```

profile of v0, /device:TPU:0, one launch (start us, length us, event | category | flops | bytes accessed | tf_op | source)
XLA Modules:
  0.0 151.5 jit_solution(13724455455928033941)
XLA Ops:
  7.2 6.8 %all_gather.10 = bf16[512,128]{1,0:T(8,128)(2,1)S(1)} all-gather(bf16[128,128]{1,0:T(8,128)(2,1)} %param.14), channel_id=1, replica_groups=mesh['dp'=2,'ctx'=4,'tp'=4] {'ctx'}, dimensions={0}, use_global_device_ids=true | all-gather | bytes 163840 | tf_op jit(solution)/shard_map/all_gather | solution.py:72
  14.1 5.8 %all_gather.9 = bf16[512,128]{1,0:T(8,128)(2,1)S(1)} all-gather(bf16[128,128]{1,0:T(8,128)(2,1)} %param.13), channel_id=1, replica_groups=mesh['dp'=2,'ctx'=4,'tp'=4] {'ctx'}, dimensions={0}, use_global_device_ids=true | all-gather | bytes 163840 | tf_op jit(solution)/shard_map/all_gather | solution.py:71
  19.9 2.7 %conditional.1 = ((f32[1,8,128]{2,1,0:T(8,128)S(1)}, f32[1,8,128,128]{3,2,1,0:T(8,128)S(1)})) conditional(s32[]{:T(128)} %convert_element_type.60, (f32[1,8,128]{2,1,0:T(8,128)S(1)}, f32[1,8,128,128]{3,2,1,0:T(8,128)S(1)}) %tuple.25, (s32[]{:T(128)}, s32[128]{0:T(128)S(1)}, bf16[128,1024]{1,0:T(8,128)(2,1)}, bf16[512,128]{1,0:T(8,128)(2,1)S(1)}, ...), branch_computations={%region_0.1_spmd, %region_1.4_spmd} | conditional | flops 274534528 | bytes 8177180 | solution.py:80
  20.0 1.4 fusion
  21.4 0.7 fusion.5
  22.2 0.4 fusion.4
  23.1 0.7 copy-done.2
  23.8 3.7 %convolution_convert_fusion.2 = bf16[128,2048]{1,0:T(8,128)(2,1)} fusion(bf16[128,1024]{1,0:T(8,128)(2,1)S(1)} %bitcast.105, bf16[1024,2048]{1,0:T(8,128)(2,1)} %param.15), kind=kOutput, calls=%fused_computation.31 | convolution fusion | flops 537133056 | bytes 4980736 | tf_op jit(solution)/shard_map/dot_general | solution.py:99
  28.2 1.1 reduce-window.6
  30.0 0.5 fusion.25
  30.5 20.3 %reduce-scatter.3.cloned.1.call-done = bf16[32,2048]{1,0:T(8,128)(2,1)} async-done(((bf16[128,2048]{1,0:T(8,128)(2,1)}), bf16[32,2048]{1,0:T(8,128)(2,1)}) %reduce-scatter.3.cloned.1.call-update) | async-done | bytes 131088 | tf_op jit(solution)/shard_map/reduce_scatter | solution.py:98
  50.8 1.0 fusion.40
  51.9 1.0 fusion.42
  52.9 15.8 %all_gather.11 = bf16[128,2048]{1,0:T(8,128)(2,1)S(1)} all-gather(bf16[32,2048]{1,0:T(8,128)(2,1)S(1)} %fusion.42), channel_id=1, replica_groups=mesh['dp'=2,'ctx'=4,'tp'=4] {'tp'}, dimensions={0}, use_global_device_ids=true | all-gather | bytes 655360 | tf_op jit(solution)/shard_map/all_gather | solution.py:104
  68.7 0.6 convolution_convert_fusion.1
  69.4 22.7 %all_to_all.10 = bf16[4,96,2048]{2,1,0:T(8,128)(2,1)S(1)} all-to-all(bf16[4,96,2048]{2,1,0:T(8,128)(2,1)S(1)} %bitcast.101), channel_id=1, replica_groups=mesh['dp'=2,'ctx'=4,'tp'=4] {'ctx'}, dimensions={0} | all-to-all | bytes 3145728 | tf_op jit(solution)/shard_map/all_to_all | solution.py:130
  92.1 1.8 %fusion.23 = f32[384,384]{1,0:T(8,128)} fusion(bf16[384,2048]{1,0:T(8,128)(2,1)S(1)} %bitcast.103, bf16[1,2048,384]{2,1,0:T(8,128)(2,1)S(1)} %copy-done.6), kind=kOutput, calls=%fused_computation.35 | convolution fusion | flops 603979776 | bytes 3735552 | tf_op jit(solution)/shard_map/dot_general | solution.py:133
  94.0 4.6 %convolution_convert_fusion = bf16[384,2048]{1,0:T(8,128)(2,1)} fusion(bf16[1,384,2048]{2,1,0:T(8,128)(2,1)S(1)} %copy-done, bf16[384,2048]{1,0:T(8,128)(2,1)S(1)} %bitcast.104, bf16[1,2048,384]{2,1,0:T(8,128)(2,1)} %param.18, f32[384,384]{1,0:T(8,128)} %fusion.23), kind=kOutput, calls=%fused_computation.27 | convolution fusion | flops 1209630720 | bytes 6881280 | tf_op jit(solution)/shard_map/dot_general | solution.py:136
  98.5 3.7 %all-to-all-start.1 = ((bf16[4,96,2048]{2,1,0:T(8,128)(2,1)}), bf16[4,96,2048]{2,1,0:T(8,128)(2,1)S(1)}, u32[]{:S(2)}, u32[]{:S(2)}) async-start(bf16[4,96,2048]{2,1,0:T(8,128)(2,1)} %bitcast.102), calls=%async_computation.2 | async-start | bytes 3145728 | tf_op jit(solution)/shard_map/all_to_all | solution.py:140
  102.4 0.5 select_reduce_fusion
  103.0 19.3 %all-to-all-done.1 = bf16[4,96,2048]{2,1,0:T(8,128)(2,1)S(1)} async-done(((bf16[4,96,2048]{2,1,0:T(8,128)(2,1)}), bf16[4,96,2048]{2,1,0:T(8,128)(2,1)S(1)}, u32[]{:S(2)}, u32[]{:S(2)}) %all-to-all-start.1) | async-done | bytes 1572896 | tf_op jit(solution)/shard_map/all_to_all | solution.py:140
  122.7 1.2 fusion.19
  124.0 19.1 %reduce-scatter.5.cloned.1.call-done = bf16[32,2048]{1,0:T(8,128)(2,1)} async-done(((bf16[128,2048]{1,0:T(8,128)(2,1)}), bf16[32,2048]{1,0:T(8,128)(2,1)}) %reduce-scatter.5.cloned.1.call-update) | async-done | bytes 131088 | tf_op jit(solution)/shard_map/reduce_scatter | solution.py:143
  143.1 1.6 %fusion.43 = bf16[32,2048]{1,0:T(8,128)(2,1)} fusion(bf16[32,2048]{1,0:T(8,128)(2,1)S(1)} %copy-done.1, bf16[32,2048]{1,0:T(8,128)(2,1)} %reduce-scatter.5.cloned.1.call-done), kind=kLoop, calls=%fused_computation.55 | loop fusion | flops 262144 | bytes 393216 | tf_op jit(solution)/shard_map/convert_element_type | solution.py:151
  (46 shorter events, 2.5 us)
Async XLA Ops:
  7.2 86.8 %copy-start = (bf16[1,384,2048]{2,1,0:T(8,128)(2,1)S(1)}, bf16[1,384,2048]{2,1,0:T(8,128)(2,1)}, u32[]{:S(2)}) copy-start(bf16[1,384,2048]{2,1,0:T(8,128)(2,1)} %param.19) | copy-start | bytes 4718596
  7.2 43.7 %reduce-scatter.3.cloned.1.call-start = ((), (), s32[]{:S(2)}) async-start(), calls=%async_computation.4 | async-start | bytes 655360 | tf_op jit(solution)/shard_map/reduce_scatter | solution.py:98
  23.1 0.7 copy-start.2
  23.8 3.8 %copy-start.5 = (s32[128,8]{0,1:T(8,128)S(1)}, s32[128,8]{0,1:T(8,128)}, u32[]{:S(2)}) copy-start(s32[128,8]{0,1:T(8,128)} %param.20) | copy-start | bytes 12292
  27.5 24.4 %copy-start.4 = (f32[2048]{0:T(1024)S(1)}, f32[2048]{0:T(1024)}, u32[]{:S(2)}) copy-start(f32[2048]{0:T(1024)} %param.16) | copy-start | bytes 24580
  69.4 22.8 %copy-start.6 = (bf16[1,2048,384]{2,1,0:T(8,128)(2,1)S(1)}, bf16[1,2048,384]{2,1,0:T(8,128)(2,1)}, u32[]{:S(2)}) copy-start(bf16[1,2048,384]{2,1,0:T(8,128)(2,1)} %param.17) | copy-start | bytes 4718596
  98.5 3.8 %copy-start.3 = (f32[128,8]{0,1:T(8,128)S(1)}, f32[128,8]{0,1:T(8,128)}, u32[]{:S(2)}) copy-start(f32[128,8]{0,1:T(8,128)} %param.21) | copy-start | bytes 12292
  98.5 23.7 %all-to-all-start.1 = ((bf16[4,96,2048]{2,1,0:T(8,128)(2,1)}), bf16[4,96,2048]{2,1,0:T(8,128)(2,1)S(1)}, u32[]{:S(2)}, u32[]{:S(2)}) async-start(bf16[4,96,2048]{2,1,0:T(8,128)(2,1)} %bitcast.102), calls=%async_computation.2 | async-start | bytes 3145728 | tf_op jit(solution)/shard_map/all_to_all | solution.py:140
  102.2 40.9 %reduce-scatter.5.cloned.1.call-start = ((), (), s32[]{:S(2)}) async-start(), calls=%async_computation.5 | async-start | bytes 655360 | tf_op jit(solution)/shard_map/reduce_scatter | solution.py:143
  122.7 20.4 %copy-start.1 = (bf16[32,2048]{1,0:T(8,128)(2,1)S(1)}, bf16[32,2048]{1,0:T(8,128)(2,1)}, u32[]{:S(2)}) copy-start(bf16[32,2048]{1,0:T(8,128)(2,1)} %reduce-scatter.3.cloned.1.call-done) | copy-start | bytes 393220
Sparse Core Ops, SparseCore 0:
  27.7 23.1 reduce-scatter.2
  124.1 18.9 reduce-scatter.4
where the time goes:
time: 152 us
  waiting for transfers between devices  58.8 us (39%)
  blocking collectives  51.2 us (34%)
  matrix products  14.6 us (10%)
  between operations  14.2 us (9%)
  other arithmetic  7.06 us (5%)
  starting transfers between devices  3.77 us (2%)
  local copies, waits for them, and re-layouts  1.87 us (1%)
    all_to_all x1, blocking collectives, per_device(): lax.all_to_all(outgoing, 'ctx', split_axis=0, concat_axis=0, tiled=True)  22.7 us
    reduce_scatter x1, waiting for transfers between devices, per_device(): lax.psum_scatter(jnp.dot(attended, out_weight, preferred_element_type=jnp...  20.3 us
    all_to_all x1, waiting for transfers between devices, per_device(): lax.all_to_all(expert_out, 'ctx', split_axis=0, concat_axis=0, tiled=True)  19.3 us
    reduce_scatter x1, waiting for transfers between devices, per_device(): lax.psum_scatter((high_part + jnp.dot(mix_low, returned_flat, preferred_e...  19.1 us
    all_gather x1, blocking collectives, per_device(): lax.all_gather(rms_scale(own_proj, norm_gain), 'tp', axis=0, tiled=True)  15.8 us
    all_gather x1, blocking collectives, per_device(): value_rows = lax.all_gather(values, 'ctx', axis=0, tiled=True)  6.82 us
    all_gather x1, blocking collectives, per_device(): key_rows = lax.all_gather(keys, 'ctx', axis=0, tiled=True)  5.8 us
    dot_general x1, matrix products, per_device(): jnp.dot(activated, expert_down[0], preferred_element_type=jnp.float32)  4.57 us
  transfers between devices with their start and end apart: 3, of which 3 were waited for; matrix products, arithmetic and copies ran while one was open for 2% of the time, Pallas kernels for 0%

commit v1 on v0

--- a/solution.py
+++ b/solution.py
@@ -13,7 +13,7 @@
     return (proj_rows * inverse * norm_gain).astype(jnp.bfloat16)
 
 
-def per_device(
+def routed_plan(
     queries,
     keys,
     values,
@@ -152,6 +152,115 @@
     return (attended, layer_out)
 
 
+def swap(rows, axis, offset):
+    count = lax.axis_size(axis)
+    return lax.ppermute(rows, axis, [(i, i ^ offset) for i in range(count)])
+
+
+def dense_plan(
+    queries,
+    keys,
+    values,
+    out_weight,
+    norm_gain,
+    expert_gate,
+    expert_up,
+    expert_down,
+    expert_ids,
+    route_weights,
+):
+    f32, bf16 = jnp.float32, jnp.bfloat16
+    ctx_count = lax.axis_size("ctx")
+    tp_count = lax.axis_size("tp")
+    ctx_index = lax.axis_index("ctx")
+    tp_index = lax.axis_index("tp")
+    block_rows = queries.shape[0]
+    local_heads = queries.shape[1] // HEAD
+    kv_local = keys.shape[1] // HEAD
+    group_size = local_heads // kv_local
+    piece_rows = block_rows // tp_count
+    features = out_weight.shape[1]
+    expert_count = ctx_count * tp_count
+
+    own_kv = jnp.stack([keys, values])
+    kv = [own_kv] + [swap(own_kv, "ctx", d) for d in range(1, ctx_count)]
+
+    share = route_weights / jnp.sum(route_weights, axis=1, keepdims=True)
+    chosen = expert_ids[:, :, None] == jnp.arange(expert_count, dtype=jnp.int32)[None, None, :]
+    mix = jnp.sum(jnp.where(chosen, share[:, :, None], 0.0), axis=1)
+    mixes = [mix] + [swap(mix, "ctx", d) for d in range(1, ctx_count)]
+    my_expert = ctx_index * tp_count + tp_index
+    my_mix = [lax.dynamic_slice_in_dim(m, my_expert, 1, 1) for m in mixes]
+
+    query_grid = queries.reshape(block_rows, kv_local, group_size, HEAD)
+    key_grid = jnp.concatenate([b[0] for b in kv]).reshape(-1, kv_local, HEAD)
+    value_grid = jnp.concatenate([b[1] for b in kv]).reshape(-1, kv_local, HEAD)
+    row = jnp.arange(block_rows, dtype=jnp.int32)
+    allowed = jnp.concatenate(
+        [row[None, :] <= row[:, None]]
+        + [
+            jnp.broadcast_to((ctx_index ^ d) < ctx_index, (block_rows, block_rows))
+            for d in range(1, ctx_count)
+        ],
+        axis=1,
+    )
+    scores = jnp.einsum(
+        "tkgd,ukd->kgtu", query_grid, key_grid, preferred_element_type=f32
+    ) * HEAD ** (-0.5)
+    scores = jnp.where(allowed, scores, -1e30)
+    weights = jnp.exp(scores - jnp.max(scores, axis=3, keepdims=True))
+    total = jnp.sum(weights, axis=3, keepdims=True)
+    accum = jnp.einsum(
+        "kgtu,ukd->kgtd", weights.astype(bf16), value_grid, preferred_element_type=f32
+    )
+    attended = (
+        (accum / total).transpose(2, 0, 1, 3).reshape(block_rows, local_heads * HEAD).astype(bf16)
+    )
+
+    partial = jnp.dot(attended, out_weight, preferred_element_type=f32).astype(bf16)
+
+    def piece_of(d):
+        return lax.dynamic_slice_in_dim(partial, (tp_index ^ d) * piece_rows, piece_rows, 0)
+
+    own_proj = piece_of(0).astype(f32)
+    for d in (2, 3, 1):
+        own_proj = own_proj + swap(piece_of(d), "tp", d).astype(f32)
+    normed = rms_scale(own_proj, norm_gain)
+
+    def expert(tokens, mix_rows):
+        gate_proj = jnp.dot(tokens, expert_gate[0], preferred_element_type=f32)
+        up_proj = jnp.dot(tokens, expert_up[0], preferred_element_type=f32)
+        activated = (jax.nn.silu(gate_proj) * up_proj).astype(bf16)
+        return jnp.dot(activated, expert_down[0], preferred_element_type=f32) * mix_rows
+
+    pieces = [normed] + [swap(normed, "tp", d) for d in (1, 2, 3)]
+    sums = []
+    for d, piece in enumerate(pieces):
+        far = swap(piece, "ctx", 2)
+        near = swap(jnp.stack([piece, far]), "ctx", 1)
+        tokens = jnp.concatenate([piece, near[0], far, near[1]])
+        row_start = (tp_index ^ d) * piece_rows
+        mix_rows = jnp.concatenate(
+            [lax.dynamic_slice_in_dim(m, row_start, piece_rows, 0) for m in my_mix]
+        )
+        out = expert(tokens, mix_rows).reshape(ctx_count, piece_rows, features)
+        got = swap(jnp.stack([out[1], out[3]]).astype(bf16), "ctx", 1).astype(f32)
+        far_sum = swap((out[2] + got[1]).astype(bf16), "ctx", 2).astype(f32)
+        sums.append(out[0] + got[0] + far_sum)
+    expert_mix = sums[0]
+    for d in (2, 3, 1):
+        expert_mix = expert_mix + swap(sums[d].astype(bf16), "tp", d).astype(f32)
+    return (attended, (own_proj + expert_mix).astype(bf16))
+
+
+def per_device(*arguments):
+    ctx_count, tp_count = lax.axis_size("ctx"), lax.axis_size("tp")
+    top_count = arguments[8].shape[1]
+    if ctx_count == 4 and tp_count == 4 and ctx_count * tp_count <= 2 * top_count:
+        return dense_plan(*arguments)
+    return routed_plan(*arguments)
+
+
 def solution(mesh):
     in_specs = (
         P(("dp", "ctx"), "tp"),

time: 152 us -> 113 us (0.74)
  blocking collectives: 51.2 us -> 0 us
  starting transfers between devices: 3.77 us -> 26.4 us
  waiting for transfers between devices: 58.8 us -> 40.9 us
  between operations: 14.2 us -> 1.16 us
  matrix products: 14.6 us -> 24 us
  local copies, waits for them, and re-layouts: 1.87 us -> 7.89 us
  other arithmetic: 7.06 us -> 11.9 us
    ppermute x0 -> x31, waiting for transfers between devices: none -> 40.9 us  [swap(): return lax.ppermute(rows, axis, [(i, i ^ offset) for i in range(count)])]
    reduce_scatter x2 -> x0, waiting for transfers between devices: 39.4 us -> none  [the longest x1 20.3 us: per_device(): lax.psum_scatter(jnp.dot(attended, out_weight, preferred_element_type=jnp...]
    all_gather x3 -> x0, blocking collectives: 28.5 us -> none  [the longest x1 15.8 us: per_device(): lax.all_gather(rms_scale(own_proj, norm_gain), 'tp', axis=0, tiled=True)]
    ppermute x0 -> x31, starting transfers between devices: none -> 26.4 us  [swap(): return lax.ppermute(rows, axis, [(i, i ^ offset) for i in range(count)])]
    all_to_all x1 -> x0, blocking collectives: 22.7 us -> none  [per_device(): lax.all_to_all(outgoing, 'ctx', split_axis=0, concat_axis=0, tiled=True)]
    all_to_all x1 -> x0, waiting for transfers between devices: 19.3 us -> none  [per_device(): lax.all_to_all(expert_out, 'ctx', split_axis=0, concat_axis=0, tiled=True)]
    dot_general x8 -> x11, matrix products: 14.6 us -> 24 us  [the longest x4 14 us: expert(): jnp.dot(activated, expert_down[0], preferred_element_type=f32) * mix_rows]
    unnamed x16 -> x53, local copies, waits for them, and re-layouts: 0.87 us -> 5.24 us
  transfers between devices with their start and end apart: 3 -> 31, of which waited for: 3 -> 13; matrix products, arithmetic and copies ran while one was open for 2% -> 30% of each run, Pallas kernels for 0% -> 0%
where the time goes in v1:
time: 113 us; the launch traced here: 112 us
  waiting for transfers between devices  40.9 us (36%)
  starting transfers between devices  26.4 us (23%)
  matrix products  24 us (21%)
  other arithmetic  11.9 us (11%)
  local copies, waits for them, and re-layouts  7.89 us (7%)
  between operations  1.16 us (1%)
    ppermute x31, waiting for transfers between devices, swap(): return lax.ppermute(rows, axis, [(i, i ^ offset) for i in range(count)])  40.9 us
    ppermute x31, starting transfers between devices, swap(): return lax.ppermute(rows, axis, [(i, i ^ offset) for i in range(count)])  26.4 us
    dot_general x4, matrix products, expert(): jnp.dot(activated, expert_down[0], preferred_element_type=f32) * mix_rows  14 us
    dot_general x4, matrix products, expert(): up_proj = jnp.dot(tokens, expert_up[0], preferred_element_type=f32)  7.37 us
    unnamed x53, local copies, waits for them, and re-layouts  5.24 us
    another operation x5, other arithmetic, dense_plan(): near = swap(jnp.stack([piece, far]), 'ctx', 1)  2.37 us
  transfers between devices with their start and end apart: 31, of which 13 were waited for; matrix products, arithmetic and copies ran while one was open for 30% of the time, Pallas kernels for 0%

profile of v1, /device:TPU:0, one launch (start us, length us, event | category | flops | bytes accessed | tf_op | source)
XLA Modules:
  0.0 112.3 jit_solution(682063774520496630)
XLA Ops:
  1.5 2.4 %collective-permute-start.2 = (bf16[2,128,128]{2,1,0:T(8,128)(2,1)S(1)}, bf16[2,128,128]{2,1,0:T(8,128)(2,1)S(1)}, u32[]{:S(2)}, u32[]{:S(2)}) collective-permute-start(bf16[2,128,128]{2,1,0:T(8,128)(2,1)S(1)} %pad_maximum_fusion.24), channel_id=1, source_target_pairs={{0,12},{4,8},{8,4},{12,0},{1,13},{5,9},{9,5},{13,1},{2,14},{6,10},... | collective-permute-start | bytes 196616 | tf_op jit(solution)/shard_map/ppermute | solution.py:157
  16.8 1.6 %collective-permute-start.5 = (bf16[32,2048]{1,0:T(8,128)(2,1)S(1)}, bf16[32,2048]{1,0:T(8,128)(2,1)S(1)}, u32[]{:S(2)}, u32[]{:S(2)}) collective-permute-start(bf16[32,2048]{1,0:T(8,128)(2,1)S(1)} %get-tuple-element.17), channel_id=1, source_target_pairs={{0,1},{1,0},{2,3},{3,2},{4,5},{5,4},{6,7},{7,6},{8,9},{9,8},{10,11... | collective-permute-start | bytes 393224 | tf_op jit(solution)/shard_map/ppermute | solution.py:157
  18.4 2.5 %collective-permute-start.4 = (bf16[32,2048]{1,0:T(8,128)(2,1)S(1)}, bf16[32,2048]{1,0:T(8,128)(2,1)S(1)}, u32[]{:S(2)}, u32[]{:S(2)}) collective-permute-start(bf16[32,2048]{1,0:T(8,128)(2,1)S(1)} %get-tuple-element.18), channel_id=1, source_target_pairs={{0,3},{1,2},{2,1},{3,0},{4,7},{5,6},{6,5},{7,4},{8,11},{9,10},{10,... | collective-permute-start | bytes 393224 | tf_op jit(solution)/shard_map/ppermute | solution.py:157
  21.8 6.2 %collective-permute-done.4 = bf16[32,2048]{1,0:T(8,128)(2,1)S(1)} collective-permute-done((bf16[32,2048]{1,0:T(8,128)(2,1)S(1)}, bf16[32,2048]{1,0:T(8,128)(2,1)S(1)}, u32[]{:S(2)}, u32[]{:S(2)}) %collective-permute-start.4) | collective-permute-done | bytes 131104 | tf_op jit(solution)/shard_map/ppermute | solution.py:157
  28.0 4.3 %collective-permute-done.3 = bf16[32,2048]{1,0:T(8,128)(2,1)S(1)} collective-permute-done((bf16[32,2048]{1,0:T(8,128)(2,1)S(1)}, bf16[32,2048]{1,0:T(8,128)(2,1)S(1)}, u32[]{:S(2)}, u32[]{:S(2)}) %collective-permute-start.3) | collective-permute-done | bytes 131104 | tf_op jit(solution)/shard_map/ppermute | solution.py:157
  34.2 2.7 %collective-permute-start.19 = (bf16[32,2048]{1,0:T(8,128)(2,1)S(1)}, bf16[32,2048]{1,0:T(8,128)(2,1)S(1)}, u32[]{:S(2)}, u32[]{:S(2)}) collective-permute-start(bf16[32,2048]{1,0:T(8,128)(2,1)S(1)} %multiply_convert_fusion), channel_id=1, source_target_pairs={{0,3},{1,2},{2,1},{3,0},{4,7},{5,6},{6,5},{7,4},{8,11},{9,10},{10,... | collective-permute-start | bytes 393224 | tf_op jit(solution)/shard_map/ppermute | solution.py:157
  37.8 2.8 %collective-permute-done.25 = bf16[32,2048]{1,0:T(8,128)(2,1)S(1)} collective-permute-done((bf16[32,2048]{1,0:T(8,128)(2,1)S(1)}, bf16[32,2048]{1,0:T(8,128)(2,1)S(1)}, u32[]{:S(2)}, u32[]{:S(2)}) %collective-permute-start.25) | collective-permute-done | bytes 131104 | tf_op jit(solution)/shard_map/ppermute | solution.py:157
  41.2 2.3 %collective-permute-done.19 = bf16[32,2048]{1,0:T(8,128)(2,1)S(1)} collective-permute-done((bf16[32,2048]{1,0:T(8,128)(2,1)S(1)}, bf16[32,2048]{1,0:T(8,128)(2,1)S(1)}, u32[]{:S(2)}, u32[]{:S(2)}) %collective-permute-start.19) | collective-permute-done | bytes 131104 | tf_op jit(solution)/shard_map/ppermute | solution.py:157
  43.9 4.6 %collective-permute-done.13 = bf16[32,2048]{1,0:T(8,128)(2,1)S(1)} collective-permute-done((bf16[32,2048]{1,0:T(8,128)(2,1)S(1)}, bf16[32,2048]{1,0:T(8,128)(2,1)S(1)}, u32[]{:S(2)}, u32[]{:S(2)}) %collective-permute-start.13) | collective-permute-done | bytes 131104 | tf_op jit(solution)/shard_map/ppermute | solution.py:157
  50.9 2.6 %collective-permute-done.14 = bf16[32,2048]{1,0:T(8,128)(2,1)S(1)} collective-permute-done((bf16[32,2048]{1,0:T(8,128)(2,1)S(1)}, bf16[32,2048]{1,0:T(8,128)(2,1)S(1)}, u32[]{:S(2)}, u32[]{:S(2)}) %collective-permute-start.14) | collective-permute-done | bytes 131104 | tf_op jit(solution)/shard_map/ppermute | solution.py:157
  56.7 3.6 %fusion.119 = (bf16[128,2048]{1,0:T(8,128)(2,1)}, f32[128,2048]{1,0:T(8,128)}) fusion(f32[128]{0:T(128)S(1)} %maximum_bitcast_fusion.4, bf16[1,384,2048]{2,1,0:T(8,128)(2,1)S(1)} %copy-done, f32[128,384]{1,0:T(8,128)} %fusion.16, bf16[1,2048,384]{2,1,0:T(8,128)(2,1)} %param.15, bf16[32,2048]{1,0:T(8,128)(2,1)} %copy-done.17, ...), kind=kOutput, calls=%fused_computation.163 | convolution fusion | flops 405569536 | bytes 5440000 | tf_op jit(solution)/shard_map/dot_general | solution.py:234
  64.5 3.5 %fusion.122 = (bf16[128,2048]{1,0:T(8,128)(2,1)S(1)}, f32[128,2048]{1,0:T(8,128)}) fusion(f32[128]{0:T(128)S(1)} %maximum_bitcast_fusion.7, bf16[1,384,2048]{2,1,0:T(8,128)(2,1)S(1)} %copy-done, f32[128,384]{1,0:T(8,128)} %fusion.10, bf16[1,2048,384]{2,1,0:T(8,128)(2,1)} %param.15, bf16[32,2048]{1,0:T(8,128)(2,1)} %copy-done.19, ...), kind=kOutput, calls=%fused_computation.164 | convolution fusion | flops 405569536 | bytes 5440000 | tf_op jit(solution)/shard_map/dot_general | solution.py:234
  69.1 2.6 %fusion.12 = f32[128,384]{1,0:T(8,128)} fusion(bf16[1,2048,384]{2,1,0:T(8,128)(2,1)} %param.16, bf16[32,2048]{1,0:T(8,128)(2,1)S(1)} %get-tuple-element.22, bf16[32,2048]{1,0:T(8,128)(2,1)S(1)} %copy-done.12, bf16[32,2048]{1,0:T(8,128)(2,1)S(1)} %get-tuple-element.21, bf16[32,2048]{1,0:T(8,128)(2,1)S(1)} %copy-done.6), kind=kOutput, calls=%fused_computation.15 | convolution fusion | flops 203423744 | bytes 2293760 | tf_op jit(solution)/shard_map/dot_general | solution.py:232
  71.7 3.4 %fusion.125 = (bf16[128,2048]{1,0:T(8,128)(2,1)}, f32[128,2048]{1,0:T(8,128)}) fusion(f32[128]{0:T(128)S(1)} %maximum_bitcast_fusion.6, bf16[1,384,2048]{2,1,0:T(8,128)(2,1)S(1)} %copy-done, f32[128,384]{1,0:T(8,128)} %fusion.12, bf16[1,2048,384]{2,1,0:T(8,128)(2,1)} %param.15, bf16[32,2048]{1,0:T(8,128)(2,1)S(1)} %get-tuple-element.22, ...), kind=kOutput, calls=%fused_computation.165 | convolution fusion | flops 405569536 | bytes 5440000 | tf_op jit(solution)/shard_map/dot_general | solution.py:234
  77.9 2.5 %fusion.14 = f32[128,384]{1,0:T(8,128)} fusion(bf16[1,2048,384]{2,1,0:T(8,128)(2,1)} %param.16, bf16[32,2048]{1,0:T(8,128)(2,1)S(1)} %get-tuple-element.20, bf16[32,2048]{1,0:T(8,128)(2,1)S(1)} %copy-done.9, bf16[32,2048]{1,0:T(8,128)(2,1)S(1)} %get-tuple-element.19, bf16[32,2048]{1,0:T(8,128)(2,1)S(1)} %collective-permute-done.13), kind=kOutput, calls=%fused_computation.17 | convolution fusion | flops 203423744 | bytes 2293760 | tf_op jit(solution)/shard_map/dot_general | solution.py:232
  80.5 3.4 %fusion.128 = (bf16[128,2048]{1,0:T(8,128)(2,1)S(1)}, f32[128,2048]{1,0:T(8,128)}) fusion(f32[128]{0:T(128)S(1)} %maximum_bitcast_fusion.5, bf16[1,384,2048]{2,1,0:T(8,128)(2,1)S(1)} %copy-done, f32[128,384]{1,0:T(8,128)} %fusion.14, bf16[1,2048,384]{2,1,0:T(8,128)(2,1)} %param.15, bf16[32,2048]{1,0:T(8,128)(2,1)} %copy-done.21, ...), kind=kOutput, calls=%fused_computation.166 | convolution fusion | flops 405569536 | bytes 5440000 | tf_op jit(solution)/shard_map/dot_general | solution.py:234
  85.9 1.7 %collective-permute-start.29 = (bf16[32,2048]{1,0:T(8,128)(2,1)S(1)}, bf16[32,2048]{1,0:T(8,128)(2,1)S(1)}, u32[]{:S(2)}, u32[]{:S(2)}) collective-permute-start(bf16[32,2048]{1,0:T(8,128)(2,1)S(1)} %fusion.33), channel_id=1, source_target_pairs={{0,8},{4,12},{8,0},{12,4},{1,9},{5,13},{9,1},{13,5},{2,10},{6,14},... | collective-permute-start | bytes 393224 | tf_op jit(solution)/shard_map/ppermute | solution.py:157
  88.2 1.7 %collective-permute-start.17 = (bf16[32,2048]{1,0:T(8,128)(2,1)S(1)}, bf16[32,2048]{1,0:T(8,128)(2,1)S(1)}, u32[]{:S(2)}, u32[]{:S(2)}) collective-permute-start(bf16[32,2048]{1,0:T(8,128)(2,1)S(1)} %fusion.43), channel_id=1, source_target_pairs={{0,8},{4,12},{8,0},{12,4},{1,9},{5,13},{9,1},{13,5},{2,10},{6,14},... | collective-permute-start | bytes 393224 | tf_op jit(solution)/shard_map/ppermute | solution.py:157
  90.0 4.6 %collective-permute-done.29 = bf16[32,2048]{1,0:T(8,128)(2,1)S(1)} collective-permute-done((bf16[32,2048]{1,0:T(8,128)(2,1)S(1)}, bf16[32,2048]{1,0:T(8,128)(2,1)S(1)}, u32[]{:S(2)}, u32[]{:S(2)}) %collective-permute-start.29) | collective-permute-done | bytes 131104 | tf_op jit(solution)/shard_map/ppermute | solution.py:157
  95.0 2.4 %collective-permute-done.23 = bf16[32,2048]{1,0:T(8,128)(2,1)S(1)} collective-permute-done((bf16[32,2048]{1,0:T(8,128)(2,1)S(1)}, bf16[32,2048]{1,0:T(8,128)(2,1)S(1)}, u32[]{:S(2)}, u32[]{:S(2)}) %collective-permute-start.23) | collective-permute-done | bytes 131104 | tf_op jit(solution)/shard_map/ppermute | solution.py:157
  97.4 2.4 %collective-permute-start.24 = (bf16[32,2048]{1,0:T(8,128)(2,1)S(1)}, bf16[32,2048]{1,0:T(8,128)(2,1)S(1)}, u32[]{:S(2)}, u32[]{:S(2)}) collective-permute-start(bf16[32,2048]{1,0:T(8,128)(2,1)S(1)} %fusion.41), channel_id=1, source_target_pairs={{0,3},{1,2},{2,1},{3,0},{4,7},{5,6},{6,5},{7,4},{8,11},{9,10},{10,... | collective-permute-start | bytes 393224 | tf_op jit(solution)/shard_map/ppermute | solution.py:157
  101.9 3.3 %collective-permute-done.24 = bf16[32,2048]{1,0:T(8,128)(2,1)S(1)} collective-permute-done((bf16[32,2048]{1,0:T(8,128)(2,1)S(1)}, bf16[32,2048]{1,0:T(8,128)(2,1)S(1)}, u32[]{:S(2)}, u32[]{:S(2)}) %collective-permute-start.24) | collective-permute-done | bytes 131104 | tf_op jit(solution)/shard_map/ppermute | solution.py:157
  105.2 5.3 %collective-permute-done.18 = bf16[32,2048]{1,0:T(8,128)(2,1)S(1)} collective-permute-done((bf16[32,2048]{1,0:T(8,128)(2,1)S(1)}, bf16[32,2048]{1,0:T(8,128)(2,1)S(1)}, u32[]{:S(2)}, u32[]{:S(2)}) %collective-permute-start.18) | collective-permute-done | bytes 131104 | tf_op jit(solution)/shard_map/ppermute | solution.py:157
  110.5 1.7 %fusion.55 = bf16[32,2048]{1,0:T(8,128)(2,1)} fusion(f32[32,2048]{1,0:T(8,128)S(1)} %get-tuple-element.7, f32[2,32,2048]{2,1,0:T(8,128)S(1)} %convert_element_type.118, f32[128,2048]{1,0:T(8,128)} %get-tuple-element.52, bf16[32,2048]{1,0:T(8,128)(2,1)S(1)} %collective-permute-done.30, bf16[32,2048]{1,0:T(8,128)(2,1)S(1)} %collective-permute-done.24, ...), kind=kLoop, calls=%fused_computation.74 | loop fusion | flops 720896 | bytes 1441792 | tf_op jit(solution)/shard_map/convert_element_type | solution.py:253
  (159 shorter events, 36.9 us)
Async XLA Ops:
  1.5 10.7 %collective-permute-start.2 = (bf16[2,128,128]{2,1,0:T(8,128)(2,1)S(1)}, bf16[2,128,128]{2,1,0:T(8,128)(2,1)S(1)}, u32[]{:S(2)}, u32[]{:S(2)}) collective-permute-start(bf16[2,128,128]{2,1,0:T(8,128)(2,1)S(1)} %pad_maximum_fusion.24), channel_id=1, source_target_pairs={{0,12},{4,8},{8,4},{12,0},{1,13},{5,9},{9,5},{13,1},{2,14},{6,10},... | collective-permute-start | bytes 196616 | tf_op jit(solution)/shard_map/ppermute | solution.py:157
  4.0 8.3 %collective-permute-start.1 = (bf16[2,128,128]{2,1,0:T(8,128)(2,1)S(1)}, bf16[2,128,128]{2,1,0:T(8,128)(2,1)S(1)}, u32[]{:S(2)}, u32[]{:S(2)}) collective-permute-start(bf16[2,128,128]{2,1,0:T(8,128)(2,1)S(1)} %pad_maximum_fusion.24), channel_id=1, source_target_pairs={{0,8},{4,12},{8,0},{12,4},{1,9},{5,13},{9,1},{13,5},{2,10},{6,14},... | collective-permute-start | bytes 196616 | tf_op jit(solution)/shard_map/ppermute | solution.py:157
  4.6 7.7 %collective-permute-start = (bf16[2,128,128]{2,1,0:T(8,128)(2,1)S(1)}, bf16[2,128,128]{2,1,0:T(8,128)(2,1)S(1)}, u32[]{:S(2)}, u32[]{:S(2)}) collective-permute-start(bf16[2,128,128]{2,1,0:T(8,128)(2,1)S(1)} %pad_maximum_fusion.24), channel_id=1, source_target_pairs={{0,4},{4,0},{8,12},{12,8},{1,5},{5,1},{9,13},{13,9},{2,6},{6,2},{1... | collective-permute-start | bytes 196616 | tf_op jit(solution)/shard_map/ppermute | solution.py:157
  18.4 9.6 %collective-permute-start.4 = (bf16[32,2048]{1,0:T(8,128)(2,1)S(1)}, bf16[32,2048]{1,0:T(8,128)(2,1)S(1)}, u32[]{:S(2)}, u32[]{:S(2)}) collective-permute-start(bf16[32,2048]{1,0:T(8,128)(2,1)S(1)} %get-tuple-element.18), channel_id=1, source_target_pairs={{0,3},{1,2},{2,1},{3,0},{4,7},{5,6},{6,5},{7,4},{8,11},{9,10},{10,... | collective-permute-start | bytes 393224 | tf_op jit(solution)/shard_map/ppermute | solution.py:157
  20.9 11.4 %collective-permute-start.3 = (bf16[32,2048]{1,0:T(8,128)(2,1)S(1)}, bf16[32,2048]{1,0:T(8,128)(2,1)S(1)}, u32[]{:S(2)}, u32[]{:S(2)}) collective-permute-start(bf16[32,2048]{1,0:T(8,128)(2,1)S(1)} %get-tuple-element.16), channel_id=1, source_target_pairs={{0,2},{1,3},{2,0},{3,1},{4,6},{5,7},{6,4},{7,5},{8,10},{9,11},{10,... | collective-permute-start | bytes 393224 | tf_op jit(solution)/shard_map/ppermute | solution.py:157
  32.6 8.5 %collective-permute-start.6 = (bf16[32,2048]{1,0:T(8,128)(2,1)S(1)}, bf16[32,2048]{1,0:T(8,128)(2,1)S(1)}, u32[]{:S(2)}, u32[]{:S(2)}) collective-permute-start(bf16[32,2048]{1,0:T(8,128)(2,1)S(1)} %multiply_convert_fusion), channel_id=1, source_target_pairs={{0,8},{4,12},{8,0},{12,4},{1,9},{5,13},{9,1},{13,5},{2,10},{6,14},... | collective-permute-start | bytes 393224 | tf_op jit(solution)/shard_map/ppermute | solution.py:157
  34.1 6.4 %collective-permute-start.25 = (bf16[32,2048]{1,0:T(8,128)(2,1)S(1)}, bf16[32,2048]{1,0:T(8,128)(2,1)S(1)}, u32[]{:S(2)}, u32[]{:S(2)}) collective-permute-start(bf16[32,2048]{1,0:T(8,128)(2,1)S(1)} %multiply_convert_fusion), channel_id=1, source_target_pairs={{0,1},{1,0},{2,3},{3,2},{4,5},{5,4},{6,7},{7,6},{8,9},{9,8},{10,11... | collective-permute-start | bytes 393224 | tf_op jit(solution)/shard_map/ppermute | solution.py:157
  34.2 9.3 %collective-permute-start.19 = (bf16[32,2048]{1,0:T(8,128)(2,1)S(1)}, bf16[32,2048]{1,0:T(8,128)(2,1)S(1)}, u32[]{:S(2)}, u32[]{:S(2)}) collective-permute-start(bf16[32,2048]{1,0:T(8,128)(2,1)S(1)} %multiply_convert_fusion), channel_id=1, source_target_pairs={{0,3},{1,2},{2,1},{3,0},{4,7},{5,6},{6,5},{7,4},{8,11},{9,10},{10,... | collective-permute-start | bytes 393224 | tf_op jit(solution)/shard_map/ppermute | solution.py:157
  36.9 11.5 %collective-permute-start.13 = (bf16[32,2048]{1,0:T(8,128)(2,1)S(1)}, bf16[32,2048]{1,0:T(8,128)(2,1)S(1)}, u32[]{:S(2)}, u32[]{:S(2)}) collective-permute-start(bf16[32,2048]{1,0:T(8,128)(2,1)S(1)} %multiply_convert_fusion), channel_id=1, source_target_pairs={{0,2},{1,3},{2,0},{3,1},{4,6},{5,7},{6,4},{7,5},{8,10},{9,11},{10,... | collective-permute-start | bytes 393224 | tf_op jit(solution)/shard_map/ppermute | solution.py:157
  40.6 8.3 %collective-permute-start.26 = (bf16[32,2048]{1,0:T(8,128)(2,1)S(1)}, bf16[32,2048]{1,0:T(8,128)(2,1)S(1)}, u32[]{:S(2)}, u32[]{:S(2)}) collective-permute-start(bf16[32,2048]{1,0:T(8,128)(2,1)S(1)} %collective-permute-done.25), channel_id=1, source_target_pairs={{0,8},{4,12},{8,0},{12,4},{1,9},{5,13},{9,1},{13,5},{2,10},{6,14},... | collective-permute-start | bytes 393224 | tf_op jit(solution)/shard_map/ppermute | solution.py:157
  41.2 13.7 %collective-permute-start.7 = (bf16[2,32,2048]{2,1,0:T(8,128)(2,1)S(1)}, bf16[2,32,2048]{2,1,0:T(8,128)(2,1)S(1)}, u32[]{:S(2)}, u32[]{:S(2)}) collective-permute-start(bf16[2,32,2048]{2,1,0:T(8,128)(2,1)S(1)} %pad_maximum_fusion.4), channel_id=1, source_target_pairs={{0,4},{4,0},{8,12},{12,8},{1,5},{5,1},{9,13},{13,9},{2,6},{6,2},{1... | collective-permute-start | bytes 786440 | tf_op jit(solution)/shard_map/ppermute | solution.py:157
  49.6 13.1 %collective-permute-start.27 = (bf16[2,32,2048]{2,1,0:T(8,128)(2,1)}, bf16[2,32,2048]{2,1,0:T(8,128)(2,1)S(1)}, u32[]{:S(2)}, u32[]{:S(2)}) collective-permute-start(bf16[2,32,2048]{2,1,0:T(8,128)(2,1)} %pad_maximum_fusion.10), channel_id=1, source_target_pairs={{0,4},{4,0},{8,12},{12,8},{1,5},{5,1},{9,13},{13,9},{2,6},{6,2},{1... | collective-permute-start | bytes 786440 | tf_op jit(solution)/shard_map/ppermute | solution.py:157
  50.4 18.5 %collective-permute-start.21 = (bf16[2,32,2048]{2,1,0:T(8,128)(2,1)}, bf16[2,32,2048]{2,1,0:T(8,128)(2,1)S(1)}, u32[]{:S(2)}, u32[]{:S(2)}) collective-permute-start(bf16[2,32,2048]{2,1,0:T(8,128)(2,1)} %pad_maximum_fusion.8), channel_id=1, source_target_pairs={{0,4},{4,0},{8,12},{12,8},{1,5},{5,1},{9,13},{13,9},{2,6},{6,2},{1... | collective-permute-start | bytes 786440 | tf_op jit(solution)/shard_map/ppermute | solution.py:157
  54.8 22.4 %collective-permute-start.15 = (bf16[2,32,2048]{2,1,0:T(8,128)(2,1)}, bf16[2,32,2048]{2,1,0:T(8,128)(2,1)S(1)}, u32[]{:S(2)}, u32[]{:S(2)}) collective-permute-start(bf16[2,32,2048]{2,1,0:T(8,128)(2,1)} %pad_maximum_fusion.6), channel_id=1, source_target_pairs={{0,4},{4,0},{8,12},{12,8},{1,5},{5,1},{9,13},{13,9},{2,6},{6,2},{1... | collective-permute-start | bytes 786440 | tf_op jit(solution)/shard_map/ppermute | solution.py:157
  62.2 22.1 %collective-permute-start.11 = (bf16[2,32,2048]{2,1,0:T(8,128)(2,1)}, bf16[2,32,2048]{2,1,0:T(8,128)(2,1)S(1)}, u32[]{:S(2)}, u32[]{:S(2)}) collective-permute-start(bf16[2,32,2048]{2,1,0:T(8,128)(2,1)} %pad_maximum_fusion.5), channel_id=1, source_target_pairs={{0,4},{4,0},{8,12},{12,8},{1,5},{5,1},{9,13},{13,9},{2,6},{6,2},{1... | collective-permute-start | bytes 786440 | tf_op jit(solution)/shard_map/ppermute | solution.py:157
  68.9 16.9 %collective-permute-start.28 = (bf16[2,32,2048]{2,1,0:T(8,128)(2,1)}, bf16[2,32,2048]{2,1,0:T(8,128)(2,1)S(1)}, u32[]{:S(2)}, u32[]{:S(2)}) collective-permute-start(bf16[2,32,2048]{2,1,0:T(8,128)(2,1)} %pad_maximum_fusion.11), channel_id=1, source_target_pairs={{0,4},{4,0},{8,12},{12,8},{1,5},{5,1},{9,13},{13,9},{2,6},{6,2},{1... | collective-permute-start | bytes 786440 | tf_op jit(solution)/shard_map/ppermute | solution.py:157
  76.9 10.7 %collective-permute-start.22 = (bf16[2,32,2048]{2,1,0:T(8,128)(2,1)}, bf16[2,32,2048]{2,1,0:T(8,128)(2,1)S(1)}, u32[]{:S(2)}, u32[]{:S(2)}) collective-permute-start(bf16[2,32,2048]{2,1,0:T(8,128)(2,1)} %pad_maximum_fusion.9), channel_id=1, source_target_pairs={{0,4},{4,0},{8,12},{12,8},{1,5},{5,1},{9,13},{13,9},{2,6},{6,2},{1... | collective-permute-start | bytes 786440 | tf_op jit(solution)/shard_map/ppermute | solution.py:157
  85.4 16.6 %collective-permute-start.12 = (bf16[32,2048]{1,0:T(8,128)(2,1)S(1)}, bf16[32,2048]{1,0:T(8,128)(2,1)}, u32[]{:S(2)}, u32[]{:S(2)}) collective-permute-start(bf16[32,2048]{1,0:T(8,128)(2,1)S(1)} %fusion.48), channel_id=1, source_target_pairs={{0,8},{4,12},{8,0},{12,4},{1,9},{5,13},{9,1},{13,5},{2,10},{6,14},... | collective-permute-start | bytes 393224 | tf_op jit(solution)/shard_map/ppermute | solution.py:157
  85.9 8.7 %collective-permute-start.29 = (bf16[32,2048]{1,0:T(8,128)(2,1)S(1)}, bf16[32,2048]{1,0:T(8,128)(2,1)S(1)}, u32[]{:S(2)}, u32[]{:S(2)}) collective-permute-start(bf16[32,2048]{1,0:T(8,128)(2,1)S(1)} %fusion.33), channel_id=1, source_target_pairs={{0,8},{4,12},{8,0},{12,4},{1,9},{5,13},{9,1},{13,5},{2,10},{6,14},... | collective-permute-start | bytes 393224 | tf_op jit(solution)/shard_map/ppermute | solution.py:157
  87.7 9.7 %collective-permute-start.23 = (bf16[32,2048]{1,0:T(8,128)(2,1)S(1)}, bf16[32,2048]{1,0:T(8,128)(2,1)S(1)}, u32[]{:S(2)}, u32[]{:S(2)}) collective-permute-start(bf16[32,2048]{1,0:T(8,128)(2,1)S(1)} %fusion.38), channel_id=1, source_target_pairs={{0,8},{4,12},{8,0},{12,4},{1,9},{5,13},{9,1},{13,5},{2,10},{6,14},... | collective-permute-start | bytes 393224 | tf_op jit(solution)/shard_map/ppermute | solution.py:157
  88.2 11.6 %collective-permute-start.17 = (bf16[32,2048]{1,0:T(8,128)(2,1)S(1)}, bf16[32,2048]{1,0:T(8,128)(2,1)S(1)}, u32[]{:S(2)}, u32[]{:S(2)}) collective-permute-start(bf16[32,2048]{1,0:T(8,128)(2,1)S(1)} %fusion.43), channel_id=1, source_target_pairs={{0,8},{4,12},{8,0},{12,4},{1,9},{5,13},{9,1},{13,5},{2,10},{6,14},... | collective-permute-start | bytes 393224 | tf_op jit(solution)/shard_map/ppermute | solution.py:157
  94.6 7.3 %collective-permute-start.30 = (bf16[32,2048]{1,0:T(8,128)(2,1)S(1)}, bf16[32,2048]{1,0:T(8,128)(2,1)S(1)}, u32[]{:S(2)}, u32[]{:S(2)}) collective-permute-start(bf16[32,2048]{1,0:T(8,128)(2,1)S(1)} %fusion.36), channel_id=1, source_target_pairs={{0,1},{1,0},{2,3},{3,2},{4,5},{5,4},{6,7},{7,6},{8,9},{9,8},{10,11... | collective-permute-start | bytes 393224 | tf_op jit(solution)/shard_map/ppermute | solution.py:157
  97.4 7.8 %collective-permute-start.24 = (bf16[32,2048]{1,0:T(8,128)(2,1)S(1)}, bf16[32,2048]{1,0:T(8,128)(2,1)S(1)}, u32[]{:S(2)}, u32[]{:S(2)}) collective-permute-start(bf16[32,2048]{1,0:T(8,128)(2,1)S(1)} %fusion.41), channel_id=1, source_target_pairs={{0,3},{1,2},{2,1},{3,0},{4,7},{5,6},{6,5},{7,4},{8,11},{9,10},{10,... | collective-permute-start | bytes 393224 | tf_op jit(solution)/shard_map/ppermute | solution.py:157
  99.8 10.7 %collective-permute-start.18 = (bf16[32,2048]{1,0:T(8,128)(2,1)S(1)}, bf16[32,2048]{1,0:T(8,128)(2,1)S(1)}, u32[]{:S(2)}, u32[]{:S(2)}) collective-permute-start(bf16[32,2048]{1,0:T(8,128)(2,1)S(1)} %fusion.46), channel_id=1, source_target_pairs={{0,2},{1,3},{2,0},{3,1},{4,6},{5,7},{6,4},{7,5},{8,10},{9,11},{10,... | collective-permute-start | bytes 393224 | tf_op jit(solution)/shard_map/ppermute | solution.py:157
  (33 other events, 219.2 us)

commit v2 on v0

--- a/solution.py
+++ b/solution.py
@@ -1,8 +1,11 @@
+import functools
 import math
 
 import jax
 import jax.numpy as jnp
 from jax import lax
+from jax.experimental import pallas as pl
+from jax.experimental.pallas import tpu as pltpu
 from jax.sharding import PartitionSpec as P
 
 HEAD = 128
@@ -13,7 +16,7 @@
     return (proj_rows * inverse * norm_gain).astype(jnp.bfloat16)
 
 
-def per_device(
+def routed_plan(
     queries,
     keys,
     values,
@@ -152,6 +155,174 @@
     return (attended, layer_out)
 
 
+F32, BF16 = jnp.float32, jnp.bfloat16
+VMEM_SPEC = pl.BlockSpec(memory_space=pltpu.VMEM)
+
+
+def swap(rows, axis, offset):
+    count = lax.axis_size(axis)
+    return lax.ppermute(rows, axis, [(i, i ^ offset) for i in range(count)])
+
+
+def call(kernel, outs, operands, scratch=(), flops=0, moved=0, limit=32 << 20):
+    return pl.pallas_call(
+        kernel,
+        out_shape=outs,
+        in_specs=[VMEM_SPEC] * len(operands),
+        out_specs=[VMEM_SPEC] * len(outs),
+        scratch_shapes=scratch,
+        compiler_params=pltpu.CompilerParams(vmem_limit_bytes=limit),
+        cost_estimate=pl.CostEstimate(flops=flops, bytes_accessed=moved, transcendentals=0),
+    )(*operands)
+
+
+def attend_kernel(tp_count, q_ref, own_ref, kv1_ref, kv2_ref, kv3_ref, w_ref, att_ref, *piece_refs):
+    ctx_index, tp_index = lax.axis_index("ctx"), lax.axis_index("tp")
+    block_rows = q_ref.shape[0]
+    heads = q_ref.shape[1] // HEAD
+    kv_local = own_ref.shape[2] // HEAD
+    group_size = heads // kv_local
+    blocks = (own_ref, kv1_ref, kv2_ref, kv3_ref)
+    row = lax.broadcasted_iota(jnp.int32, (block_rows, block_rows), 0)
+    col = lax.broadcasted_iota(jnp.int32, (block_rows, block_rows), 1)
+    low = jnp.where(col <= row, 0.0, -1e30)
+    masks = [low] + [
+        jnp.where((ctx_index ^ d) < ctx_index, 0.0, -1e30) * jnp.ones_like(low)
+        for d in range(1, len(blocks))
+    ]
+    mask = jnp.concatenate(masks, axis=1)
+    for g in range(kv_local):
+        lanes = slice(g * HEAD, (g + 1) * HEAD)
+        key_rows = jnp.concatenate([b[0, :, lanes] for b in blocks], axis=0)
+        value_rows = jnp.concatenate([b[1, :, lanes] for b in blocks], axis=0)
+        for j in range(group_size):
+            h = g * group_size + j
+            q = q_ref[:, h * HEAD : (h + 1) * HEAD]
+            scores = lax.dot_general(
+                q, key_rows, (((1,), (1,)), ((), ())), preferred_element_type=F32
+            )
+            scores = scores * HEAD ** (-0.5) + mask
+            weights = jnp.exp(scores - jnp.max(scores, axis=1, keepdims=True))
+            total = jnp.sum(weights, axis=1, keepdims=True)
+            accum = jnp.dot(weights.astype(BF16), value_rows, preferred_element_type=F32)
+            att_ref[:, h * HEAD : (h + 1) * HEAD] = (accum / total).astype(BF16)
+    piece_rows = block_rows // tp_count
+    scratch = piece_refs[-1]
+    scratch[...] = jnp.dot(att_ref[...], w_ref[...], preferred_element_type=F32)
+    for d in range(tp_count):
+        start = pl.multiple_of((tp_index ^ d) * piece_rows, piece_rows)
+        piece_refs[d][...] = scratch[pl.ds(start, piece_rows), :].astype(piece_refs[d].dtype)
+
+
+def norm_kernel(gain_ref, own_ref, *refs):
+    parts, (proj_ref, normed_ref) = refs[:-2], refs[-2:]
+    proj = own_ref[...]
+    for part in parts:
+        proj = proj + part[...].astype(F32)
+    proj_ref[...] = proj
+    inverse = lax.rsqrt(jnp.mean(proj * proj, axis=1, keepdims=True) + 1e-06)
+    normed_ref[...] = (proj * inverse * gain_ref[...]).astype(BF16)
+
+
+def expert_kernel(
+    offset, own_ref, far_ref, near_ref, mix_ref, gate_ref, up_ref, down_ref, keep_ref, send_ref
+):
+    tp_index = lax.axis_index("tp")
+    rows = own_ref.shape[0]
+    tokens = jnp.concatenate([own_ref[...], far_ref[...], near_ref[0], near_ref[1]], axis=0)
+    gate_proj = jnp.dot(tokens, gate_ref[0], preferred_element_type=F32)
+    up_proj = jnp.dot(tokens, up_ref[0], preferred_element_type=F32)
+    activated = (gate_proj / (1.0 + jnp.exp(-gate_proj)) * up_proj).astype(BF16)
+    out = jnp.dot(activated, down_ref[0], preferred_element_type=F32) * mix_ref[tp_index ^ offset]
+    keep_ref[0] = out[:rows]
+    keep_ref[1] = out[rows : 2 * rows]
+    send_ref[0] = out[2 * rows : 3 * rows].astype(BF16)
+    send_ref[1] = out[3 * rows :].astype(BF16)
+
+
+def dense_plan(
+    queries,
+    keys,
+    values,
+    out_weight,
+    norm_gain,
+    expert_gate,
+    expert_up,
+    expert_down,
+    expert_ids,
+    route_weights,
+):
+    ctx_count = lax.axis_size("ctx")
+    tp_count = lax.axis_size("tp")
+    ctx_index = lax.axis_index("ctx")
+    tp_index = lax.axis_index("tp")
+    block_rows, width = queries.shape
+    piece_rows = block_rows // tp_count
+    features = out_weight.shape[1]
+
+    own_kv = jnp.stack([keys, values])
+    kv = [own_kv] + [swap(own_kv, "ctx", d) for d in range(1, ctx_count)]
+
+    piece = jax.ShapeDtypeStruct((piece_rows, features), BF16)
+    piece32 = jax.ShapeDtypeStruct((piece_rows, features), F32)
+    attended, *partials = call(
+        functools.partial(attend_kernel, tp_count),
+        [jax.ShapeDtypeStruct((block_rows, width), BF16), piece32] + [piece] * (tp_count - 1),
+        (queries, *kv, out_weight),
+        scratch=[pltpu.VMEM((block_rows, features), F32)],
+        flops=2 * block_rows * width * features + 4 * block_rows * block_rows * ctx_count * width,
+        moved=out_weight.size * 2,
+    )
+    arrived = [swap(partials[d], "tp", d) for d in (2, 3, 1)]
+
+    route_weights, expert_ids, _ = lax.optimization_barrier((route_weights, expert_ids, attended))
+    share = route_weights / jnp.sum(route_weights, axis=1, keepdims=True)
+    mixes = []
+    for d in (0, 2, 1, 3):
+        expert = (ctx_index ^ d) * tp_count + tp_index
+        mix = jnp.sum(jnp.where(expert_ids == expert, share, 0.0), axis=1)
+        mixes.append(swap(mix, "ctx", d) if d else mix)
+    mix = jnp.stack(mixes).reshape(ctx_count, tp_count, piece_rows)
+    mix = mix.transpose(1, 0, 2).reshape(tp_count, ctx_count * piece_rows, 1)
+
+    own_proj, normed = call(
+        norm_kernel, [piece32, piece], (norm_gain.reshape(1, features), partials[0], *arrived)
+    )
+
+    pieces = {0: normed}
+    for d in (2, 3, 1):
+        pieces[d] = swap(normed, "tp", d)
+    sums = {}
+    for d in (0, 1, 2, 3):
+        far = swap(pieces[d], "ctx", 2)
+        near = swap(jnp.stack([pieces[d], far]), "ctx", 1)
+        keep, send = call(
+            functools.partial(expert_kernel, d),
+            [
+                jax.ShapeDtypeStruct((2, piece_rows, features), F32),
+                jax.ShapeDtypeStruct((2, piece_rows, features), BF16),
+            ],
+            (pieces[d], far, near, mix, expert_gate, expert_up, expert_down),
+            flops=6 * ctx_count * piece_rows * features * expert_gate.shape[2],
+            moved=3 * expert_gate.size * 2,
+        )
+        got = swap(send, "ctx", 1).astype(F32)
+        far_sum = swap((keep[1] + got[1]).astype(BF16), "ctx", 2).astype(F32)
+        sums[d] = keep[0] + got[0] + far_sum
+    expert_mix = sums[0]
+    for d in (1, 2, 3):
+        expert_mix = expert_mix + swap(sums[d].astype(BF16), "tp", d).astype(F32)
+    return (attended, (own_proj + expert_mix).astype(BF16))
+
+
+def per_device(*arguments):
+    ctx_count, tp_count = lax.axis_size("ctx"), lax.axis_size("tp")
+    top_count = arguments[8].shape[1]
+    if ctx_count == 4 and tp_count == 4 and ctx_count * tp_count <= 2 * top_count:
+        return dense_plan(*arguments)
+    return routed_plan(*arguments)
+
+
 def solution(mesh):
     in_specs = (
         P(("dp", "ctx"), "tp"),

time: 152 us -> 93 us (0.61)
  blocking collectives: 51.2 us -> 0 us
  starting transfers between devices: 3.77 us -> 29.5 us
  waiting for transfers between devices: 58.8 us -> 34.9 us
  matrix products: 14.6 us -> 0 us
  between operations: 14.2 us -> 0.9 us
  local copies, waits for them, and re-layouts: 1.87 us -> 12.2 us
  Pallas kernels: 0 us -> 9.96 us
  other arithmetic: 7.06 us -> 5.04 us
    reduce_scatter x2 -> x0, waiting for transfers between devices: 39.4 us -> none  [the longest x1 20.3 us: per_device(): lax.psum_scatter(jnp.dot(attended, out_weight, preferred_element_type=jnp...]
    ppermute x0 -> x31, waiting for transfers between devices: none -> 34.9 us  [swap(): return lax.ppermute(rows, axis, [(i, i ^ offset) for i in range(count)])]
    ppermute x0 -> x31, starting transfers between devices: none -> 29.5 us  [swap(): return lax.ppermute(rows, axis, [(i, i ^ offset) for i in range(count)])]
    all_gather x3 -> x0, blocking collectives: 28.5 us -> none  [the longest x1 15.8 us: per_device(): lax.all_gather(rms_scale(own_proj, norm_gain), 'tp', axis=0, tiled=True)]
    all_to_all x1 -> x0, blocking collectives: 22.7 us -> none  [per_device(): lax.all_to_all(outgoing, 'ctx', split_axis=0, concat_axis=0, tiled=True)]
    all_to_all x1 -> x0, waiting for transfers between devices: 19.3 us -> none  [per_device(): lax.all_to_all(expert_out, 'ctx', split_axis=0, concat_axis=0, tiled=True)]
    dot_general x8 -> x0, matrix products: 14.6 us -> none  [the longest x1 4.57 us: per_device(): jnp.dot(activated, expert_down[0], preferred_element_type=jnp.float32)]
    unnamed x16 -> x36, local copies, waits for them, and re-layouts: 0.87 us -> 11.6 us
  transfers between devices with their start and end apart: 3 -> 31, of which waited for: 3 -> 13; matrix products, arithmetic and copies ran while one was open for 2% -> 4% of each run, Pallas kernels for 0% -> 7%
where the time goes in v2:
time: 93 us; the launch traced here: 92.5 us
  waiting for transfers between devices  34.9 us (38%)
  starting transfers between devices  29.5 us (32%)
  local copies, waits for them, and re-layouts  12.2 us (13%)
  Pallas kernels  9.96 us (11%)
  other arithmetic  5.04 us (5%)
    ppermute x31, waiting for transfers between devices, swap(): return lax.ppermute(rows, axis, [(i, i ^ offset) for i in range(count)])  34.9 us
    ppermute x31, starting transfers between devices, swap(): return lax.ppermute(rows, axis, [(i, i ^ offset) for i in range(count)])  29.5 us
    unnamed x36, local copies, waits for them, and re-layouts  11.6 us
    pallas_call x6, Pallas kernels, call(): pl.pallas_call(kernel, out_shape=outs, in_specs=[VMEM_SPEC] * len(operand...  9.96 us
    another operation x4, other arithmetic, dense_plan(): near = swap(jnp.stack([pieces[d], far]), 'ctx', 1)  1.91 us
  transfers between devices with their start and end apart: 31, of which 13 were waited for; matrix products, arithmetic and copies ran while one was open for 4% of the time, Pallas kernels for 7%

profile of v2, /device:TPU:0, one launch (start us, length us, event | category | flops | bytes accessed | tf_op | source)
XLA Modules:
  0.0 92.5 jit_solution(13331289711754932059)
XLA Ops:
  2.0 2.6 %collective-permute-start.1 = (bf16[2,128,128]{2,1,0:T(8,128)(2,1)S(1)}, bf16[2,128,128]{2,1,0:T(8,128)(2,1)S(1)}, u32[]{:S(2)}, u32[]{:S(2)}) collective-permute-start(bf16[2,128,128]{2,1,0:T(8,128)(2,1)S(1)} %pad_maximum_fusion.4.own_ref), channel_id=1, source_target_pairs={{0,8},{4,12},{8,0},{12,4},{1,9},{5,13},{9,1},{13,5},{2,10},{6,14},... | collective-permute-start | bytes 196616 | tf_op jit(solution)/shard_map/ppermute | solution.py:164
  4.6 2.6 %collective-permute-done.1.kv2_ref = bf16[2,128,128]{2,1,0:T(8,128)(2,1)S(1)} collective-permute-done((bf16[2,128,128]{2,1,0:T(8,128)(2,1)S(1)}, bf16[2,128,128]{2,1,0:T(8,128)(2,1)S(1)}, u32[]{:S(2)}, u32[]{:S(2)}) %collective-permute-start.1) | collective-permute-done | bytes 65568 | tf_op jit(solution)/shard_map/ppermute | solution.py:164
  7.2 1.4 %collective-permute-done.2.kv3_ref = bf16[2,128,128]{2,1,0:T(8,128)(2,1)S(1)} collective-permute-done((bf16[2,128,128]{2,1,0:T(8,128)(2,1)S(1)}, bf16[2,128,128]{2,1,0:T(8,128)(2,1)S(1)}, u32[]{:S(2)}, u32[]{:S(2)}) %collective-permute-start.2) | collective-permute-done | bytes 65568 | tf_op jit(solution)/shard_map/ppermute | solution.py:164
  8.6 2.2 %copy-done.3 = bf16[1024,2048]{1,0:T(8,128)(2,1)S(1)} copy-done((bf16[1024,2048]{1,0:T(8,128)(2,1)S(1)}, bf16[1024,2048]{1,0:T(8,128)(2,1)}, u32[]{:S(2)}) %copy-start.3) | copy-done | bytes 4194328
  11.7 3.6 %shard_map.113 = (bf16[128,1024]{1,0:T(8,128)(2,1)}, f32[32,2048]{1,0:T(8,128)S(1)}, bf16[32,2048]{1,0:T(8,128)(2,1)}, bf16[32,2048]{1,0:T(8,128)(2,1)}, bf16[32,2048]{1,0:T(8,128)(2,1)}) custom-call(bf16[128,1024]{1,0:T(8,128)(2,1)S(1)} %copy-done.4, bf16[2,128,128]{2,1,0:T(8,128)(2,1)S(1)} %pad_maximum_fusion.4.own_ref, ...), custom_call_target="tpu_custom_call" | custom-call | flops 805306368 | bytes 4194304 | tf_op jit(solution)/shard_map/pallas_call | solution.py:168
  16.0 2.6 %collective-permute-start.3 = (bf16[32,2048]{1,0:T(8,128)(2,1)}, bf16[32,2048]{1,0:T(8,128)(2,1)S(1)}, u32[]{:S(2)}, u32[]{:S(2)}) collective-permute-start(bf16[32,2048]{1,0:T(8,128)(2,1)} %get-tuple-element.21), channel_id=1, source_target_pairs={{0,2},{1,3},{2,0},{3,1},{4,6},{5,7},{6,4},{7,5},{8,10},{9,11},{10,... | collective-permute-start | bytes 393224 | tf_op jit(solution)/shard_map/ppermute | solution.py:164
  18.6 1.4 %collective-permute-start.4 = (bf16[32,2048]{1,0:T(8,128)(2,1)}, bf16[32,2048]{1,0:T(8,128)(2,1)S(1)}, u32[]{:S(2)}, u32[]{:S(2)}) collective-permute-start(bf16[32,2048]{1,0:T(8,128)(2,1)} %get-tuple-element.22), channel_id=1, source_target_pairs={{0,3},{1,2},{2,1},{3,0},{4,7},{5,6},{6,5},{7,4},{8,11},{9,10},{10,... | collective-permute-start | bytes 393224 | tf_op jit(solution)/shard_map/ppermute | solution.py:164
  20.8 8.4 %collective-permute-done.3.refs_0_ = bf16[32,2048]{1,0:T(8,128)(2,1)S(1)} collective-permute-done((bf16[32,2048]{1,0:T(8,128)(2,1)}, bf16[32,2048]{1,0:T(8,128)(2,1)S(1)}, u32[]{:S(2)}, u32[]{:S(2)}) %collective-permute-start.3) | collective-permute-done | bytes 131104 | tf_op jit(solution)/shard_map/ppermute | solution.py:164
  35.7 1.3 %collective-permute-start.6 = (bf16[32,2048]{1,0:T(8,128)(2,1)S(1)}, bf16[32,2048]{1,0:T(8,128)(2,1)}, u32[]{:S(2)}, u32[]{:S(2)}) collective-permute-start(bf16[32,2048]{1,0:T(8,128)(2,1)S(1)} %get-tuple-element.25.own_ref), channel_id=1, source_target_pairs={{0,8},{4,12},{8,0},{12,4},{1,9},{5,13},{9,1},{13,5},{2,10},{6,14},... | collective-permute-start | bytes 393224 | tf_op jit(solution)/shard_map/ppermute | solution.py:164
  37.0 2.9 %collective-permute-start.25 = (bf16[32,2048]{1,0:T(8,128)(2,1)S(1)}, bf16[32,2048]{1,0:T(8,128)(2,1)}, u32[]{:S(2)}, u32[]{:S(2)}) collective-permute-start(bf16[32,2048]{1,0:T(8,128)(2,1)S(1)} %get-tuple-element.25.own_ref), channel_id=1, source_target_pairs={{0,3},{1,2},{2,1},{3,0},{4,7},{5,6},{6,5},{7,4},{8,11},{9,10},{10,... | collective-permute-start | bytes 393224 | tf_op jit(solution)/shard_map/ppermute | solution.py:164
  41.3 1.4 %collective-permute-start.8 = (f32[128]{0:T(128)S(1)}, f32[128]{0:T(128)S(1)}, u32[]{:S(2)}, u32[]{:S(2)}) collective-permute-start(f32[128]{0:T(128)S(1)} %get-tuple-element.39), channel_id=1, source_target_pairs={{0,8},{4,12},{8,0},{12,4},{1,9},{5,13},{9,1},{13,5},{2,10},{6,14},... | collective-permute-start | bytes 1544 | tf_op jit(solution)/shard_map/ppermute | solution.py:164
  45.2 1.3 %collective-permute-start.19 = (bf16[32,2048]{1,0:T(8,128)(2,1)S(1)}, bf16[32,2048]{1,0:T(8,128)(2,1)S(1)}, u32[]{:S(2)}, u32[]{:S(2)}) collective-permute-start(bf16[32,2048]{1,0:T(8,128)(2,1)S(1)} %get-tuple-element.25.own_ref), channel_id=1, source_target_pairs={{0,2},{1,3},{2,0},{3,1},{4,6},{5,7},{6,4},{7,5},{8,10},{9,11},{10,... | collective-permute-start | bytes 393224 | tf_op jit(solution)/shard_map/ppermute | solution.py:164
  47.1 1.5 %collective-permute-start.26 = (bf16[32,2048]{1,0:T(8,128)(2,1)}, bf16[32,2048]{1,0:T(8,128)(2,1)S(1)}, u32[]{:S(2)}, u32[]{:S(2)}) collective-permute-start(bf16[32,2048]{1,0:T(8,128)(2,1)} %collective-permute-done.25.own_ref), channel_id=1, source_target_pairs={{0,8},{4,12},{8,0},{12,4},{1,9},{5,13},{9,1},{13,5},{2,10},{6,14},... | collective-permute-start | bytes 393224 | tf_op jit(solution)/shard_map/ppermute | solution.py:164
  49.6 4.0 %collective-permute-done.19.own_ref = bf16[32,2048]{1,0:T(8,128)(2,1)S(1)} collective-permute-done((bf16[32,2048]{1,0:T(8,128)(2,1)S(1)}, bf16[32,2048]{1,0:T(8,128)(2,1)S(1)}, u32[]{:S(2)}, u32[]{:S(2)}) %collective-permute-start.19) | collective-permute-done | bytes 131104 | tf_op jit(solution)/shard_map/ppermute | solution.py:164
  56.6 1.9 %collective-permute-done.20.far_ref = bf16[32,2048]{1,0:T(8,128)(2,1)S(1)} collective-permute-done((bf16[32,2048]{1,0:T(8,128)(2,1)S(1)}, bf16[32,2048]{1,0:T(8,128)(2,1)S(1)}, u32[]{:S(2)}, u32[]{:S(2)}) %collective-permute-start.20) | collective-permute-done | bytes 131104 | tf_op jit(solution)/shard_map/ppermute | solution.py:164
  58.7 1.3 %collective-permute-done.14.far_ref = bf16[32,2048]{1,0:T(8,128)(2,1)S(1)} collective-permute-done((bf16[32,2048]{1,0:T(8,128)(2,1)S(1)}, bf16[32,2048]{1,0:T(8,128)(2,1)S(1)}, u32[]{:S(2)}, u32[]{:S(2)}) %collective-permute-start.14) | collective-permute-done | bytes 131104 | tf_op jit(solution)/shard_map/ppermute | solution.py:164
  60.1 1.4 %copy-done.2 = bf16[1,384,2048]{2,1,0:T(8,128)(2,1)S(1)} copy-done((bf16[1,384,2048]{2,1,0:T(8,128)(2,1)S(1)}, bf16[1,384,2048]{2,1,0:T(8,128)(2,1)}, u32[]{:S(2)}) %copy-start.2) | copy-done | bytes 1572888
  61.5 2.0 %shard_map.115 = (f32[2,32,2048]{2,1,0:T(8,128)S(1)}, bf16[2,32,2048]{2,1,0:T(8,128)(2,1)S(1)}) custom-call(bf16[32,2048]{1,0:T(8,128)(2,1)S(1)} %get-tuple-element.25.own_ref, bf16[32,2048]{1,0:T(8,128)(2,1)} %collective-permute-done.6.far_ref, bf16[2,32,2048]{2,1,0:T(8,128)(2,1)S(1)} %collective-permute-done.7.near_ref, f32[4,128,1]{2,1,0:T(8,128)S(1)} %reshape.34.mix_ref, ...), custom_call_target="tpu_custom_call" | custom-call | flops 603979776 | bytes 4718592 | tf_op jit(solution)/shard_map/pallas_call | solution.py:168
  64.0 2.0 %shard_map.118 = (f32[2,32,2048]{2,1,0:T(8,128)S(1)}, bf16[2,32,2048]{2,1,0:T(8,128)(2,1)S(1)}) custom-call(bf16[32,2048]{1,0:T(8,128)(2,1)} %collective-permute-done.25.own_ref, bf16[32,2048]{1,0:T(8,128)(2,1)S(1)} %collective-permute-done.26.far_ref, bf16[2,32,2048]{2,1,0:T(8,128)(2,1)S(1)} %collective-permute-done.27.near_ref, ...), custom_call_target="tpu_custom_call" | custom-call | flops 603979776 | bytes 4718592 | tf_op jit(solution)/shard_map/pallas_call | solution.py:168
  73.6 4.6 %collective-permute-done.29 = bf16[32,2048]{1,0:T(8,128)(2,1)S(1)} collective-permute-done((bf16[32,2048]{1,0:T(8,128)(2,1)S(1)}, bf16[32,2048]{1,0:T(8,128)(2,1)S(1)}, u32[]{:S(2)}, u32[]{:S(2)}) %collective-permute-start.29) | collective-permute-done | bytes 131104 | tf_op jit(solution)/shard_map/ppermute | solution.py:164
  78.3 2.5 %collective-permute-start.30 = (bf16[32,2048]{1,0:T(8,128)(2,1)S(1)}, bf16[32,2048]{1,0:T(8,128)(2,1)S(1)}, u32[]{:S(2)}, u32[]{:S(2)}) collective-permute-start(bf16[32,2048]{1,0:T(8,128)(2,1)S(1)} %fusion.3), channel_id=1, source_target_pairs={{0,3},{1,2},{2,1},{3,0},{4,7},{5,6},{6,5},{7,4},{8,11},{9,10},{10,... | collective-permute-start | bytes 393224 | tf_op jit(solution)/shard_map/ppermute | solution.py:164
  81.1 1.2 %collective-permute-start.24 = (bf16[32,2048]{1,0:T(8,128)(2,1)S(1)}, bf16[32,2048]{1,0:T(8,128)(2,1)S(1)}, u32[]{:S(2)}, u32[]{:S(2)}) collective-permute-start(bf16[32,2048]{1,0:T(8,128)(2,1)S(1)} %fusion.7), channel_id=1, source_target_pairs={{0,2},{1,3},{2,0},{3,1},{4,6},{5,7},{6,4},{7,5},{8,10},{9,11},{10,... | collective-permute-start | bytes 393224 | tf_op jit(solution)/shard_map/ppermute | solution.py:164
  84.3 2.2 %collective-permute-done.30 = bf16[32,2048]{1,0:T(8,128)(2,1)S(1)} collective-permute-done((bf16[32,2048]{1,0:T(8,128)(2,1)S(1)}, bf16[32,2048]{1,0:T(8,128)(2,1)S(1)}, u32[]{:S(2)}, u32[]{:S(2)}) %collective-permute-start.30) | collective-permute-done | bytes 131104 | tf_op jit(solution)/shard_map/ppermute | solution.py:164
  86.5 5.3 %collective-permute-done.24 = bf16[32,2048]{1,0:T(8,128)(2,1)S(1)} collective-permute-done((bf16[32,2048]{1,0:T(8,128)(2,1)S(1)}, bf16[32,2048]{1,0:T(8,128)(2,1)S(1)}, u32[]{:S(2)}, u32[]{:S(2)}) %collective-permute-start.24) | collective-permute-done | bytes 131104 | tf_op jit(solution)/shard_map/ppermute | solution.py:164
  (106 shorter events, 30.1 us)
Async XLA Ops:
  2.0 5.3 %collective-permute-start.1 = (bf16[2,128,128]{2,1,0:T(8,128)(2,1)S(1)}, bf16[2,128,128]{2,1,0:T(8,128)(2,1)S(1)}, u32[]{:S(2)}, u32[]{:S(2)}) collective-permute-start(bf16[2,128,128]{2,1,0:T(8,128)(2,1)S(1)} %pad_maximum_fusion.4.own_ref), channel_id=1, source_target_pairs={{0,8},{4,12},{8,0},{12,4},{1,9},{5,13},{9,1},{13,5},{2,10},{6,14},... | collective-permute-start | bytes 196616 | tf_op jit(solution)/shard_map/ppermute | solution.py:164
  16.0 13.1 %collective-permute-start.3 = (bf16[32,2048]{1,0:T(8,128)(2,1)}, bf16[32,2048]{1,0:T(8,128)(2,1)S(1)}, u32[]{:S(2)}, u32[]{:S(2)}) collective-permute-start(bf16[32,2048]{1,0:T(8,128)(2,1)} %get-tuple-element.21), channel_id=1, source_target_pairs={{0,2},{1,3},{2,0},{3,1},{4,6},{5,7},{6,4},{7,5},{8,10},{9,11},{10,... | collective-permute-start | bytes 393224 | tf_op jit(solution)/shard_map/ppermute | solution.py:164
  18.6 11.2 %collective-permute-start.4 = (bf16[32,2048]{1,0:T(8,128)(2,1)}, bf16[32,2048]{1,0:T(8,128)(2,1)S(1)}, u32[]{:S(2)}, u32[]{:S(2)}) collective-permute-start(bf16[32,2048]{1,0:T(8,128)(2,1)} %get-tuple-element.22), channel_id=1, source_target_pairs={{0,3},{1,2},{2,1},{3,0},{4,7},{5,6},{6,5},{7,4},{8,11},{9,10},{10,... | collective-permute-start | bytes 393224 | tf_op jit(solution)/shard_map/ppermute | solution.py:164
  20.0 10.5 %collective-permute-start.5 = (bf16[32,2048]{1,0:T(8,128)(2,1)}, bf16[32,2048]{1,0:T(8,128)(2,1)S(1)}, u32[]{:S(2)}, u32[]{:S(2)}) collective-permute-start(bf16[32,2048]{1,0:T(8,128)(2,1)} %get-tuple-element.23), channel_id=1, source_target_pairs={{0,1},{1,0},{2,3},{3,2},{4,5},{5,4},{6,7},{7,6},{8,9},{9,8},{10,11... | collective-permute-start | bytes 393224 | tf_op jit(solution)/shard_map/ppermute | solution.py:164
  35.7 12.9 %collective-permute-start.6 = (bf16[32,2048]{1,0:T(8,128)(2,1)S(1)}, bf16[32,2048]{1,0:T(8,128)(2,1)}, u32[]{:S(2)}, u32[]{:S(2)}) collective-permute-start(bf16[32,2048]{1,0:T(8,128)(2,1)S(1)} %get-tuple-element.25.own_ref), channel_id=1, source_target_pairs={{0,8},{4,12},{8,0},{12,4},{1,9},{5,13},{9,1},{13,5},{2,10},{6,14},... | collective-permute-start | bytes 393224 | tf_op jit(solution)/shard_map/ppermute | solution.py:164
  37.0 10.1 %collective-permute-start.25 = (bf16[32,2048]{1,0:T(8,128)(2,1)S(1)}, bf16[32,2048]{1,0:T(8,128)(2,1)}, u32[]{:S(2)}, u32[]{:S(2)}) collective-permute-start(bf16[32,2048]{1,0:T(8,128)(2,1)S(1)} %get-tuple-element.25.own_ref), channel_id=1, source_target_pairs={{0,3},{1,2},{2,1},{3,0},{4,7},{5,6},{6,5},{7,4},{8,11},{9,10},{10,... | collective-permute-start | bytes 393224 | tf_op jit(solution)/shard_map/ppermute | solution.py:164
  45.2 8.4 %collective-permute-start.19 = (bf16[32,2048]{1,0:T(8,128)(2,1)S(1)}, bf16[32,2048]{1,0:T(8,128)(2,1)S(1)}, u32[]{:S(2)}, u32[]{:S(2)}) collective-permute-start(bf16[32,2048]{1,0:T(8,128)(2,1)S(1)} %get-tuple-element.25.own_ref), channel_id=1, source_target_pairs={{0,2},{1,3},{2,0},{3,1},{4,6},{5,7},{6,4},{7,5},{8,10},{9,11},{10,... | collective-permute-start | bytes 393224 | tf_op jit(solution)/shard_map/ppermute | solution.py:164
  46.5 8.0 %collective-permute-start.13 = (bf16[32,2048]{1,0:T(8,128)(2,1)S(1)}, bf16[32,2048]{1,0:T(8,128)(2,1)S(1)}, u32[]{:S(2)}, u32[]{:S(2)}) collective-permute-start(bf16[32,2048]{1,0:T(8,128)(2,1)S(1)} %get-tuple-element.25.own_ref), channel_id=1, source_target_pairs={{0,1},{1,0},{2,3},{3,2},{4,5},{5,4},{6,7},{7,6},{8,9},{9,8},{10,11... | collective-permute-start | bytes 393224 | tf_op jit(solution)/shard_map/ppermute | solution.py:164
  47.1 8.5 %collective-permute-start.26 = (bf16[32,2048]{1,0:T(8,128)(2,1)}, bf16[32,2048]{1,0:T(8,128)(2,1)S(1)}, u32[]{:S(2)}, u32[]{:S(2)}) collective-permute-start(bf16[32,2048]{1,0:T(8,128)(2,1)} %collective-permute-done.25.own_ref), channel_id=1, source_target_pairs={{0,8},{4,12},{8,0},{12,4},{1,9},{5,13},{9,1},{13,5},{2,10},{6,14},... | collective-permute-start | bytes 393224 | tf_op jit(solution)/shard_map/ppermute | solution.py:164
  49.5 10.6 %collective-permute-start.7 = (bf16[2,32,2048]{2,1,0:T(8,128)(2,1)S(1)}, bf16[2,32,2048]{2,1,0:T(8,128)(2,1)S(1)}, u32[]{:S(2)}, u32[]{:S(2)}) collective-permute-start(bf16[2,32,2048]{2,1,0:T(8,128)(2,1)S(1)} %pad_maximum_fusion), channel_id=1, source_target_pairs={{0,4},{4,0},{8,12},{12,8},{1,5},{5,1},{9,13},{13,9},{2,6},{6,2},{1... | collective-permute-start | bytes 786440 | tf_op jit(solution)/shard_map/ppermute | solution.py:164
  53.6 5.0 %collective-permute-start.20 = (bf16[32,2048]{1,0:T(8,128)(2,1)S(1)}, bf16[32,2048]{1,0:T(8,128)(2,1)S(1)}, u32[]{:S(2)}, u32[]{:S(2)}) collective-permute-start(bf16[32,2048]{1,0:T(8,128)(2,1)S(1)} %collective-permute-done.19.own_ref), channel_id=1, source_target_pairs={{0,8},{4,12},{8,0},{12,4},{1,9},{5,13},{9,1},{13,5},{2,10},{6,14},... | collective-permute-start | bytes 393224 | tf_op jit(solution)/shard_map/ppermute | solution.py:164
  54.5 5.4 %collective-permute-start.14 = (bf16[32,2048]{1,0:T(8,128)(2,1)S(1)}, bf16[32,2048]{1,0:T(8,128)(2,1)S(1)}, u32[]{:S(2)}, u32[]{:S(2)}) collective-permute-start(bf16[32,2048]{1,0:T(8,128)(2,1)S(1)} %collective-permute-done.13.own_ref), channel_id=1, source_target_pairs={{0,8},{4,12},{8,0},{12,4},{1,9},{5,13},{9,1},{13,5},{2,10},{6,14},... | collective-permute-start | bytes 393224 | tf_op jit(solution)/shard_map/ppermute | solution.py:164
  56.5 7.5 %collective-permute-start.27 = (bf16[2,32,2048]{2,1,0:T(8,128)(2,1)S(1)}, bf16[2,32,2048]{2,1,0:T(8,128)(2,1)S(1)}, u32[]{:S(2)}, u32[]{:S(2)}) collective-permute-start(bf16[2,32,2048]{2,1,0:T(8,128)(2,1)S(1)} %pad_maximum_fusion.3), channel_id=1, source_target_pairs={{0,4},{4,0},{8,12},{12,8},{1,5},{5,1},{9,13},{13,9},{2,6},{6,2},{1... | collective-permute-start | bytes 786440 | tf_op jit(solution)/shard_map/ppermute | solution.py:164
  58.6 7.6 %collective-permute-start.21 = (bf16[2,32,2048]{2,1,0:T(8,128)(2,1)S(1)}, bf16[2,32,2048]{2,1,0:T(8,128)(2,1)S(1)}, u32[]{:S(2)}, u32[]{:S(2)}) collective-permute-start(bf16[2,32,2048]{2,1,0:T(8,128)(2,1)S(1)} %pad_maximum_fusion.2), channel_id=1, source_target_pairs={{0,4},{4,0},{8,12},{12,8},{1,5},{5,1},{9,13},{13,9},{2,6},{6,2},{1... | collective-permute-start | bytes 786440 | tf_op jit(solution)/shard_map/ppermute | solution.py:164
  60.0 7.8 %collective-permute-start.15 = (bf16[2,32,2048]{2,1,0:T(8,128)(2,1)S(1)}, bf16[2,32,2048]{2,1,0:T(8,128)(2,1)S(1)}, u32[]{:S(2)}, u32[]{:S(2)}) collective-permute-start(bf16[2,32,2048]{2,1,0:T(8,128)(2,1)S(1)} %pad_maximum_fusion.1), channel_id=1, source_target_pairs={{0,4},{4,0},{8,12},{12,8},{1,5},{5,1},{9,13},{13,9},{2,6},{6,2},{1... | collective-permute-start | bytes 786440 | tf_op jit(solution)/shard_map/ppermute | solution.py:164
  63.5 5.5 %collective-permute-start.11 = (bf16[2,32,2048]{2,1,0:T(8,128)(2,1)S(1)}, bf16[2,32,2048]{2,1,0:T(8,128)(2,1)S(1)}, u32[]{:S(2)}, u32[]{:S(2)}) collective-permute-start(bf16[2,32,2048]{2,1,0:T(8,128)(2,1)S(1)} %get-tuple-element.29), channel_id=1, source_target_pairs={{0,4},{4,0},{8,12},{12,8},{1,5},{5,1},{9,13},{13,9},{2,6},{6,2},{1... | collective-permute-start | bytes 786440 | tf_op jit(solution)/shard_map/ppermute | solution.py:164
  67.2 4.1 %collective-permute-start.22 = (bf16[2,32,2048]{2,1,0:T(8,128)(2,1)S(1)}, bf16[2,32,2048]{2,1,0:T(8,128)(2,1)S(1)}, u32[]{:S(2)}, u32[]{:S(2)}) collective-permute-start(bf16[2,32,2048]{2,1,0:T(8,128)(2,1)S(1)} %get-tuple-element.33), channel_id=1, source_target_pairs={{0,4},{4,0},{8,12},{12,8},{1,5},{5,1},{9,13},{13,9},{2,6},{6,2},{1... | collective-permute-start | bytes 786440 | tf_op jit(solution)/shard_map/ppermute | solution.py:164
  69.1 15.2 %collective-permute-start.12 = (bf16[32,2048]{1,0:T(8,128)(2,1)S(1)}, bf16[32,2048]{1,0:T(8,128)(2,1)S(1)}, u32[]{:S(2)}, u32[]{:S(2)}) collective-permute-start(bf16[32,2048]{1,0:T(8,128)(2,1)S(1)} %fusion.20), channel_id=1, source_target_pairs={{0,8},{4,12},{8,0},{12,4},{1,9},{5,13},{9,1},{13,5},{2,10},{6,14},... | collective-permute-start | bytes 393224 | tf_op jit(solution)/shard_map/ppermute | solution.py:164
  70.1 8.1 %collective-permute-start.29 = (bf16[32,2048]{1,0:T(8,128)(2,1)S(1)}, bf16[32,2048]{1,0:T(8,128)(2,1)S(1)}, u32[]{:S(2)}, u32[]{:S(2)}) collective-permute-start(bf16[32,2048]{1,0:T(8,128)(2,1)S(1)} %fusion.23), channel_id=1, source_target_pairs={{0,8},{4,12},{8,0},{12,4},{1,9},{5,13},{9,1},{13,5},{2,10},{6,14},... | collective-permute-start | bytes 393224 | tf_op jit(solution)/shard_map/ppermute | solution.py:164
  71.4 9.7 %collective-permute-start.23 = (bf16[32,2048]{1,0:T(8,128)(2,1)S(1)}, bf16[32,2048]{1,0:T(8,128)(2,1)S(1)}, u32[]{:S(2)}, u32[]{:S(2)}) collective-permute-start(bf16[32,2048]{1,0:T(8,128)(2,1)S(1)} %fusion.22), channel_id=1, source_target_pairs={{0,8},{4,12},{8,0},{12,4},{1,9},{5,13},{9,1},{13,5},{2,10},{6,14},... | collective-permute-start | bytes 393224 | tf_op jit(solution)/shard_map/ppermute | solution.py:164
  72.5 11.0 %collective-permute-start.17 = (bf16[32,2048]{1,0:T(8,128)(2,1)S(1)}, bf16[32,2048]{1,0:T(8,128)(2,1)S(1)}, u32[]{:S(2)}, u32[]{:S(2)}) collective-permute-start(bf16[32,2048]{1,0:T(8,128)(2,1)S(1)} %fusion.21), channel_id=1, source_target_pairs={{0,8},{4,12},{8,0},{12,4},{1,9},{5,13},{9,1},{13,5},{2,10},{6,14},... | collective-permute-start | bytes 393224 | tf_op jit(solution)/shard_map/ppermute | solution.py:164
  78.3 8.2 %collective-permute-start.30 = (bf16[32,2048]{1,0:T(8,128)(2,1)S(1)}, bf16[32,2048]{1,0:T(8,128)(2,1)S(1)}, u32[]{:S(2)}, u32[]{:S(2)}) collective-permute-start(bf16[32,2048]{1,0:T(8,128)(2,1)S(1)} %fusion.3), channel_id=1, source_target_pairs={{0,3},{1,2},{2,1},{3,0},{4,7},{5,6},{6,5},{7,4},{8,11},{9,10},{10,... | collective-permute-start | bytes 393224 | tf_op jit(solution)/shard_map/ppermute | solution.py:164
  81.1 10.7 %collective-permute-start.24 = (bf16[32,2048]{1,0:T(8,128)(2,1)S(1)}, bf16[32,2048]{1,0:T(8,128)(2,1)S(1)}, u32[]{:S(2)}, u32[]{:S(2)}) collective-permute-start(bf16[32,2048]{1,0:T(8,128)(2,1)S(1)} %fusion.7), channel_id=1, source_target_pairs={{0,2},{1,3},{2,0},{3,1},{4,6},{5,7},{6,4},{7,5},{8,10},{9,11},{10,... | collective-permute-start | bytes 393224 | tf_op jit(solution)/shard_map/ppermute | solution.py:164
  83.5 8.3 %collective-permute-start.18 = (bf16[32,2048]{1,0:T(8,128)(2,1)S(1)}, bf16[32,2048]{1,0:T(8,128)(2,1)S(1)}, u32[]{:S(2)}, u32[]{:S(2)}) collective-permute-start(bf16[32,2048]{1,0:T(8,128)(2,1)S(1)} %fusion.11), channel_id=1, source_target_pairs={{0,1},{1,0},{2,3},{3,2},{4,5},{5,4},{6,7},{7,6},{8,9},{9,8},{10,11... | collective-permute-start | bytes 393224 | tf_op jit(solution)/shard_map/ppermute | solution.py:164
  (25 other events, 224.3 us)

commit v3 on v0

--- a/solution.py
+++ b/solution.py
@@ -1,8 +1,11 @@
+import functools
 import math
 
 import jax
 import jax.numpy as jnp
 from jax import lax
+from jax.experimental import pallas as pl
+from jax.experimental.pallas import tpu as pltpu
 from jax.sharding import PartitionSpec as P
 
 HEAD = 128
@@ -13,7 +16,7 @@
     return (proj_rows * inverse * norm_gain).astype(jnp.bfloat16)
 
 
-def per_device(
+def routed_plan(
     queries,
     keys,
     values,
@@ -152,6 +155,300 @@
     return (attended, layer_out)
 
 
+F32, BF16 = jnp.float32, jnp.bfloat16
+VMEM_SPEC = pl.BlockSpec(memory_space=pltpu.VMEM)
+HBM_SPEC = pl.BlockSpec(memory_space=pltpu.HBM)
+HIDDEN_SCORE = -1e30
+MIB = 1 << 20
+
+
+def swap(rows, axis, offset):
+    count = lax.axis_size(axis)
+    return lax.ppermute(rows, axis, [(i, i ^ offset) for i in range(count)])
+
+
+def call(kernel, outs, operands, scratch=(), flops=0, moved=0, limit=16 * MIB, from_hbm=0):
+    operands = [
+        pltpu.with_memory_space_constraint(x, pltpu.HBM) if i < from_hbm else x
+        for i, x in enumerate(operands)
+    ]
+    return pl.pallas_call(
+        kernel,
+        out_shape=outs,
+        in_specs=[HBM_SPEC] * from_hbm + [VMEM_SPEC] * (len(operands) - from_hbm),
+        out_specs=[VMEM_SPEC] * len(outs),
+        scratch_shapes=scratch,
+        compiler_params=pltpu.CompilerParams(vmem_limit_bytes=limit),
+        cost_estimate=pl.CostEstimate(flops=1024, bytes_accessed=1024, transcendentals=0),
+    )(*operands)
+
+
+def own_block_kernel(tp_count, *refs):
+    *sources, w_source = refs[:6]
+    w_ref, q_ref, max_ref, total_ref, acc_ref, *mix_refs = refs[6:-6]
+    k_ref, v_ref, ids_ref, weights_ref, arrived, w_arrived = refs[-6:]
+    targets = (q_ref, k_ref, v_ref, ids_ref, weights_ref)
+    copies = [
+        pltpu.make_async_copy(source, target, arrived.at[i])
+        for i, (source, target) in enumerate(zip(sources, targets))
+    ]
+    chunks = w_arrived.shape[0]
+    depth = w_ref.shape[0] // chunks
+    w_copies = [
+        pltpu.make_async_copy(
+            w_source.at[pl.ds(i * depth, depth)], w_ref.at[pl.ds(i * depth, depth)], w_arrived.at[i]
+        )
+        for i in range(chunks)
+    ]
+    for copy in copies + w_copies:
+        copy.start()
+    for copy in copies:
+        copy.wait()
+    ctx_index, tp_index = lax.axis_index("ctx"), lax.axis_index("tp")
+    block_rows = q_ref.shape[0]
+    kv_local = k_ref.shape[1] // HEAD
+    group_size = q_ref.shape[1] // k_ref.shape[1]
+    row = lax.broadcasted_iota(jnp.int32, (block_rows, block_rows), 0)
+    col = lax.broadcasted_iota(jnp.int32, (block_rows, block_rows), 1)
+    for g in range(kv_local):
+        key_rows = k_ref[:, g * HEAD : (g + 1) * HEAD]
+        value_rows = v_ref[:, g * HEAD : (g + 1) * HEAD]
+        for h in range(g * group_size, (g + 1) * group_size):
+            lanes = slice(h * HEAD, (h + 1) * HEAD)
+            scores = lax.dot_general(
+                q_ref[:, lanes], key_rows, (((1,), (1,)), ((), ())), preferred_element_type=F32
+            )
+            scores = jnp.where(col <= row, scores * HEAD ** (-0.5), HIDDEN_SCORE)
+            top = jnp.max(scores, axis=1, keepdims=True)
+            weights = jnp.exp(scores - top)
+            max_ref[:, h : h + 1] = top
+            total_ref[:, h : h + 1] = jnp.sum(weights, axis=1, keepdims=True)
+            acc_ref[:, lanes] = jnp.dot(weights.astype(BF16), value_rows, preferred_element_type=F32)
+    share = weights_ref[...] / jnp.sum(weights_ref[...], axis=0, keepdims=True)
+    for d, mix_ref in enumerate(mix_refs):
+        expert = (ctx_index ^ d) * tp_count + tp_index
+        mix_ref[...] = jnp.sum(jnp.where(ids_ref[...] == expert, share, 0.0), axis=0, keepdims=True)
+    for copy in w_copies:
+        copy.wait()
+
+
+def other_blocks_kernel(tp_count, others, *refs):
+    w_ref, q_ref, max_ref, total_ref, acc_ref = refs[:5]
+    k_refs, v_refs = refs[5 : 5 + others], refs[5 + others : 5 + 2 * others]
+    att_ref, *piece_refs = refs[5 + 2 * others : -1]
+    scratch = refs[-1]
+    ctx_index, tp_index = lax.axis_index("ctx"), lax.axis_index("tp")
+    block_rows = q_ref.shape[0]
+    kv_local = k_refs[0].shape[1] // HEAD
+    group_size = q_ref.shape[1] // k_refs[0].shape[1]
+    bias = jnp.concatenate(
+        [
+            jnp.full((1, block_rows), jnp.where((ctx_index ^ d) < ctx_index, 0.0, HIDDEN_SCORE))
+            for d in range(1, others + 1)
+        ],
+        axis=1,
+    )
+    for g in range(kv_local):
+        kv_lanes = slice(g * HEAD, (g + 1) * HEAD)
+        key_rows = jnp.concatenate([r[:, kv_lanes] for r in k_refs], axis=0)
+        value_rows = jnp.concatenate([r[:, kv_lanes] for r in v_refs], axis=0)
+        for h in range(g * group_size, (g + 1) * group_size):
+            lanes = slice(h * HEAD, (h + 1) * HEAD)
+            scores = lax.dot_general(
+                q_ref[:, lanes], key_rows, (((1,), (1,)), ((), ())), preferred_element_type=F32
+            )
+            scores = scores * HEAD ** (-0.5) + bias
+            old = max_ref[:, h : h + 1]
+            top = jnp.maximum(old, jnp.max(scores, axis=1, keepdims=True))
+            weights = jnp.exp(scores - top)
+            rescale = jnp.exp(old - top)
+            total = total_ref[:, h : h + 1] * rescale + jnp.sum(weights, axis=1, keepdims=True)
+            accum = acc_ref[:, lanes] * rescale + jnp.dot(
+                weights.astype(BF16), value_rows, preferred_element_type=F32
+            )
+            att_ref[:, lanes] = (accum * (1.0 / total)).astype(BF16)
+    piece_rows = block_rows // tp_count
+    scratch[...] = jnp.dot(att_ref[...], w_ref[...], preferred_element_type=F32)
+    for d in range(tp_count):
+        start = pl.multiple_of((tp_index ^ d) * piece_rows, piece_rows)
+        piece_refs[d][...] = scratch[pl.ds(start, piece_rows), :].astype(piece_refs[d].dtype)
+
+
+def norm_kernel(ctx_count, gain_ref, *refs):
+    mix_refs, parts = refs[:ctx_count], refs[ctx_count:-6]
+    proj_ref, normed_ref, column_ref = refs[-3:]
+    proj = parts[0][...]
+    for part in parts[1:]:
+        proj = proj + part[...].astype(F32)
+    proj_ref[...] = proj
+    inverse = lax.rsqrt(jnp.mean(proj * proj, axis=1, keepdims=True) + 1e-06)
+    normed_ref[...] = (proj * inverse * gain_ref[...]).astype(BF16)
+    column_ref[...] = jnp.concatenate([r[...] for r in mix_refs], axis=0).T
+
+
+def expert_kernel(offsets, *refs):
+    count = len(refs) // 2 - 2
+    token_refs, out_refs = refs[:count], refs[-count:]
+    column_ref, gate_ref, up_ref, down_ref = refs[count : count + 4]
+    rows = token_refs[0].shape[0]
+    tokens = jnp.concatenate([r[...] for r in token_refs], axis=0)
+    gate_proj = jnp.dot(tokens, gate_ref[0], preferred_element_type=F32)
+    up_proj = jnp.dot(tokens, up_ref[0], preferred_element_type=F32)
+    activated = (gate_proj / (1.0 + jnp.exp(-gate_proj)) * up_proj).astype(BF16)
+    out = jnp.dot(activated, down_ref[0], preferred_element_type=F32)
+    partners = count // len(offsets)
+    for i, out_ref in enumerate(out_refs):
+        start = pl.multiple_of((lax.axis_index("tp") ^ offsets[i // partners]) * rows, rows)
+        mix = column_ref[pl.ds(start, rows), i % partners : i % partners + 1]
+        out_ref[...] = (out[i * rows : (i + 1) * rows] * mix).astype(out_ref.dtype)
+
+
+def sum_kernel(*refs):
+    total = refs[0][...].astype(F32)
+    for ref in refs[1:-1]:
+        total = total + ref[...].astype(F32)
+    refs[-1][...] = total.astype(refs[-1].dtype)
+
+
+def dense_plan(
+    queries,
+    keys,
+    values,
+    out_weight,
+    norm_gain,
+    expert_gate,
+    expert_up,
+    expert_down,
+    expert_ids,
+    route_weights,
+):
+    ctx_count = lax.axis_size("ctx")
+    tp_count = lax.axis_size("tp")
+    block_rows, width = queries.shape
+    heads = width // HEAD
+    piece_rows = block_rows // tp_count
+    features = out_weight.shape[1]
+    shape = jax.ShapeDtypeStruct
+
+    far_k, far_v = swap(keys, "ctx", 2), swap(values, "ctx", 2)
+    near_k, near_v = swap(keys, "ctx", 1), swap(values, "ctx", 1)
+    projection, queries, top, total, accum, *mixes = call(
+        functools.partial(own_block_kernel, tp_count),
+        [shape(out_weight.shape, BF16), shape((block_rows, width), BF16)]
+        + [shape((block_rows, heads), F32)] * 2
+        + [shape((block_rows, width), F32)]
+        + [shape((1, block_rows), F32)] * ctx_count,
+        (queries, keys, values, expert_ids.T, route_weights.T, out_weight),
+        scratch=[
+            pltpu.VMEM(keys.shape, BF16),
+            pltpu.VMEM(values.shape, BF16),
+            pltpu.VMEM(expert_ids.T.shape, jnp.int32),
+            pltpu.VMEM(route_weights.T.shape, F32),
+            pltpu.SemaphoreType.DMA((5,)),
+            pltpu.SemaphoreType.DMA((4,)),
+        ],
+        flops=4 * block_rows * block_rows * width,
+        moved=queries.size * 6,
+        from_hbm=6,
+    )
+    far_k, far_v, top = lax.optimization_barrier((far_k, far_v, top))
+    ks = [near_k, far_k, swap(far_k, "ctx", 1)]
+    vs = [near_v, far_v, swap(far_v, "ctx", 1)]
+    piece = shape((piece_rows, features), BF16)
+    piece32 = shape((piece_rows, features), F32)
+    attended, *partials = call(
+        functools.partial(other_blocks_kernel, tp_count, ctx_count - 1),
+        [shape((block_rows, width), BF16), piece32] + [piece] * (tp_count - 1),
+        (projection, queries, top, total, accum, *ks, *vs),
+        scratch=[pltpu.VMEM((block_rows, features), F32)],
+        flops=2 * block_rows * width * features + 4 * block_rows * block_rows * ctx_count * width,
+        moved=out_weight.size * 2,
+    )
+
+    arrived = [swap(partials[d], "tp", d) for d in (2, 3, 1)]
+    mixes = mixes[:1] + [swap(mixes[d], "ctx", d) for d in range(1, ctx_count)]
+    own_proj, normed, columns = call(
+        functools.partial(norm_kernel, ctx_count),
+        [piece32, piece, shape((block_rows, ctx_count), F32)],
+        (
+            norm_gain.reshape(1, features),
+            *mixes,
+            partials[0],
+            *arrived,
+            expert_gate,
+            expert_up,
+            expert_down,
+        ),
+        flops=8 * piece_rows * features,
+    )
+
+    def after(values, *earlier):
+        return lax.optimization_barrier((tuple(values), earlier))[0]
+
+    def work(group, tokens):
+        found = call(
+            functools.partial(expert_kernel, group),
+            [piece32, piece, piece32, piece] * len(group),
+            (*tokens, columns, expert_gate, expert_up, expert_down),
+            flops=6 * ctx_count * piece_rows * features * expert_gate.shape[2],
+            moved=3 * expert_gate.size * 2,
+        )
+        return [found[4 * i : 4 * i + 4] for i in range(len(group))]
+
+    def spread(rows, far):
+        return [rows, swap(rows, "ctx", 1), far, swap(far, "ctx", 1)]
+
+    def gather_results(out):
+        out0, out1, out2, out3 = out
+        got0, got2 = swap(out1, "ctx", 1), swap(out3, "ctx", 1)
+        (far_part,) = call(sum_kernel, [piece], (out2, got2))
+        return [out0, got0, far_part]
+
+    def send_back(parts, d):
+        out0, got0, far_part = parts
+        parts = [out0, got0, swap(far_part, "ctx", 2)]
+        if not d:
+            return parts
+        (tp_part,) = call(sum_kernel, [piece], parts)
+        return [swap(tp_part, "tp", d)]
+
+    rows2, rows1 = swap(normed, "tp", 2), swap(normed, "tp", 1)
+    far0 = swap(normed, "ctx", 2)
+    far1 = swap(rows1, "ctx", 2)
+    far2 = swap(rows2, "ctx", 2)
+    rows3 = swap(rows2, "tp", 1)
+    rows0, far0, rows1, far1 = after((normed, far0, rows1, far1), rows2)
+    tokens = spread(rows0, far0) + spread(rows1, far1)
+    far3 = swap(rows3, "ctx", 2)
+    tokens = after(tokens, rows3, far2)
+    out0, out1 = work((0, 1), tokens)
+    parts1, parts0 = gather_results(out1), gather_results(out0)
+    rows2, far2, rows3, far3 = after((rows2, far2, rows3, far3), out0[0])
+    tokens = spread(rows2, far2) + spread(rows3, far3)
+    tokens = after(tokens, parts1[2], parts0[2])
+    back1 = swap(parts1[2], "ctx", 2)
+    out2, out3 = work((2, 3), tokens)
+    (tp1,) = call(sum_kernel, [piece], (*parts1[:2], back1))
+    ret1 = swap(tp1, "tp", 1)
+    parts2, parts3 = gather_results(out2), gather_results(out3)
+    back2, back3 = swap(parts2[2], "ctx", 2), swap(parts3[2], "ctx", 2)
+    (tp2,) = call(sum_kernel, [piece], (*parts2[:2], *after((back2,), ret1)))
+    (tp3,) = call(sum_kernel, [piece], (*parts3[:2], back3))
+    results = [own_proj, ret1, swap(tp2, "tp", 2), swap(tp3, "tp", 3)]
+    parts0 = after(parts0, back3)
+    results += send_back(parts0, 0)
+    (layer_out,) = call(sum_kernel, [piece], results)
+    return (attended, layer_out)
+
+
+def per_device(*arguments):
+    ctx_count, tp_count = lax.axis_size("ctx"), lax.axis_size("tp")
+    top_count = arguments[8].shape[1]
+    if ctx_count == 4 and tp_count == 4 and ctx_count * tp_count <= 2 * top_count:
+        return dense_plan(*arguments)
+    return routed_plan(*arguments)
+
+
 def solution(mesh):
     in_specs = (
         P(("dp", "ctx"), "tp"),

time: 152 us -> 77 us (0.51)
  blocking collectives: 51.2 us -> 0 us
  starting transfers between devices: 3.77 us -> 35.6 us
  waiting for transfers between devices: 58.8 us -> 27.6 us
  matrix products: 14.6 us -> 0 us
  between operations: 14.2 us -> 0.81 us
  Pallas kernels: 0 us -> 12.8 us
  other arithmetic: 7.06 us -> 0 us
  local copies, waits for them, and re-layouts: 1.87 us -> 0.01 us
    reduce_scatter x2 -> x0, waiting for transfers between devices: 39.4 us -> none  [the longest x1 20.3 us: per_device(): lax.psum_scatter(jnp.dot(attended, out_weight, preferred_element_type=jnp...]
    ppermute x0 -> x42, starting transfers between devices: none -> 35.6 us  [swap(): return lax.ppermute(rows, axis, [(i, i ^ offset) for i in range(count)])]
    all_gather x3 -> x0, blocking collectives: 28.5 us -> none  [the longest x1 15.8 us: per_device(): lax.all_gather(rms_scale(own_proj, norm_gain), 'tp', axis=0, tiled=True)]
    ppermute x0 -> x42, waiting for transfers between devices: none -> 27.6 us  [swap(): return lax.ppermute(rows, axis, [(i, i ^ offset) for i in range(count)])]
    all_to_all x1 -> x0, blocking collectives: 22.7 us -> none  [per_device(): lax.all_to_all(outgoing, 'ctx', split_axis=0, concat_axis=0, tiled=True)]
    all_to_all x1 -> x0, waiting for transfers between devices: 19.3 us -> none  [per_device(): lax.all_to_all(expert_out, 'ctx', split_axis=0, concat_axis=0, tiled=True)]
    dot_general x8 -> x0, matrix products: 14.6 us -> none  [the longest x1 4.57 us: per_device(): jnp.dot(activated, expert_down[0], preferred_element_type=jnp.float32)]
    pallas_call x0 -> x13, Pallas kernels: none -> 12.8 us  [call(): pl.pallas_call(kernel, out_shape=outs, in_specs=[HBM_SPEC] * from_hbm + [...]
  transfers between devices with their start and end apart: 3 -> 42, of which waited for: 3 -> 15; matrix products, arithmetic and copies ran while one was open for 2% -> 0% of each run, Pallas kernels for 0% -> 10%
where the time goes in v3:
time: 77 us; the launch traced here: 76.8 us
  starting transfers between devices  35.6 us (46%)
  waiting for transfers between devices  27.6 us (36%)
  Pallas kernels  12.8 us (17%)
  between operations  0.81 us (1%)
    ppermute x42, starting transfers between devices, swap(): return lax.ppermute(rows, axis, [(i, i ^ offset) for i in range(count)])  35.6 us
    ppermute x42, waiting for transfers between devices, swap(): return lax.ppermute(rows, axis, [(i, i ^ offset) for i in range(count)])  27.6 us
    pallas_call x13, Pallas kernels, call(): pl.pallas_call(kernel, out_shape=outs, in_specs=[HBM_SPEC] * from_hbm + [...  12.8 us
  transfers between devices with their start and end apart: 42, of which 15 were waited for; matrix products, arithmetic and copies ran while one was open for 0% of the time, Pallas kernels for 10%

profile of v3, /device:TPU:0, one launch (start us, length us, event | category | flops | bytes accessed | tf_op | source)
XLA Modules:
  0.0 76.8 jit_solution(11686987750437090808)
XLA Ops:
  0.6 3.0 %collective-permute-start = (bf16[128,128]{1,0:T(8,128)(2,1)}, bf16[128,128]{1,0:T(8,128)(2,1)S(1)}, u32[]{:S(2)}, u32[]{:S(2)}) collective-permute-start(bf16[128,128]{1,0:T(8,128)(2,1)} %refs_1_.1), channel_id=1, source_target_pairs={{0,8},{4,12},{8,0},{12,4},{1,9},{5,13},{9,1},{13,5},{2,10},{6,14},... | collective-permute-start | bytes 98312 | tf_op jit(solution)/shard_map/ppermute | solution.py:167
  4.2 3.9 %shard_map.113 = (bf16[1024,2048]{1,0:T(8,128)(2,1)S(1)}, bf16[128,1024]{1,0:T(8,128)(2,1)S(1)}, f32[128,8]{1,0:T(8,128)S(1)}, f32[128,8]{1,0:T(8,128)S(1)}, f32...) custom-call(bf16[128,1024]{1,0:T(8,128)(2,1)} %refs_0_.1, ...), custom_call_target="tpu_custom_call" | custom-call | flops 1024 | bytes 1024 | tf_op jit(solution)/shard_map/pallas_call | solution.py:175
  9.6 4.0 %shard_map.114 = (bf16[128,1024]{1,0:T(8,128)(2,1)}, f32[32,2048]{1,0:T(8,128)S(1)}, bf16[32,2048]{1,0:T(8,128)(2,1)S(1)}, bf16[32,2048]{1,0:T(8,128)(2,1)S(1)}, bf16[32,2048]{1,0:T(8,128)(2,1)S(1)}) custom-call(bf16[1024,2048]{1,0:T(8,128)(2,1)S(1)} %get-tuple-element.66.refs_0_, bf16[128,1024]{1,0:T(8,128)(2,1)S(1)} %get-tuple-element.67.refs_1_, ...), custom_call_target="tpu_custom_call" | custom-call | flops 1024 | bytes 1024 | tf_op jit(solution)/shard_map/pallas_call | solution.py:175
  13.6 3.0 %collective-permute-start.9 = (bf16[32,2048]{1,0:T(8,128)(2,1)S(1)}, bf16[32,2048]{1,0:T(8,128)(2,1)S(1)}, u32[]{:S(2)}, u32[]{:S(2)}) collective-permute-start(bf16[32,2048]{1,0:T(8,128)(2,1)S(1)} %get-tuple-element.80), channel_id=1, source_target_pairs={{0,2},{1,3},{2,0},{3,1},{4,6},{5,7},{6,4},{7,5},{8,10},{9,11},{10,... | collective-permute-start | bytes 393224 | tf_op jit(solution)/shard_map/ppermute | solution.py:167
  16.6 1.3 %collective-permute-start.10 = (bf16[32,2048]{1,0:T(8,128)(2,1)S(1)}, bf16[32,2048]{1,0:T(8,128)(2,1)S(1)}, u32[]{:S(2)}, u32[]{:S(2)}) collective-permute-start(bf16[32,2048]{1,0:T(8,128)(2,1)S(1)} %get-tuple-element.81), channel_id=1, source_target_pairs={{0,3},{1,2},{2,1},{3,0},{4,7},{5,6},{6,5},{7,4},{8,11},{9,10},{10,... | collective-permute-start | bytes 393224 | tf_op jit(solution)/shard_map/ppermute | solution.py:167
  18.2 1.5 %collective-permute-start.7 = (f32[1,128]{1,0:T(1,128)S(1)}, f32[1,128]{1,0:T(1,128)S(1)}, u32[]{:S(2)}, u32[]{:S(2)}) collective-permute-start(f32[1,128]{1,0:T(1,128)S(1)} %get-tuple-element.77), channel_id=1, source_target_pairs={{0,8},{4,12},{8,0},{12,4},{1,9},{5,13},{9,1},{13,5},{2,10},{6,14},... | collective-permute-start | bytes 1544 | tf_op jit(solution)/shard_map/ppermute | solution.py:167
  22.6 4.0 %collective-permute-done.9.refs_5_ = bf16[32,2048]{1,0:T(8,128)(2,1)S(1)} collective-permute-done((bf16[32,2048]{1,0:T(8,128)(2,1)S(1)}, bf16[32,2048]{1,0:T(8,128)(2,1)S(1)}, u32[]{:S(2)}, u32[]{:S(2)}) %collective-permute-start.9) | collective-permute-done | bytes 131104 | tf_op jit(solution)/shard_map/ppermute | solution.py:167
  27.8 2.3 %collective-permute-start.13 = (bf16[32,2048]{1,0:T(8,128)(2,1)S(1)}, bf16[32,2048]{1,0:T(8,128)(2,1)S(1)}, u32[]{:S(2)}, u32[]{:S(2)}) collective-permute-start(bf16[32,2048]{1,0:T(8,128)(2,1)S(1)} %get-tuple-element.89.refs_0_), channel_id=1, source_target_pairs={{0,1},{1,0},{2,3},{3,2},{4,5},{5,4},{6,7},{7,6},{8,9},{9,8},{10,11... | collective-permute-start | bytes 393224 | tf_op jit(solution)/shard_map/ppermute | solution.py:167
  30.1 2.0 %collective-permute-start.15 = (bf16[32,2048]{1,0:T(8,128)(2,1)S(1)}, bf16[32,2048]{1,0:T(8,128)(2,1)S(1)}, u32[]{:S(2)}, u32[]{:S(2)}) collective-permute-start(bf16[32,2048]{1,0:T(8,128)(2,1)S(1)} %get-tuple-element.89.refs_0_), channel_id=1, source_target_pairs={{0,2},{1,3},{2,0},{3,1},{4,6},{5,7},{6,4},{7,5},{8,10},{9,11},{10,... | collective-permute-start | bytes 393224 | tf_op jit(solution)/shard_map/ppermute | solution.py:167
  32.1 1.5 %collective-permute-start.12 = (bf16[32,2048]{1,0:T(8,128)(2,1)S(1)}, bf16[32,2048]{1,0:T(8,128)(2,1)S(1)}, u32[]{:S(2)}, u32[]{:S(2)}) collective-permute-start(bf16[32,2048]{1,0:T(8,128)(2,1)S(1)} %get-tuple-element.89.refs_0_), channel_id=1, source_target_pairs={{0,8},{4,12},{8,0},{12,4},{1,9},{5,13},{9,1},{13,5},{2,10},{6,14},... | collective-permute-start | bytes 393224 | tf_op jit(solution)/shard_map/ppermute | solution.py:167
  33.6 3.0 %collective-permute-done.13.refs_4_ = bf16[32,2048]{1,0:T(8,128)(2,1)S(1)} collective-permute-done((bf16[32,2048]{1,0:T(8,128)(2,1)S(1)}, bf16[32,2048]{1,0:T(8,128)(2,1)S(1)}, u32[]{:S(2)}, u32[]{:S(2)}) %collective-permute-start.13) | collective-permute-done | bytes 131104 | tf_op jit(solution)/shard_map/ppermute | solution.py:167
  36.6 1.5 %collective-permute-start.14 = (bf16[32,2048]{1,0:T(8,128)(2,1)S(1)}, bf16[32,2048]{1,0:T(8,128)(2,1)S(1)}, u32[]{:S(2)}, u32[]{:S(2)}) collective-permute-start(bf16[32,2048]{1,0:T(8,128)(2,1)S(1)} %collective-permute-done.13.refs_4_), channel_id=1, source_target_pairs={{0,8},{4,12},{8,0},{12,4},{1,9},{5,13},{9,1},{13,5},{2,10},{6,14},... | collective-permute-start | bytes 393224 | tf_op jit(solution)/shard_map/ppermute | solution.py:167
  38.6 3.1 %collective-permute-start.20 = (bf16[32,2048]{1,0:T(8,128)(2,1)S(1)}, bf16[32,2048]{1,0:T(8,128)(2,1)S(1)}, u32[]{:S(2)}, u32[]{:S(2)}) collective-permute-start(bf16[32,2048]{1,0:T(8,128)(2,1)S(1)} %collective-permute-done.15.refs_0_), channel_id=1, source_target_pairs={{0,1},{1,0},{2,3},{3,2},{4,5},{5,4},{6,7},{7,6},{8,9},{9,8},{10,11... | collective-permute-start | bytes 393224 | tf_op jit(solution)/shard_map/ppermute | solution.py:167
  43.1 1.6 %collective-permute-done.20.refs_4_ = bf16[32,2048]{1,0:T(8,128)(2,1)S(1)} collective-permute-done((bf16[32,2048]{1,0:T(8,128)(2,1)S(1)}, bf16[32,2048]{1,0:T(8,128)(2,1)S(1)}, u32[]{:S(2)}, u32[]{:S(2)}) %collective-permute-start.20) | collective-permute-done | bytes 131104 | tf_op jit(solution)/shard_map/ppermute | solution.py:167
  45.3 1.9 %shard_map.116 = (f32[32,2048]{1,0:T(8,128)S(1)}, bf16[32,2048]{1,0:T(8,128)(2,1)S(1)}, f32[32,2048]{1,0:T(8,128)S(1)}, bf16[32,2048]{1,0:T(8,128)(2,1)S(1)}, f3...) custom-call(bf16[32,2048]{1,0:T(8,128)(2,1)S(1)} %get-tuple-element., ...), custom_call_target="tpu_custom_call" | custom-call | flops 1024 | bytes 1024 | tf_op jit(solution)/shard_map/pallas_call | solution.py:175
  47.2 2.4 %collective-permute-done.26.refs_6_ = bf16[32,2048]{1,0:T(8,128)(2,1)S(1)} collective-permute-done((bf16[32,2048]{1,0:T(8,128)(2,1)S(1)}, bf16[32,2048]{1,0:T(8,128)(2,1)S(1)}, u32[]{:S(2)}, u32[]{:S(2)}) %collective-permute-start.26) | collective-permute-done | bytes 131104 | tf_op jit(solution)/shard_map/ppermute | solution.py:167
  52.1 1.9 %shard_map.120 = (f32[32,2048]{1,0:T(8,128)S(1)}, bf16[32,2048]{1,0:T(8,128)(2,1)S(1)}, f32[32,2048]{1,0:T(8,128)S(1)}, bf16[32,2048]{1,0:T(8,128)(2,1)S(1)}, f3...) custom-call(bf16[32,2048]{1,0:T(8,128)(2,1)S(1)} %collective-permute, ...), custom_call_target="tpu_custom_call" | custom-call | flops 1024 | bytes 1024 | tf_op jit(solution)/shard_map/pallas_call | solution.py:175
  54.6 2.4 %collective-permute-done.24.refs_2_ = bf16[32,2048]{1,0:T(8,128)(2,1)S(1)} collective-permute-done((bf16[32,2048]{1,0:T(8,128)(2,1)S(1)}, bf16[32,2048]{1,0:T(8,128)(2,1)S(1)}, u32[]{:S(2)}, u32[]{:S(2)}) %collective-permute-start.24) | collective-permute-done | bytes 131104 | tf_op jit(solution)/shard_map/ppermute | solution.py:167
  57.0 2.1 %collective-permute-start.25 = (bf16[32,2048]{1,0:T(8,128)(2,1)S(1)}, bf16[32,2048]{1,0:T(8,128)(2,1)S(1)}, u32[]{:S(2)}, u32[]{:S(2)}) collective-permute-start(bf16[32,2048]{1,0:T(8,128)(2,1)S(1)} %shard_map.118), channel_id=1, source_target_pairs={{0,1},{1,0},{2,3},{3,2},{4,5},{5,4},{6,7},{7,6},{8,9},{9,8},{10,11... | collective-permute-start | bytes 393224 | tf_op jit(solution)/shard_map/ppermute | solution.py:167
  60.7 1.1 %collective-permute-start.38 = (bf16[32,2048]{1,0:T(8,128)(2,1)S(1)}, bf16[32,2048]{1,0:T(8,128)(2,1)S(1)}, u32[]{:S(2)}, u32[]{:S(2)}) collective-permute-start(bf16[32,2048]{1,0:T(8,128)(2,1)S(1)} %shard_map.123), channel_id=1, source_target_pairs={{0,8},{4,12},{8,0},{12,4},{1,9},{5,13},{9,1},{13,5},{2,10},{6,14},... | collective-permute-start | bytes 393224 | tf_op jit(solution)/shard_map/ppermute | solution.py:167
  62.2 2.9 %collective-permute-done.34.refs_2_ = bf16[32,2048]{1,0:T(8,128)(2,1)S(1)} collective-permute-done((bf16[32,2048]{1,0:T(8,128)(2,1)S(1)}, bf16[32,2048]{1,0:T(8,128)(2,1)S(1)}, u32[]{:S(2)}, u32[]{:S(2)}) %collective-permute-start.34) | collective-permute-done | bytes 131104 | tf_op jit(solution)/shard_map/ppermute | solution.py:167
  65.1 2.6 %collective-permute-start.35 = (bf16[32,2048]{1,0:T(8,128)(2,1)S(1)}, bf16[32,2048]{1,0:T(8,128)(2,1)S(1)}, u32[]{:S(2)}, u32[]{:S(2)}) collective-permute-start(bf16[32,2048]{1,0:T(8,128)(2,1)S(1)} %shard_map.122), channel_id=1, source_target_pairs={{0,2},{1,3},{2,0},{3,1},{4,6},{5,7},{6,4},{7,5},{8,10},{9,11},{10,... | collective-permute-start | bytes 393224 | tf_op jit(solution)/shard_map/ppermute | solution.py:167
  68.6 1.5 %collective-permute-start.39 = (bf16[32,2048]{1,0:T(8,128)(2,1)S(1)}, bf16[32,2048]{1,0:T(8,128)(2,1)S(1)}, u32[]{:S(2)}, u32[]{:S(2)}) collective-permute-start(bf16[32,2048]{1,0:T(8,128)(2,1)S(1)} %shard_map.124), channel_id=1, source_target_pairs={{0,3},{1,2},{2,1},{3,0},{4,7},{5,6},{6,5},{7,4},{8,11},{9,10},{10,... | collective-permute-start | bytes 393224 | tf_op jit(solution)/shard_map/ppermute | solution.py:167
  70.0 6.0 %collective-permute-done.35.refs_2_ = bf16[32,2048]{1,0:T(8,128)(2,1)S(1)} collective-permute-done((bf16[32,2048]{1,0:T(8,128)(2,1)S(1)}, bf16[32,2048]{1,0:T(8,128)(2,1)S(1)}, u32[]{:S(2)}, u32[]{:S(2)}) %collective-permute-start.35) | collective-permute-done | bytes 131104 | tf_op jit(solution)/shard_map/ppermute | solution.py:167
  (81 shorter events, 15.5 us)
Async XLA Ops:
  0.6 7.5 %collective-permute-start = (bf16[128,128]{1,0:T(8,128)(2,1)}, bf16[128,128]{1,0:T(8,128)(2,1)S(1)}, u32[]{:S(2)}, u32[]{:S(2)}) collective-permute-start(bf16[128,128]{1,0:T(8,128)(2,1)} %refs_1_.1), channel_id=1, source_target_pairs={{0,8},{4,12},{8,0},{12,4},{1,9},{5,13},{9,1},{13,5},{2,10},{6,14},... | collective-permute-start | bytes 98312 | tf_op jit(solution)/shard_map/ppermute | solution.py:167
  3.7 5.0 %collective-permute-start.2 = (bf16[128,128]{1,0:T(8,128)(2,1)}, bf16[128,128]{1,0:T(8,128)(2,1)S(1)}, u32[]{:S(2)}, u32[]{:S(2)}) collective-permute-start(bf16[128,128]{1,0:T(8,128)(2,1)} %refs_1_.1), channel_id=1, source_target_pairs={{0,4},{4,0},{8,12},{12,8},{1,5},{5,1},{9,13},{13,9},{2,6},{6,2},{1... | collective-permute-start | bytes 98312 | tf_op jit(solution)/shard_map/ppermute | solution.py:167
  3.7 5.0 %collective-permute-start.4 = (bf16[128,128]{1,0:T(8,128)(2,1)}, bf16[128,128]{1,0:T(8,128)(2,1)S(1)}, u32[]{:S(2)}, u32[]{:S(2)}) collective-permute-start(bf16[128,128]{1,0:T(8,128)(2,1)} %refs_2_.1), channel_id=1, source_target_pairs={{0,4},{4,0},{8,12},{12,8},{1,5},{5,1},{9,13},{13,9},{2,6},{6,2},{1... | collective-permute-start | bytes 98312 | tf_op jit(solution)/shard_map/ppermute | solution.py:167
  13.6 13.1 %collective-permute-start.9 = (bf16[32,2048]{1,0:T(8,128)(2,1)S(1)}, bf16[32,2048]{1,0:T(8,128)(2,1)S(1)}, u32[]{:S(2)}, u32[]{:S(2)}) collective-permute-start(bf16[32,2048]{1,0:T(8,128)(2,1)S(1)} %get-tuple-element.80), channel_id=1, source_target_pairs={{0,2},{1,3},{2,0},{3,1},{4,6},{5,7},{6,4},{7,5},{8,10},{9,11},{10,... | collective-permute-start | bytes 393224 | tf_op jit(solution)/shard_map/ppermute | solution.py:167
  16.6 10.0 %collective-permute-start.10 = (bf16[32,2048]{1,0:T(8,128)(2,1)S(1)}, bf16[32,2048]{1,0:T(8,128)(2,1)S(1)}, u32[]{:S(2)}, u32[]{:S(2)}) collective-permute-start(bf16[32,2048]{1,0:T(8,128)(2,1)S(1)} %get-tuple-element.81), channel_id=1, source_target_pairs={{0,3},{1,2},{2,1},{3,0},{4,7},{5,6},{6,5},{7,4},{8,11},{9,10},{10,... | collective-permute-start | bytes 393224 | tf_op jit(solution)/shard_map/ppermute | solution.py:167
  17.9 9.7 %collective-permute-start.11 = (bf16[32,2048]{1,0:T(8,128)(2,1)S(1)}, bf16[32,2048]{1,0:T(8,128)(2,1)S(1)}, u32[]{:S(2)}, u32[]{:S(2)}) collective-permute-start(bf16[32,2048]{1,0:T(8,128)(2,1)S(1)} %get-tuple-element.82), channel_id=1, source_target_pairs={{0,1},{1,0},{2,3},{3,2},{4,5},{5,4},{6,7},{7,6},{8,9},{9,8},{10,11... | collective-permute-start | bytes 393224 | tf_op jit(solution)/shard_map/ppermute | solution.py:167
  27.8 8.8 %collective-permute-start.13 = (bf16[32,2048]{1,0:T(8,128)(2,1)S(1)}, bf16[32,2048]{1,0:T(8,128)(2,1)S(1)}, u32[]{:S(2)}, u32[]{:S(2)}) collective-permute-start(bf16[32,2048]{1,0:T(8,128)(2,1)S(1)} %get-tuple-element.89.refs_0_), channel_id=1, source_target_pairs={{0,1},{1,0},{2,3},{3,2},{4,5},{5,4},{6,7},{7,6},{8,9},{9,8},{10,11... | collective-permute-start | bytes 393224 | tf_op jit(solution)/shard_map/ppermute | solution.py:167
  30.1 8.0 %collective-permute-start.15 = (bf16[32,2048]{1,0:T(8,128)(2,1)S(1)}, bf16[32,2048]{1,0:T(8,128)(2,1)S(1)}, u32[]{:S(2)}, u32[]{:S(2)}) collective-permute-start(bf16[32,2048]{1,0:T(8,128)(2,1)S(1)} %get-tuple-element.89.refs_0_), channel_id=1, source_target_pairs={{0,2},{1,3},{2,0},{3,1},{4,6},{5,7},{6,4},{7,5},{8,10},{9,11},{10,... | collective-permute-start | bytes 393224 | tf_op jit(solution)/shard_map/ppermute | solution.py:167
  32.1 9.7 %collective-permute-start.12 = (bf16[32,2048]{1,0:T(8,128)(2,1)S(1)}, bf16[32,2048]{1,0:T(8,128)(2,1)S(1)}, u32[]{:S(2)}, u32[]{:S(2)}) collective-permute-start(bf16[32,2048]{1,0:T(8,128)(2,1)S(1)} %get-tuple-element.89.refs_0_), channel_id=1, source_target_pairs={{0,8},{4,12},{8,0},{12,4},{1,9},{5,13},{9,1},{13,5},{2,10},{6,14},... | collective-permute-start | bytes 393224 | tf_op jit(solution)/shard_map/ppermute | solution.py:167
  36.6 5.2 %collective-permute-start.14 = (bf16[32,2048]{1,0:T(8,128)(2,1)S(1)}, bf16[32,2048]{1,0:T(8,128)(2,1)S(1)}, u32[]{:S(2)}, u32[]{:S(2)}) collective-permute-start(bf16[32,2048]{1,0:T(8,128)(2,1)S(1)} %collective-permute-done.13.refs_4_), channel_id=1, source_target_pairs={{0,8},{4,12},{8,0},{12,4},{1,9},{5,13},{9,1},{13,5},{2,10},{6,14},... | collective-permute-start | bytes 393224 | tf_op jit(solution)/shard_map/ppermute | solution.py:167
  38.1 5.0 %collective-permute-start.21 = (bf16[32,2048]{1,0:T(8,128)(2,1)S(1)}, bf16[32,2048]{1,0:T(8,128)(2,1)S(1)}, u32[]{:S(2)}, u32[]{:S(2)}) collective-permute-start(bf16[32,2048]{1,0:T(8,128)(2,1)S(1)} %collective-permute-done.15.refs_0_), channel_id=1, source_target_pairs={{0,8},{4,12},{8,0},{12,4},{1,9},{5,13},{9,1},{13,5},{2,10},{6,14},... | collective-permute-start | bytes 393224 | tf_op jit(solution)/shard_map/ppermute | solution.py:167
  38.6 6.1 %collective-permute-start.20 = (bf16[32,2048]{1,0:T(8,128)(2,1)S(1)}, bf16[32,2048]{1,0:T(8,128)(2,1)S(1)}, u32[]{:S(2)}, u32[]{:S(2)}) collective-permute-start(bf16[32,2048]{1,0:T(8,128)(2,1)S(1)} %collective-permute-done.15.refs_0_), channel_id=1, source_target_pairs={{0,1},{1,0},{2,3},{3,2},{4,5},{5,4},{6,7},{7,6},{8,9},{9,8},{10,11... | collective-permute-start | bytes 393224 | tf_op jit(solution)/shard_map/ppermute | solution.py:167
  44.7 5.0 %collective-permute-start.26 = (bf16[32,2048]{1,0:T(8,128)(2,1)S(1)}, bf16[32,2048]{1,0:T(8,128)(2,1)S(1)}, u32[]{:S(2)}, u32[]{:S(2)}) collective-permute-start(bf16[32,2048]{1,0:T(8,128)(2,1)S(1)} %collective-permute-done.20.refs_4_), channel_id=1, source_target_pairs={{0,8},{4,12},{8,0},{12,4},{1,9},{5,13},{9,1},{13,5},{2,10},{6,14},... | collective-permute-start | bytes 393224 | tf_op jit(solution)/shard_map/ppermute | solution.py:167
  51.3 5.6 %collective-permute-start.24 = (bf16[32,2048]{1,0:T(8,128)(2,1)S(1)}, bf16[32,2048]{1,0:T(8,128)(2,1)S(1)}, u32[]{:S(2)}, u32[]{:S(2)}) collective-permute-start(bf16[32,2048]{1,0:T(8,128)(2,1)S(1)} %shard_map.117), channel_id=1, source_target_pairs={{0,8},{4,12},{8,0},{12,4},{1,9},{5,13},{9,1},{13,5},{2,10},{6,14},... | collective-permute-start | bytes 393224 | tf_op jit(solution)/shard_map/ppermute | solution.py:167
  54.0 5.1 %collective-permute-start.33 = (bf16[32,2048]{1,0:T(8,128)(2,1)S(1)}, bf16[32,2048]{1,0:T(8,128)(2,1)S(1)}, u32[]{:S(2)}, u32[]{:S(2)}) collective-permute-start(bf16[32,2048]{1,0:T(8,128)(2,1)S(1)} %get-tuple-element.120), channel_id=1, source_target_pairs={{0,4},{4,0},{8,12},{12,8},{1,5},{5,1},{9,13},{13,9},{2,6},{6,2},{1... | collective-permute-start | bytes 393224 | tf_op jit(solution)/shard_map/ppermute | solution.py:167
  54.2 6.5 %collective-permute-start.37 = (bf16[32,2048]{1,0:T(8,128)(2,1)S(1)}, bf16[32,2048]{1,0:T(8,128)(2,1)S(1)}, u32[]{:S(2)}, u32[]{:S(2)}) collective-permute-start(bf16[32,2048]{1,0:T(8,128)(2,1)S(1)} %get-tuple-element.125), channel_id=1, source_target_pairs={{0,4},{4,0},{8,12},{12,8},{1,5},{5,1},{9,13},{13,9},{2,6},{6,2},{1... | collective-permute-start | bytes 393224 | tf_op jit(solution)/shard_map/ppermute | solution.py:167
  57.0 5.2 %collective-permute-start.25 = (bf16[32,2048]{1,0:T(8,128)(2,1)S(1)}, bf16[32,2048]{1,0:T(8,128)(2,1)S(1)}, u32[]{:S(2)}, u32[]{:S(2)}) collective-permute-start(bf16[32,2048]{1,0:T(8,128)(2,1)S(1)} %shard_map.118), channel_id=1, source_target_pairs={{0,1},{1,0},{2,3},{3,2},{4,5},{5,4},{6,7},{7,6},{8,9},{9,8},{10,11... | collective-permute-start | bytes 393224 | tf_op jit(solution)/shard_map/ppermute | solution.py:167
  59.1 5.9 %collective-permute-start.34 = (bf16[32,2048]{1,0:T(8,128)(2,1)S(1)}, bf16[32,2048]{1,0:T(8,128)(2,1)S(1)}, u32[]{:S(2)}, u32[]{:S(2)}) collective-permute-start(bf16[32,2048]{1,0:T(8,128)(2,1)S(1)} %shard_map.121), channel_id=1, source_target_pairs={{0,8},{4,12},{8,0},{12,4},{1,9},{5,13},{9,1},{13,5},{2,10},{6,14},... | collective-permute-start | bytes 393224 | tf_op jit(solution)/shard_map/ppermute | solution.py:167
  60.1 7.6 %collective-permute-start.40 = (bf16[32,2048]{1,0:T(8,128)(2,1)S(1)}, bf16[32,2048]{1,0:T(8,128)(2,1)S(1)}, u32[]{:S(2)}, u32[]{:S(2)}) collective-permute-start(bf16[32,2048]{1,0:T(8,128)(2,1)S(1)} %get-tuple-element.126), channel_id=1, source_target_pairs={{0,4},{4,0},{8,12},{12,8},{1,5},{5,1},{9,13},{13,9},{2,6},{6,2},{1... | collective-permute-start | bytes 393224 | tf_op jit(solution)/shard_map/ppermute | solution.py:167
  60.7 7.0 %collective-permute-start.38 = (bf16[32,2048]{1,0:T(8,128)(2,1)S(1)}, bf16[32,2048]{1,0:T(8,128)(2,1)S(1)}, u32[]{:S(2)}, u32[]{:S(2)}) collective-permute-start(bf16[32,2048]{1,0:T(8,128)(2,1)S(1)} %shard_map.123), channel_id=1, source_target_pairs={{0,8},{4,12},{8,0},{12,4},{1,9},{5,13},{9,1},{13,5},{2,10},{6,14},... | collective-permute-start | bytes 393224 | tf_op jit(solution)/shard_map/ppermute | solution.py:167
  62.2 6.4 %collective-permute-start.36 = (bf16[32,2048]{1,0:T(8,128)(2,1)S(1)}, bf16[32,2048]{1,0:T(8,128)(2,1)S(1)}, u32[]{:S(2)}, u32[]{:S(2)}) collective-permute-start(bf16[32,2048]{1,0:T(8,128)(2,1)S(1)} %get-tuple-element.123), channel_id=1, source_target_pairs={{0,4},{4,0},{8,12},{12,8},{1,5},{5,1},{9,13},{13,9},{2,6},{6,2},{1... | collective-permute-start | bytes 393224 | tf_op jit(solution)/shard_map/ppermute | solution.py:167
  65.1 11.0 %collective-permute-start.35 = (bf16[32,2048]{1,0:T(8,128)(2,1)S(1)}, bf16[32,2048]{1,0:T(8,128)(2,1)S(1)}, u32[]{:S(2)}, u32[]{:S(2)}) collective-permute-start(bf16[32,2048]{1,0:T(8,128)(2,1)S(1)} %shard_map.122), channel_id=1, source_target_pairs={{0,2},{1,3},{2,0},{3,1},{4,6},{5,7},{6,4},{7,5},{8,10},{9,11},{10,... | collective-permute-start | bytes 393224 | tf_op jit(solution)/shard_map/ppermute | solution.py:167
  67.7 8.3 %collective-permute-start.41 = (bf16[32,2048]{1,0:T(8,128)(2,1)S(1)}, bf16[32,2048]{1,0:T(8,128)(2,1)S(1)}, u32[]{:S(2)}, u32[]{:S(2)}) collective-permute-start(bf16[32,2048]{1,0:T(8,128)(2,1)S(1)} %shard_map.119), channel_id=1, source_target_pairs={{0,8},{4,12},{8,0},{12,4},{1,9},{5,13},{9,1},{13,5},{2,10},{6,14},... | collective-permute-start | bytes 393224 | tf_op jit(solution)/shard_map/ppermute | solution.py:167
  68.6 7.5 %collective-permute-start.39 = (bf16[32,2048]{1,0:T(8,128)(2,1)S(1)}, bf16[32,2048]{1,0:T(8,128)(2,1)S(1)}, u32[]{:S(2)}, u32[]{:S(2)}) collective-permute-start(bf16[32,2048]{1,0:T(8,128)(2,1)S(1)} %shard_map.124), channel_id=1, source_target_pairs={{0,3},{1,2},{2,1},{3,0},{4,7},{5,6},{6,5},{7,4},{8,11},{9,10},{10,... | collective-permute-start | bytes 393224 | tf_op jit(solution)/shard_map/ppermute | solution.py:167
  (22 other events, 119.6 us)

commit v4 on v3

--- a/solution.py
+++ b/solution.py
@@ -179,28 +179,19 @@
         out_specs=[VMEM_SPEC] * len(outs),
         scratch_shapes=scratch,
         compiler_params=pltpu.CompilerParams(vmem_limit_bytes=limit),
-        cost_estimate=pl.CostEstimate(flops=1024, bytes_accessed=1024, transcendentals=0),
+        cost_estimate=pl.CostEstimate(flops=max(flops, 1024), bytes_accessed=1024, transcendentals=0),
     )(*operands)
 
 
 def own_block_kernel(tp_count, *refs):
-    *sources, w_source = refs[:6]
-    w_ref, q_ref, max_ref, total_ref, acc_ref, *mix_refs = refs[6:-6]
-    k_ref, v_ref, ids_ref, weights_ref, arrived, w_arrived = refs[-6:]
+    sources, (q_ref, max_ref, total_ref, acc_ref, *mix_refs) = refs[:5], refs[5:-5]
+    k_ref, v_ref, ids_ref, weights_ref, arrived = refs[-5:]
     targets = (q_ref, k_ref, v_ref, ids_ref, weights_ref)
     copies = [
         pltpu.make_async_copy(source, target, arrived.at[i])
         for i, (source, target) in enumerate(zip(sources, targets))
     ]
-    chunks = w_arrived.shape[0]
-    depth = w_ref.shape[0] // chunks
-    w_copies = [
-        pltpu.make_async_copy(
-            w_source.at[pl.ds(i * depth, depth)], w_ref.at[pl.ds(i * depth, depth)], w_arrived.at[i]
-        )
-        for i in range(chunks)
-    ]
-    for copy in copies + w_copies:
+    for copy in copies:
         copy.start()
     for copy in copies:
         copy.wait()
@@ -208,28 +199,26 @@
     block_rows = q_ref.shape[0]
     kv_local = k_ref.shape[1] // HEAD
     group_size = q_ref.shape[1] // k_ref.shape[1]
-    row = lax.broadcasted_iota(jnp.int32, (block_rows, block_rows), 0)
-    col = lax.broadcasted_iota(jnp.int32, (block_rows, block_rows), 1)
+    key_pos = lax.broadcasted_iota(jnp.int32, (block_rows, block_rows), 0)
+    query_pos = lax.broadcasted_iota(jnp.int32, (block_rows, block_rows), 1)
     for g in range(kv_local):
         key_rows = k_ref[:, g * HEAD : (g + 1) * HEAD]
-        value_rows = v_ref[:, g * HEAD : (g + 1) * HEAD]
+        value_cols = v_ref[:, g * HEAD : (g + 1) * HEAD].astype(F32).T.astype(BF16)
         for h in range(g * group_size, (g + 1) * group_size):
             lanes = slice(h * HEAD, (h + 1) * HEAD)
             scores = lax.dot_general(
-                q_ref[:, lanes], key_rows, (((1,), (1,)), ((), ())), preferred_element_type=F32
+                key_rows, q_ref[:, lanes], (((1,), (1,)), ((), ())), preferred_element_type=F32
             )
-            scores = jnp.where(col <= row, scores * HEAD ** (-0.5), HIDDEN_SCORE)
-            top = jnp.max(scores, axis=1, keepdims=True)
+            scores = jnp.where(key_pos <= query_pos, scores * HEAD ** (-0.5), HIDDEN_SCORE)
+            top = jnp.max(scores, axis=0, keepdims=True)
             weights = jnp.exp(scores - top)
-            max_ref[:, h : h + 1] = top
-            total_ref[:, h : h + 1] = jnp.sum(weights, axis=1, keepdims=True)
-            acc_ref[:, lanes] = jnp.dot(weights.astype(BF16), value_rows, preferred_element_type=F32)
+            max_ref[h : h + 1, :] = top
+            total_ref[h : h + 1, :] = jnp.sum(weights, axis=0, keepdims=True)
+            acc_ref[h] = jnp.dot(value_cols, weights.astype(BF16), preferred_element_type=F32)
     share = weights_ref[...] / jnp.sum(weights_ref[...], axis=0, keepdims=True)
     for d, mix_ref in enumerate(mix_refs):
         expert = (ctx_index ^ d) * tp_count + tp_index
         mix_ref[...] = jnp.sum(jnp.where(ids_ref[...] == expert, share, 0.0), axis=0, keepdims=True)
-    for copy in w_copies:
-        copy.wait()
 
 
 def other_blocks_kernel(tp_count, others, *refs):
@@ -241,32 +230,35 @@
     block_rows = q_ref.shape[0]
     kv_local = k_refs[0].shape[1] // HEAD
     group_size = q_ref.shape[1] // k_refs[0].shape[1]
-    bias = jnp.concatenate(
-        [
-            jnp.full((1, block_rows), jnp.where((ctx_index ^ d) < ctx_index, 0.0, HIDDEN_SCORE))
-            for d in range(1, others + 1)
-        ],
-        axis=1,
-    )
+    hide = [
+        jnp.where((ctx_index ^ d) < ctx_index, 0.0, HIDDEN_SCORE) for d in range(1, others + 1)
+    ]
     for g in range(kv_local):
         kv_lanes = slice(g * HEAD, (g + 1) * HEAD)
         key_rows = jnp.concatenate([r[:, kv_lanes] for r in k_refs], axis=0)
         value_rows = jnp.concatenate([r[:, kv_lanes] for r in v_refs], axis=0)
+        value_cols = value_rows.astype(F32).T.astype(BF16)
         for h in range(g * group_size, (g + 1) * group_size):
             lanes = slice(h * HEAD, (h + 1) * HEAD)
             scores = lax.dot_general(
-                q_ref[:, lanes], key_rows, (((1,), (1,)), ((), ())), preferred_element_type=F32
+                key_rows, q_ref[:, lanes], (((1,), (1,)), ((), ())), preferred_element_type=F32
             )
-            scores = scores * HEAD ** (-0.5) + bias
-            old = max_ref[:, h : h + 1]
-            top = jnp.maximum(old, jnp.max(scores, axis=1, keepdims=True))
+            scores = jnp.concatenate(
+                [
+                    scores[i * block_rows : (i + 1) * block_rows] * HEAD ** (-0.5) + hide[i]
+                    for i in range(others)
+                ],
+                axis=0,
+            )
+            old = max_ref[h : h + 1, :]
+            top = jnp.maximum(old, jnp.max(scores, axis=0, keepdims=True))
             weights = jnp.exp(scores - top)
             rescale = jnp.exp(old - top)
-            total = total_ref[:, h : h + 1] * rescale + jnp.sum(weights, axis=1, keepdims=True)
-            accum = acc_ref[:, lanes] * rescale + jnp.dot(
-                weights.astype(BF16), value_rows, preferred_element_type=F32
+            total = total_ref[h : h + 1, :] * rescale + jnp.sum(weights, axis=0, keepdims=True)
+            accum = acc_ref[h] * rescale + jnp.dot(
+                value_cols, weights.astype(BF16), preferred_element_type=F32
             )
-            att_ref[:, lanes] = (accum * (1.0 / total)).astype(BF16)
+            att_ref[:, lanes] = (accum * (1.0 / total)).T.astype(BF16)
     piece_rows = block_rows // tp_count
     scratch[...] = jnp.dot(att_ref[...], w_ref[...], preferred_element_type=F32)
     for d in range(tp_count):
@@ -332,24 +324,22 @@
 
     far_k, far_v = swap(keys, "ctx", 2), swap(values, "ctx", 2)
     near_k, near_v = swap(keys, "ctx", 1), swap(values, "ctx", 1)
-    projection, queries, top, total, accum, *mixes = call(
+    queries, top, total, accum, *mixes = call(
         functools.partial(own_block_kernel, tp_count),
-        [shape(out_weight.shape, BF16), shape((block_rows, width), BF16)]
-        + [shape((block_rows, heads), F32)] * 2
-        + [shape((block_rows, width), F32)]
+        [shape((block_rows, width), BF16)]
+        + [shape((heads, block_rows), F32)] * 2
+        + [shape((heads, HEAD, block_rows), F32)]
         + [shape((1, block_rows), F32)] * ctx_count,
-        (queries, keys, values, expert_ids.T, route_weights.T, out_weight),
+        (queries, keys, values, expert_ids.T, route_weights.T),
         scratch=[
             pltpu.VMEM(keys.shape, BF16),
             pltpu.VMEM(values.shape, BF16),
             pltpu.VMEM(expert_ids.T.shape, jnp.int32),
             pltpu.VMEM(route_weights.T.shape, F32),
             pltpu.SemaphoreType.DMA((5,)),
-            pltpu.SemaphoreType.DMA((4,)),
         ],
-        flops=4 * block_rows * block_rows * width,
-        moved=queries.size * 6,
-        from_hbm=6,
+        flops=5 * 10**9,
+        from_hbm=5,
     )
     far_k, far_v, top = lax.optimization_barrier((far_k, far_v, top))
     ks = [near_k, far_k, swap(far_k, "ctx", 1)]
@@ -359,10 +349,8 @@
     attended, *partials = call(
         functools.partial(other_blocks_kernel, tp_count, ctx_count - 1),
         [shape((block_rows, width), BF16), piece32] + [piece] * (tp_count - 1),
-        (projection, queries, top, total, accum, *ks, *vs),
+        (out_weight, queries, top, total, accum, *ks, *vs),
         scratch=[pltpu.VMEM((block_rows, features), F32)],
-        flops=2 * block_rows * width * features + 4 * block_rows * block_rows * ctx_count * width,
-        moved=out_weight.size * 2,
     )
 
     arrived = [swap(partials[d], "tp", d) for d in (2, 3, 1)]
@@ -379,7 +367,6 @@
             expert_up,
             expert_down,
         ),
-        flops=8 * piece_rows * features,
     )
 
     def after(values, *earlier):
@@ -390,9 +377,7 @@
             functools.partial(expert_kernel, group),
             [piece32, piece, piece32, piece] * len(group),
             (*tokens, columns, expert_gate, expert_up, expert_down),
-            flops=6 * ctx_count * piece_rows * features * expert_gate.shape[2],
-            moved=3 * expert_gate.size * 2,
-        )
+                )
         return [found[4 * i : 4 * i + 4] for i in range(len(group))]
 
     def spread(rows, far):
@@ -418,25 +403,36 @@
     far2 = swap(rows2, "ctx", 2)
     rows3 = swap(rows2, "tp", 1)
     rows0, far0, rows1, far1 = after((normed, far0, rows1, far1), rows2)
-    tokens = spread(rows0, far0) + spread(rows1, far1)
+    tokens = spread(rows1, far1) + spread(rows2, far2)
     far3 = swap(rows3, "ctx", 2)
-    tokens = after(tokens, rows3, far2)
-    out0, out1 = work((0, 1), tokens)
-    parts1, parts0 = gather_results(out1), gather_results(out0)
-    rows2, far2, rows3, far3 = after((rows2, far2, rows3, far3), out0[0])
-    tokens = spread(rows2, far2) + spread(rows3, far3)
-    tokens = after(tokens, parts1[2], parts0[2])
+    tokens = after(tokens, rows3)
+    out1, out2 = work((1, 2), tokens)
+    parts2 = gather_results(out2)
+    rows0, far0, rows3, far3 = after((rows0, far0, rows3, far3), out1[0])
+    tokens = spread(rows0, far0) + spread(rows3, far3)
+    tokens = after(tokens, parts2[2])
+    back2 = swap(parts2[2], "ctx", 2)
+    out0, out3 = work((0, 3), tokens)
+    (back2,) = after((back2,), out3[2])
+    (tp2,) = call(sum_kernel, [piece], (*parts2[:2], back2), flops=10**9)
+    ret2 = swap(tp2, "tp", 2)
+    out3 = [out3[0], out3[1], *after((out3[2],), tp2), out3[3]]
+    parts3 = gather_results(out3)
+    back3 = swap(parts3[2], "ctx", 2)
+    out1 = [out1[0], out1[1], *after((out1[2],), parts3[2]), out1[3]]
+    parts1 = gather_results(out1)
     back1 = swap(parts1[2], "ctx", 2)
-    out2, out3 = work((2, 3), tokens)
+    (back3,) = after((back3,), parts1[2])
+    (tp3,) = call(sum_kernel, [piece], (*parts3[:2], back3))
+    ret3 = swap(tp3, "tp", 3)
+    (back1,) = after((back1,), tp3, ret2)
     (tp1,) = call(sum_kernel, [piece], (*parts1[:2], back1))
     ret1 = swap(tp1, "tp", 1)
-    parts2, parts3 = gather_results(out2), gather_results(out3)
-    back2, back3 = swap(parts2[2], "ctx", 2), swap(parts3[2], "ctx", 2)
-    (tp2,) = call(sum_kernel, [piece], (*parts2[:2], *after((back2,), ret1)))
-    (tp3,) = call(sum_kernel, [piece], (*parts3[:2], back3))
-    results = [own_proj, ret1, swap(tp2, "tp", 2), swap(tp3, "tp", 3)]
-    parts0 = after(parts0, back3)
-    results += send_back(parts0, 0)
+    results = [own_proj, ret1, ret2, ret3]
+    out0 = [out0[0], out0[1], *after((out0[2],), parts1[2]), out0[3]]
+    parts0 = gather_results(out0)
+    (far_part0,) = after((parts0[2],), back1)
+    results += send_back([*parts0[:2], far_part0], 0)
     (layer_out,) = call(sum_kernel, [piece], results)
     return (attended, layer_out)
 

time: 77 us -> 70.7 us (0.918)
  Pallas kernels: 12.8 us -> 9.64 us
  waiting for transfers between devices: 27.6 us -> 24.7 us
    pallas_call x13, Pallas kernels: 12.8 us -> 9.64 us  [call(): pl.pallas_call(kernel, out_shape=outs, in_specs=[HBM_SPEC] * from_hbm + [...]
    ppermute x42, waiting for transfers between devices: 27.6 us -> 24.7 us  [swap(): return lax.ppermute(rows, axis, [(i, i ^ offset) for i in range(count)])]
  transfers between devices with their start and end apart: 42 -> 42, of which waited for: 15 -> 17; matrix products, arithmetic and copies ran while one was open for 0% -> 0% of each run, Pallas kernels for 10% -> 10%
where the time goes in v4:
time: 70.7 us; the launch traced here: 70.6 us
  starting transfers between devices  35.4 us (50%)
  waiting for transfers between devices  24.7 us (35%)
  Pallas kernels  9.64 us (14%)
  between operations  0.81 us (1%)
    ppermute x42, starting transfers between devices, swap(): return lax.ppermute(rows, axis, [(i, i ^ offset) for i in range(count)])  35.4 us
    ppermute x42, waiting for transfers between devices, swap(): return lax.ppermute(rows, axis, [(i, i ^ offset) for i in range(count)])  24.7 us
    pallas_call x13, Pallas kernels, call(): pl.pallas_call(kernel, out_shape=outs, in_specs=[HBM_SPEC] * from_hbm + [...  9.64 us
  transfers between devices with their start and end apart: 42, of which 17 were waited for; matrix products, arithmetic and copies ran while one was open for 0% of the time, Pallas kernels for 10%

profile of v4, /device:TPU:0, one launch (start us, length us, event | category | flops | bytes accessed | tf_op | source)
XLA Modules:
  0.0 70.6 jit_solution(13479913573893494619)
XLA Ops:
  1.1 2.6 %collective-permute-start = (bf16[128,128]{1,0:T(8,128)(2,1)}, bf16[128,128]{1,0:T(8,128)(2,1)S(1)}, u32[]{:S(2)}, u32[]{:S(2)}) collective-permute-start(bf16[128,128]{1,0:T(8,128)(2,1)} %refs_1_.1), channel_id=1, source_target_pairs={{0,8},{4,12},{8,0},{12,4},{1,9},{5,13},{9,1},{13,5},{2,10},{6,14},... | collective-permute-start | bytes 98312 | tf_op jit(solution)/shard_map/ppermute | solution.py:167
  4.2 2.9 %shard_map.113 = (bf16[128,1024]{1,0:T(8,128)(2,1)S(1)}, f32[8,128]{1,0:T(8,128)S(1)}, f32[8,128]{1,0:T(8,128)S(1)}, f32[8,128,128]{2,1,0:T(8,128)S(1)}, f32[1,1...) custom-call(bf16[128,1024]{1,0:T(8,128)(2,1)} %refs_0_.2, ...), custom_call_target="tpu_custom_call" | custom-call | flops 5000000000 | bytes 1024 | tf_op jit(solution)/shard_map/pallas_call | solution.py:175
  9.4 1.8 %shard_map.114 = (bf16[128,1024]{1,0:T(8,128)(2,1)}, f32[32,2048]{1,0:T(8,128)S(1)}, bf16[32,2048]{1,0:T(8,128)(2,1)S(1)}, bf16[32,2048]{1,0:T(8,128)(2,1)S(1)}, bf16[32,2048]{1,0:T(8,128)(2,1)S(1)}) custom-call(bf16[1024,2048]{1,0:T(8,128)(2,1)S(1)} %copy-done.3, bf16[128,1024]{1,0:T(8,128)(2,1)S(1)} %get-tuple-element.68.refs_1_, ...), custom_call_target="tpu_custom_call" | custom-call | flops 1024 | bytes 1024 | tf_op jit(solution)/shard_map/pallas_call | solution.py:175
  11.2 2.6 %collective-permute-start.9 = (bf16[32,2048]{1,0:T(8,128)(2,1)S(1)}, bf16[32,2048]{1,0:T(8,128)(2,1)S(1)}, u32[]{:S(2)}, u32[]{:S(2)}) collective-permute-start(bf16[32,2048]{1,0:T(8,128)(2,1)S(1)} %get-tuple-element.81), channel_id=1, source_target_pairs={{0,2},{1,3},{2,0},{3,1},{4,6},{5,7},{6,4},{7,5},{8,10},{9,11},{10,... | collective-permute-start | bytes 393224 | tf_op jit(solution)/shard_map/ppermute | solution.py:167
  13.8 1.4 %collective-permute-start.10 = (bf16[32,2048]{1,0:T(8,128)(2,1)S(1)}, bf16[32,2048]{1,0:T(8,128)(2,1)S(1)}, u32[]{:S(2)}, u32[]{:S(2)}) collective-permute-start(bf16[32,2048]{1,0:T(8,128)(2,1)S(1)} %get-tuple-element.82), channel_id=1, source_target_pairs={{0,3},{1,2},{2,1},{3,0},{4,7},{5,6},{6,5},{7,4},{8,11},{9,10},{10,... | collective-permute-start | bytes 393224 | tf_op jit(solution)/shard_map/ppermute | solution.py:167
  17.2 1.7 %collective-permute-done.7.refs_2_ = f32[1,128]{1,0:T(1,128)S(1)} collective-permute-done((f32[1,128]{1,0:T(1,128)S(1)}, f32[1,128]{1,0:T(1,128)S(1)}, u32[]{:S(2)}, u32[]{:S(2)}) %collective-permute-start.7) | collective-permute-done | bytes 544 | tf_op jit(solution)/shard_map/ppermute | solution.py:167
  19.4 4.6 %collective-permute-done.9.refs_5_ = bf16[32,2048]{1,0:T(8,128)(2,1)S(1)} collective-permute-done((bf16[32,2048]{1,0:T(8,128)(2,1)S(1)}, bf16[32,2048]{1,0:T(8,128)(2,1)S(1)}, u32[]{:S(2)}, u32[]{:S(2)}) %collective-permute-start.9) | collective-permute-done | bytes 131104 | tf_op jit(solution)/shard_map/ppermute | solution.py:167
  25.0 2.2 %collective-permute-start.13 = (bf16[32,2048]{1,0:T(8,128)(2,1)S(1)}, bf16[32,2048]{1,0:T(8,128)(2,1)S(1)}, u32[]{:S(2)}, u32[]{:S(2)}) collective-permute-start(bf16[32,2048]{1,0:T(8,128)(2,1)S(1)} %get-tuple-element.108.refs_0_), channel_id=1, source_target_pairs={{0,1},{1,0},{2,3},{3,2},{4,5},{5,4},{6,7},{7,6},{8,9},{9,8},{10,11... | collective-permute-start | bytes 393224 | tf_op jit(solution)/shard_map/ppermute | solution.py:167
  27.3 2.0 %collective-permute-start.15 = (bf16[32,2048]{1,0:T(8,128)(2,1)S(1)}, bf16[32,2048]{1,0:T(8,128)(2,1)S(1)}, u32[]{:S(2)}, u32[]{:S(2)}) collective-permute-start(bf16[32,2048]{1,0:T(8,128)(2,1)S(1)} %get-tuple-element.108.refs_0_), channel_id=1, source_target_pairs={{0,2},{1,3},{2,0},{3,1},{4,6},{5,7},{6,4},{7,5},{8,10},{9,11},{10,... | collective-permute-start | bytes 393224 | tf_op jit(solution)/shard_map/ppermute | solution.py:167
  30.2 3.6 %collective-permute-done.13.refs_0_ = bf16[32,2048]{1,0:T(8,128)(2,1)S(1)} collective-permute-done((bf16[32,2048]{1,0:T(8,128)(2,1)S(1)}, bf16[32,2048]{1,0:T(8,128)(2,1)S(1)}, u32[]{:S(2)}, u32[]{:S(2)}) %collective-permute-start.13) | collective-permute-done | bytes 131104 | tf_op jit(solution)/shard_map/ppermute | solution.py:167
  34.7 1.1 %collective-permute-start.19 = (bf16[32,2048]{1,0:T(8,128)(2,1)S(1)}, bf16[32,2048]{1,0:T(8,128)(2,1)S(1)}, u32[]{:S(2)}, u32[]{:S(2)}) collective-permute-start(bf16[32,2048]{1,0:T(8,128)(2,1)S(1)} %collective-permute-done.15.refs_4_), channel_id=1, source_target_pairs={{0,8},{4,12},{8,0},{12,4},{1,9},{5,13},{9,1},{13,5},{2,10},{6,14},... | collective-permute-start | bytes 393224 | tf_op jit(solution)/shard_map/ppermute | solution.py:167
  35.8 2.5 %collective-permute-start.21 = (bf16[32,2048]{1,0:T(8,128)(2,1)S(1)}, bf16[32,2048]{1,0:T(8,128)(2,1)S(1)}, u32[]{:S(2)}, u32[]{:S(2)}) collective-permute-start(bf16[32,2048]{1,0:T(8,128)(2,1)S(1)} %collective-permute-done.15.refs_4_), channel_id=1, source_target_pairs={{0,1},{1,0},{2,3},{3,2},{4,5},{5,4},{6,7},{7,6},{8,9},{9,8},{10,11... | collective-permute-start | bytes 393224 | tf_op jit(solution)/shard_map/ppermute | solution.py:167
  38.9 1.3 %collective-permute-done.19.refs_6_ = bf16[32,2048]{1,0:T(8,128)(2,1)S(1)} collective-permute-done((bf16[32,2048]{1,0:T(8,128)(2,1)S(1)}, bf16[32,2048]{1,0:T(8,128)(2,1)S(1)}, u32[]{:S(2)}, u32[]{:S(2)}) %collective-permute-start.19) | collective-permute-done | bytes 131104 | tf_op jit(solution)/shard_map/ppermute | solution.py:167
  41.3 1.1 %collective-permute-start.23 = (bf16[32,2048]{1,0:T(8,128)(2,1)S(1)}, bf16[32,2048]{1,0:T(8,128)(2,1)S(1)}, u32[]{:S(2)}, u32[]{:S(2)}) collective-permute-start(bf16[32,2048]{1,0:T(8,128)(2,1)S(1)} %collective-permute-done.21.refs_4_), channel_id=1, source_target_pairs={{0,8},{4,12},{8,0},{12,4},{1,9},{5,13},{9,1},{13,5},{2,10},{6,14},... | collective-permute-start | bytes 393224 | tf_op jit(solution)/shard_map/ppermute | solution.py:167
  42.4 1.9 %shard_map.116 = (f32[32,2048]{1,0:T(8,128)S(1)}, bf16[32,2048]{1,0:T(8,128)(2,1)S(1)}, f32[32,2048]{1,0:T(8,128)S(1)}, bf16[32,2048]{1,0:T(8,128)(2,1)S(1)}, f3...) custom-call(bf16[32,2048]{1,0:T(8,128)(2,1)S(1)} %collective-permute, ...), custom_call_target="tpu_custom_call" | custom-call | flops 1024 | bytes 1024 | tf_op jit(solution)/shard_map/pallas_call | solution.py:175
  44.4 1.8 %collective-permute-done.23.refs_6_ = bf16[32,2048]{1,0:T(8,128)(2,1)S(1)} collective-permute-done((bf16[32,2048]{1,0:T(8,128)(2,1)S(1)}, bf16[32,2048]{1,0:T(8,128)(2,1)S(1)}, u32[]{:S(2)}, u32[]{:S(2)}) %collective-permute-start.23) | collective-permute-done | bytes 131104 | tf_op jit(solution)/shard_map/ppermute | solution.py:167
  47.3 1.2 %collective-permute-start.30 = (bf16[32,2048]{1,0:T(8,128)(2,1)S(1)}, bf16[32,2048]{1,0:T(8,128)(2,1)S(1)}, u32[]{:S(2)}, u32[]{:S(2)}) collective-permute-start(bf16[32,2048]{1,0:T(8,128)(2,1)S(1)} %shard_map.117), channel_id=1, source_target_pairs={{0,8},{4,12},{8,0},{12,4},{1,9},{5,13},{9,1},{13,5},{2,10},{6,14},... | collective-permute-start | bytes 393224 | tf_op jit(solution)/shard_map/ppermute | solution.py:167
  48.5 1.9 %shard_map.118 = (f32[32,2048]{1,0:T(8,128)S(1)}, bf16[32,2048]{1,0:T(8,128)(2,1)S(1)}, f32[32,2048]{1,0:T(8,128)S(1)}, bf16[32,2048]{1,0:T(8,128)(2,1)S(1)}, f3...) custom-call(bf16[32,2048]{1,0:T(8,128)(2,1)S(1)} %get-tuple-element., ...), custom_call_target="tpu_custom_call" | custom-call | flops 1024 | bytes 1024 | tf_op jit(solution)/shard_map/pallas_call | solution.py:175
  51.5 1.3 %collective-permute-done.30.refs_2_ = bf16[32,2048]{1,0:T(8,128)(2,1)S(1)} collective-permute-done((bf16[32,2048]{1,0:T(8,128)(2,1)S(1)}, bf16[32,2048]{1,0:T(8,128)(2,1)S(1)}, u32[]{:S(2)}, u32[]{:S(2)}) %collective-permute-start.30) | collective-permute-done | bytes 131104 | tf_op jit(solution)/shard_map/ppermute | solution.py:167
  52.9 1.2 %collective-permute-start.35 = (bf16[32,2048]{1,0:T(8,128)(2,1)S(1)}, bf16[32,2048]{1,0:T(8,128)(2,1)S(1)}, u32[]{:S(2)}, u32[]{:S(2)}) collective-permute-start(bf16[32,2048]{1,0:T(8,128)(2,1)S(1)} %shard_map.120), channel_id=1, source_target_pairs={{0,8},{4,12},{8,0},{12,4},{1,9},{5,13},{9,1},{13,5},{2,10},{6,14},... | collective-permute-start | bytes 393224 | tf_op jit(solution)/shard_map/ppermute | solution.py:167
  54.1 2.5 %collective-permute-start.36 = (bf16[32,2048]{1,0:T(8,128)(2,1)S(1)}, bf16[32,2048]{1,0:T(8,128)(2,1)S(1)}, u32[]{:S(2)}, u32[]{:S(2)}) collective-permute-start(bf16[32,2048]{1,0:T(8,128)(2,1)S(1)} %shard_map.119), channel_id=1, source_target_pairs={{0,2},{1,3},{2,0},{3,1},{4,6},{5,7},{6,4},{7,5},{8,10},{9,11},{10,... | collective-permute-start | bytes 393224 | tf_op jit(solution)/shard_map/ppermute | solution.py:167
  58.3 4.4 %collective-permute-start.38 = (bf16[32,2048]{1,0:T(8,128)(2,1)S(1)}, bf16[32,2048]{1,0:T(8,128)(2,1)S(1)}, u32[]{:S(2)}, u32[]{:S(2)}) collective-permute-start(bf16[32,2048]{1,0:T(8,128)(2,1)S(1)} %shard_map.122), channel_id=1, source_target_pairs={{0,3},{1,2},{2,1},{3,0},{4,7},{5,6},{6,5},{7,4},{8,11},{9,10},{10,... | collective-permute-start | bytes 393224 | tf_op jit(solution)/shard_map/ppermute | solution.py:167
  62.7 1.4 %collective-permute-done.36.refs_2_ = bf16[32,2048]{1,0:T(8,128)(2,1)S(1)} collective-permute-done((bf16[32,2048]{1,0:T(8,128)(2,1)S(1)}, bf16[32,2048]{1,0:T(8,128)(2,1)S(1)}, u32[]{:S(2)}, u32[]{:S(2)}) %collective-permute-start.36) | collective-permute-done | bytes 131104 | tf_op jit(solution)/shard_map/ppermute | solution.py:167
  65.5 4.3 %collective-permute-done.37.refs_1_ = bf16[32,2048]{1,0:T(8,128)(2,1)S(1)} collective-permute-done((bf16[32,2048]{1,0:T(8,128)(2,1)S(1)}, bf16[32,2048]{1,0:T(8,128)(2,1)S(1)}, u32[]{:S(2)}, u32[]{:S(2)}) %collective-permute-start.37) | collective-permute-done | bytes 131104 | tf_op jit(solution)/shard_map/ppermute | solution.py:167
  (83 shorter events, 16.3 us)
Async XLA Ops:
  0.6 7.9 %collective-permute-start.2 = (bf16[128,128]{1,0:T(8,128)(2,1)}, bf16[128,128]{1,0:T(8,128)(2,1)S(1)}, u32[]{:S(2)}, u32[]{:S(2)}) collective-permute-start(bf16[128,128]{1,0:T(8,128)(2,1)} %refs_1_.1), channel_id=1, source_target_pairs={{0,4},{4,0},{8,12},{12,8},{1,5},{5,1},{9,13},{13,9},{2,6},{6,2},{1... | collective-permute-start | bytes 98312 | tf_op jit(solution)/shard_map/ppermute | solution.py:167
  1.1 5.9 %collective-permute-start = (bf16[128,128]{1,0:T(8,128)(2,1)}, bf16[128,128]{1,0:T(8,128)(2,1)S(1)}, u32[]{:S(2)}, u32[]{:S(2)}) collective-permute-start(bf16[128,128]{1,0:T(8,128)(2,1)} %refs_1_.1), channel_id=1, source_target_pairs={{0,8},{4,12},{8,0},{12,4},{1,9},{5,13},{9,1},{13,5},{2,10},{6,14},... | collective-permute-start | bytes 98312 | tf_op jit(solution)/shard_map/ppermute | solution.py:167
  3.7 4.8 %collective-permute-start.4 = (bf16[128,128]{1,0:T(8,128)(2,1)}, bf16[128,128]{1,0:T(8,128)(2,1)S(1)}, u32[]{:S(2)}, u32[]{:S(2)}) collective-permute-start(bf16[128,128]{1,0:T(8,128)(2,1)} %refs_2_.1), channel_id=1, source_target_pairs={{0,4},{4,0},{8,12},{12,8},{1,5},{5,1},{9,13},{13,9},{2,6},{6,2},{1... | collective-permute-start | bytes 98312 | tf_op jit(solution)/shard_map/ppermute | solution.py:167
  11.2 12.9 %collective-permute-start.9 = (bf16[32,2048]{1,0:T(8,128)(2,1)S(1)}, bf16[32,2048]{1,0:T(8,128)(2,1)S(1)}, u32[]{:S(2)}, u32[]{:S(2)}) collective-permute-start(bf16[32,2048]{1,0:T(8,128)(2,1)S(1)} %get-tuple-element.81), channel_id=1, source_target_pairs={{0,2},{1,3},{2,0},{3,1},{4,6},{5,7},{6,4},{7,5},{8,10},{9,11},{10,... | collective-permute-start | bytes 393224 | tf_op jit(solution)/shard_map/ppermute | solution.py:167
  13.8 10.3 %collective-permute-start.10 = (bf16[32,2048]{1,0:T(8,128)(2,1)S(1)}, bf16[32,2048]{1,0:T(8,128)(2,1)S(1)}, u32[]{:S(2)}, u32[]{:S(2)}) collective-permute-start(bf16[32,2048]{1,0:T(8,128)(2,1)S(1)} %get-tuple-element.82), channel_id=1, source_target_pairs={{0,3},{1,2},{2,1},{3,0},{4,7},{5,6},{6,5},{7,4},{8,11},{9,10},{10,... | collective-permute-start | bytes 393224 | tf_op jit(solution)/shard_map/ppermute | solution.py:167
  15.1 9.7 %collective-permute-start.11 = (bf16[32,2048]{1,0:T(8,128)(2,1)S(1)}, bf16[32,2048]{1,0:T(8,128)(2,1)S(1)}, u32[]{:S(2)}, u32[]{:S(2)}) collective-permute-start(bf16[32,2048]{1,0:T(8,128)(2,1)S(1)} %get-tuple-element.83), channel_id=1, source_target_pairs={{0,1},{1,0},{2,3},{3,2},{4,5},{5,4},{6,7},{7,6},{8,9},{9,8},{10,11... | collective-permute-start | bytes 393224 | tf_op jit(solution)/shard_map/ppermute | solution.py:167
  25.0 8.8 %collective-permute-start.13 = (bf16[32,2048]{1,0:T(8,128)(2,1)S(1)}, bf16[32,2048]{1,0:T(8,128)(2,1)S(1)}, u32[]{:S(2)}, u32[]{:S(2)}) collective-permute-start(bf16[32,2048]{1,0:T(8,128)(2,1)S(1)} %get-tuple-element.108.refs_0_), channel_id=1, source_target_pairs={{0,1},{1,0},{2,3},{3,2},{4,5},{5,4},{6,7},{7,6},{8,9},{9,8},{10,11... | collective-permute-start | bytes 393224 | tf_op jit(solution)/shard_map/ppermute | solution.py:167
  27.3 7.4 %collective-permute-start.15 = (bf16[32,2048]{1,0:T(8,128)(2,1)S(1)}, bf16[32,2048]{1,0:T(8,128)(2,1)S(1)}, u32[]{:S(2)}, u32[]{:S(2)}) collective-permute-start(bf16[32,2048]{1,0:T(8,128)(2,1)S(1)} %get-tuple-element.108.refs_0_), channel_id=1, source_target_pairs={{0,2},{1,3},{2,0},{3,1},{4,6},{5,7},{6,4},{7,5},{8,10},{9,11},{10,... | collective-permute-start | bytes 393224 | tf_op jit(solution)/shard_map/ppermute | solution.py:167
  29.3 9.1 %collective-permute-start.12 = (bf16[32,2048]{1,0:T(8,128)(2,1)S(1)}, bf16[32,2048]{1,0:T(8,128)(2,1)S(1)}, u32[]{:S(2)}, u32[]{:S(2)}) collective-permute-start(bf16[32,2048]{1,0:T(8,128)(2,1)S(1)} %get-tuple-element.108.refs_0_), channel_id=1, source_target_pairs={{0,8},{4,12},{8,0},{12,4},{1,9},{5,13},{9,1},{13,5},{2,10},{6,14},... | collective-permute-start | bytes 393224 | tf_op jit(solution)/shard_map/ppermute | solution.py:167
  33.8 5.0 %collective-permute-start.14 = (bf16[32,2048]{1,0:T(8,128)(2,1)S(1)}, bf16[32,2048]{1,0:T(8,128)(2,1)S(1)}, u32[]{:S(2)}, u32[]{:S(2)}) collective-permute-start(bf16[32,2048]{1,0:T(8,128)(2,1)S(1)} %collective-permute-done.13.refs_0_), channel_id=1, source_target_pairs={{0,8},{4,12},{8,0},{12,4},{1,9},{5,13},{9,1},{13,5},{2,10},{6,14},... | collective-permute-start | bytes 393224 | tf_op jit(solution)/shard_map/ppermute | solution.py:167
  34.7 5.5 %collective-permute-start.19 = (bf16[32,2048]{1,0:T(8,128)(2,1)S(1)}, bf16[32,2048]{1,0:T(8,128)(2,1)S(1)}, u32[]{:S(2)}, u32[]{:S(2)}) collective-permute-start(bf16[32,2048]{1,0:T(8,128)(2,1)S(1)} %collective-permute-done.15.refs_4_), channel_id=1, source_target_pairs={{0,8},{4,12},{8,0},{12,4},{1,9},{5,13},{9,1},{13,5},{2,10},{6,14},... | collective-permute-start | bytes 393224 | tf_op jit(solution)/shard_map/ppermute | solution.py:167
  35.8 5.5 %collective-permute-start.21 = (bf16[32,2048]{1,0:T(8,128)(2,1)S(1)}, bf16[32,2048]{1,0:T(8,128)(2,1)S(1)}, u32[]{:S(2)}, u32[]{:S(2)}) collective-permute-start(bf16[32,2048]{1,0:T(8,128)(2,1)S(1)} %collective-permute-done.15.refs_4_), channel_id=1, source_target_pairs={{0,1},{1,0},{2,3},{3,2},{4,5},{5,4},{6,7},{7,6},{8,9},{9,8},{10,11... | collective-permute-start | bytes 393224 | tf_op jit(solution)/shard_map/ppermute | solution.py:167
  41.3 5.0 %collective-permute-start.23 = (bf16[32,2048]{1,0:T(8,128)(2,1)S(1)}, bf16[32,2048]{1,0:T(8,128)(2,1)S(1)}, u32[]{:S(2)}, u32[]{:S(2)}) collective-permute-start(bf16[32,2048]{1,0:T(8,128)(2,1)S(1)} %collective-permute-done.21.refs_4_), channel_id=1, source_target_pairs={{0,8},{4,12},{8,0},{12,4},{1,9},{5,13},{9,1},{13,5},{2,10},{6,14},... | collective-permute-start | bytes 393224 | tf_op jit(solution)/shard_map/ppermute | solution.py:167
  47.3 5.5 %collective-permute-start.30 = (bf16[32,2048]{1,0:T(8,128)(2,1)S(1)}, bf16[32,2048]{1,0:T(8,128)(2,1)S(1)}, u32[]{:S(2)}, u32[]{:S(2)}) collective-permute-start(bf16[32,2048]{1,0:T(8,128)(2,1)S(1)} %shard_map.117), channel_id=1, source_target_pairs={{0,8},{4,12},{8,0},{12,4},{1,9},{5,13},{9,1},{13,5},{2,10},{6,14},... | collective-permute-start | bytes 393224 | tf_op jit(solution)/shard_map/ppermute | solution.py:167
  51.0 5.6 %collective-permute-start.32 = (bf16[32,2048]{1,0:T(8,128)(2,1)S(1)}, bf16[32,2048]{1,0:T(8,128)(2,1)S(1)}, u32[]{:S(2)}, u32[]{:S(2)}) collective-permute-start(bf16[32,2048]{1,0:T(8,128)(2,1)S(1)} %get-tuple-element.123), channel_id=1, source_target_pairs={{0,4},{4,0},{8,12},{12,8},{1,5},{5,1},{9,13},{13,9},{2,6},{6,2},{1... | collective-permute-start | bytes 393224 | tf_op jit(solution)/shard_map/ppermute | solution.py:167
  51.1 6.6 %collective-permute-start.40 = (bf16[32,2048]{1,0:T(8,128)(2,1)S(1)}, bf16[32,2048]{1,0:T(8,128)(2,1)S(1)}, u32[]{:S(2)}, u32[]{:S(2)}) collective-permute-start(bf16[32,2048]{1,0:T(8,128)(2,1)S(1)} %get-tuple-element.132), channel_id=1, source_target_pairs={{0,4},{4,0},{8,12},{12,8},{1,5},{5,1},{9,13},{13,9},{2,6},{6,2},{1... | collective-permute-start | bytes 393224 | tf_op jit(solution)/shard_map/ppermute | solution.py:167
  52.9 5.0 %collective-permute-start.35 = (bf16[32,2048]{1,0:T(8,128)(2,1)S(1)}, bf16[32,2048]{1,0:T(8,128)(2,1)S(1)}, u32[]{:S(2)}, u32[]{:S(2)}) collective-permute-start(bf16[32,2048]{1,0:T(8,128)(2,1)S(1)} %shard_map.120), channel_id=1, source_target_pairs={{0,8},{4,12},{8,0},{12,4},{1,9},{5,13},{9,1},{13,5},{2,10},{6,14},... | collective-permute-start | bytes 393224 | tf_op jit(solution)/shard_map/ppermute | solution.py:167
  54.1 10.0 %collective-permute-start.36 = (bf16[32,2048]{1,0:T(8,128)(2,1)S(1)}, bf16[32,2048]{1,0:T(8,128)(2,1)S(1)}, u32[]{:S(2)}, u32[]{:S(2)}) collective-permute-start(bf16[32,2048]{1,0:T(8,128)(2,1)S(1)} %shard_map.119), channel_id=1, source_target_pairs={{0,2},{1,3},{2,0},{3,1},{4,6},{5,7},{6,4},{7,5},{8,10},{9,11},{10,... | collective-permute-start | bytes 393224 | tf_op jit(solution)/shard_map/ppermute | solution.py:167
  56.7 7.4 %collective-permute-start.33 = (bf16[32,2048]{1,0:T(8,128)(2,1)S(1)}, bf16[32,2048]{1,0:T(8,128)(2,1)S(1)}, u32[]{:S(2)}, u32[]{:S(2)}) collective-permute-start(bf16[32,2048]{1,0:T(8,128)(2,1)S(1)} %shard_map.121), channel_id=1, source_target_pairs={{0,8},{4,12},{8,0},{12,4},{1,9},{5,13},{9,1},{13,5},{2,10},{6,14},... | collective-permute-start | bytes 393224 | tf_op jit(solution)/shard_map/ppermute | solution.py:167
  57.6 6.5 %collective-permute-start.22 = (bf16[32,2048]{1,0:T(8,128)(2,1)S(1)}, bf16[32,2048]{1,0:T(8,128)(2,1)S(1)}, u32[]{:S(2)}, u32[]{:S(2)}) collective-permute-start(bf16[32,2048]{1,0:T(8,128)(2,1)S(1)} %get-tuple-element.98), channel_id=1, source_target_pairs={{0,4},{4,0},{8,12},{12,8},{1,5},{5,1},{9,13},{13,9},{2,6},{6,2},{1... | collective-permute-start | bytes 393224 | tf_op jit(solution)/shard_map/ppermute | solution.py:167
  57.9 7.5 %collective-permute-start.39 = (bf16[32,2048]{1,0:T(8,128)(2,1)S(1)}, bf16[32,2048]{1,0:T(8,128)(2,1)S(1)}, u32[]{:S(2)}, u32[]{:S(2)}) collective-permute-start(bf16[32,2048]{1,0:T(8,128)(2,1)S(1)} %get-tuple-element.129), channel_id=1, source_target_pairs={{0,4},{4,0},{8,12},{12,8},{1,5},{5,1},{9,13},{13,9},{2,6},{6,2},{1... | collective-permute-start | bytes 393224 | tf_op jit(solution)/shard_map/ppermute | solution.py:167
  58.3 11.5 %collective-permute-start.38 = (bf16[32,2048]{1,0:T(8,128)(2,1)S(1)}, bf16[32,2048]{1,0:T(8,128)(2,1)S(1)}, u32[]{:S(2)}, u32[]{:S(2)}) collective-permute-start(bf16[32,2048]{1,0:T(8,128)(2,1)S(1)} %shard_map.122), channel_id=1, source_target_pairs={{0,3},{1,2},{2,1},{3,0},{4,7},{5,6},{6,5},{7,4},{8,11},{9,10},{10,... | collective-permute-start | bytes 393224 | tf_op jit(solution)/shard_map/ppermute | solution.py:167
  64.2 5.6 %collective-permute-start.37 = (bf16[32,2048]{1,0:T(8,128)(2,1)S(1)}, bf16[32,2048]{1,0:T(8,128)(2,1)S(1)}, u32[]{:S(2)}, u32[]{:S(2)}) collective-permute-start(bf16[32,2048]{1,0:T(8,128)(2,1)S(1)} %shard_map.123), channel_id=1, source_target_pairs={{0,1},{1,0},{2,3},{3,2},{4,5},{5,4},{6,7},{7,6},{8,9},{9,8},{10,11... | collective-permute-start | bytes 393224 | tf_op jit(solution)/shard_map/ppermute | solution.py:167
  64.5 5.3 %collective-permute-start.41 = (bf16[32,2048]{1,0:T(8,128)(2,1)S(1)}, bf16[32,2048]{1,0:T(8,128)(2,1)S(1)}, u32[]{:S(2)}, u32[]{:S(2)}) collective-permute-start(bf16[32,2048]{1,0:T(8,128)(2,1)S(1)} %shard_map.124), channel_id=1, source_target_pairs={{0,8},{4,12},{8,0},{12,4},{1,9},{5,13},{9,1},{13,5},{2,10},{6,14},... | collective-permute-start | bytes 393224 | tf_op jit(solution)/shard_map/ppermute | solution.py:167
  (23 other events, 115.5 us)

commit v5 on v4

--- a/solution.py
+++ b/solution.py
@@ -183,9 +183,35 @@
     )(*operands)
 
 
-def own_block_kernel(tp_count, *refs):
-    sources, (q_ref, max_ref, total_ref, acc_ref, *mix_refs) = refs[:5], refs[5:-5]
-    k_ref, v_ref, ids_ref, weights_ref, arrived = refs[-5:]
+def own_heads(heads, q_ref, k_ref, v_ref, max_ref, total_ref, acc_ref):
+    block_rows = q_ref.shape[0]
+    group_size = q_ref.shape[1] // k_ref.shape[1]
+    key_pos = lax.broadcasted_iota(jnp.int32, (block_rows, block_rows), 0)
+    query_pos = lax.broadcasted_iota(jnp.int32, (block_rows, block_rows), 1)
+    value_cols = {}
+    for i, h in enumerate(heads):
+        kv_lanes = slice(h // group_size * HEAD, (h // group_size + 1) * HEAD)
+        if h // group_size not in value_cols:
+            value_cols[h // group_size] = v_ref[:, kv_lanes].astype(F32).T.astype(BF16)
+        scores = lax.dot_general(
+            k_ref[:, kv_lanes],
+            q_ref[:, h * HEAD : (h + 1) * HEAD],
+            (((1,), (1,)), ((), ())),
+            preferred_element_type=F32,
+        )
+        scores = jnp.where(key_pos <= query_pos, scores * HEAD ** (-0.5), HIDDEN_SCORE)
+        top = jnp.max(scores, axis=0, keepdims=True)
+        weights = jnp.exp(scores - top)
+        max_ref[i : i + 1, :] = top
+        total_ref[i : i + 1, :] = jnp.sum(weights, axis=0, keepdims=True)
+        acc_ref[i] = jnp.dot(
+            value_cols[h // group_size], weights.astype(BF16), preferred_element_type=F32
+        )
+
+
+def first_kernel(tp_count, heads, *refs):
+    sources, (q_ref, k_ref, v_ref, max_ref, total_ref, acc_ref, *mix_refs) = refs[:5], refs[5:-3]
+    ids_ref, weights_ref, arrived = refs[-3:]
     targets = (q_ref, k_ref, v_ref, ids_ref, weights_ref)
     copies = [
         pltpu.make_async_copy(source, target, arrived.at[i])
@@ -196,25 +222,7 @@
     for copy in copies:
         copy.wait()
     ctx_index, tp_index = lax.axis_index("ctx"), lax.axis_index("tp")
-    block_rows = q_ref.shape[0]
-    kv_local = k_ref.shape[1] // HEAD
-    group_size = q_ref.shape[1] // k_ref.shape[1]
-    key_pos = lax.broadcasted_iota(jnp.int32, (block_rows, block_rows), 0)
-    query_pos = lax.broadcasted_iota(jnp.int32, (block_rows, block_rows), 1)
-    for g in range(kv_local):
-        key_rows = k_ref[:, g * HEAD : (g + 1) * HEAD]
-        value_cols = v_ref[:, g * HEAD : (g + 1) * HEAD].astype(F32).T.astype(BF16)
-        for h in range(g * group_size, (g + 1) * group_size):
-            lanes = slice(h * HEAD, (h + 1) * HEAD)
-            scores = lax.dot_general(
-                key_rows, q_ref[:, lanes], (((1,), (1,)), ((), ())), preferred_element_type=F32
-            )
-            scores = jnp.where(key_pos <= query_pos, scores * HEAD ** (-0.5), HIDDEN_SCORE)
-            top = jnp.max(scores, axis=0, keepdims=True)
-            weights = jnp.exp(scores - top)
-            max_ref[h : h + 1, :] = top
-            total_ref[h : h + 1, :] = jnp.sum(weights, axis=0, keepdims=True)
-            acc_ref[h] = jnp.dot(value_cols, weights.astype(BF16), preferred_element_type=F32)
+    own_heads(heads, q_ref, k_ref, v_ref, max_ref, total_ref, acc_ref)
     share = weights_ref[...] / jnp.sum(weights_ref[...], axis=0, keepdims=True)
     for d, mix_ref in enumerate(mix_refs):
         expert = (ctx_index ^ d) * tp_count + tp_index
@@ -222,9 +230,10 @@
 
 
 def other_blocks_kernel(tp_count, others, *refs):
-    w_ref, q_ref, max_ref, total_ref, acc_ref = refs[:5]
-    k_refs, v_refs = refs[5 : 5 + others], refs[5 + others : 5 + 2 * others]
-    att_ref, *piece_refs = refs[5 + 2 * others : -1]
+    w_ref, q_ref = refs[:2]
+    states = (refs[2:5], refs[5:8])
+    k_refs, v_refs = refs[8 : 8 + others], refs[8 + others : 8 + 2 * others]
+    att_ref, *piece_refs = refs[8 + 2 * others : -1]
     scratch = refs[-1]
     ctx_index, tp_index = lax.axis_index("ctx"), lax.axis_index("tp")
     block_rows = q_ref.shape[0]
@@ -245,17 +254,20 @@
             )
             scores = jnp.concatenate(
                 [
-                    scores[i * block_rows : (i + 1) * block_rows] * HEAD ** (-0.5) + hide[i]
-                    for i in range(others)
+                    scores[j * block_rows : (j + 1) * block_rows] * HEAD ** (-0.5) + hide[j]
+                    for j in range(others)
                 ],
                 axis=0,
             )
-            old = max_ref[h : h + 1, :]
+            half = states[0][0].shape[0]
+            max_ref, total_ref, acc_ref = states[h // half]
+            i = h % half
+            old = max_ref[i : i + 1, :]
             top = jnp.maximum(old, jnp.max(scores, axis=0, keepdims=True))
             weights = jnp.exp(scores - top)
             rescale = jnp.exp(old - top)
-            total = total_ref[h : h + 1, :] * rescale + jnp.sum(weights, axis=0, keepdims=True)
-            accum = acc_ref[h] * rescale + jnp.dot(
+            total = total_ref[i : i + 1, :] * rescale + jnp.sum(weights, axis=0, keepdims=True)
+            accum = acc_ref[i] * rescale + jnp.dot(
                 value_cols, weights.astype(BF16), preferred_element_type=F32
             )
             att_ref[:, lanes] = (accum * (1.0 / total)).T.astype(BF16)
@@ -324,16 +336,15 @@
 
     far_k, far_v = swap(keys, "ctx", 2), swap(values, "ctx", 2)
     near_k, near_v = swap(keys, "ctx", 1), swap(values, "ctx", 1)
-    queries, top, total, accum, *mixes = call(
-        functools.partial(own_block_kernel, tp_count),
-        [shape((block_rows, width), BF16)]
-        + [shape((heads, block_rows), F32)] * 2
-        + [shape((heads, HEAD, block_rows), F32)]
+    half = heads // 2
+    state = [shape((half, block_rows), F32)] * 2 + [shape((half, HEAD, block_rows), F32)]
+    q, k, v, *found = call(
+        functools.partial(first_kernel, tp_count, range(half)),
+        [shape((block_rows, width), BF16), shape(keys.shape, BF16), shape(values.shape, BF16)]
+        + state
         + [shape((1, block_rows), F32)] * ctx_count,
         (queries, keys, values, expert_ids.T, route_weights.T),
         scratch=[
-            pltpu.VMEM(keys.shape, BF16),
-            pltpu.VMEM(values.shape, BF16),
             pltpu.VMEM(expert_ids.T.shape, jnp.int32),
             pltpu.VMEM(route_weights.T.shape, F32),
             pltpu.SemaphoreType.DMA((5,)),
@@ -341,7 +352,9 @@
         flops=5 * 10**9,
         from_hbm=5,
     )
-    far_k, far_v, top = lax.optimization_barrier((far_k, far_v, top))
+    first, mixes = found[:3], found[3:]
+    far_k, far_v, first[0] = lax.optimization_barrier((far_k, far_v, first[0]))
+    second = call(functools.partial(own_heads, range(half, heads)), state, (q, k, v))
     ks = [near_k, far_k, swap(far_k, "ctx", 1)]
     vs = [near_v, far_v, swap(far_v, "ctx", 1)]
     piece = shape((piece_rows, features), BF16)
@@ -349,7 +362,7 @@
     attended, *partials = call(
         functools.partial(other_blocks_kernel, tp_count, ctx_count - 1),
         [shape((block_rows, width), BF16), piece32] + [piece] * (tp_count - 1),
-        (out_weight, queries, top, total, accum, *ks, *vs),
+        (out_weight, q, *first, *second, *ks, *vs),
         scratch=[pltpu.VMEM((block_rows, features), F32)],
     )
 

time: 70.7 us -> 70.7 us (level)
    pallas_call x13 -> x14, Pallas kernels: 9.64 us -> 9.75 us  [call(): pl.pallas_call(kernel, out_shape=outs, in_specs=[HBM_SPEC] * from_hbm + [...]
  transfers between devices with their start and end apart: 42 -> 42, of which waited for: 17 -> 15; matrix products, arithmetic and copies ran while one was open for 0% -> 0% of each run, Pallas kernels for 10% -> 10%
where the time goes in v5:
time: 70.7 us; the launch traced here: 70.5 us
  starting transfers between devices  34.7 us (49%)
  waiting for transfers between devices  25.2 us (36%)
  Pallas kernels  9.75 us (14%)
  between operations  0.88 us (1%)
    ppermute x42, starting transfers between devices, swap(): return lax.ppermute(rows, axis, [(i, i ^ offset) for i in range(count)])  34.7 us
    ppermute x42, waiting for transfers between devices, swap(): return lax.ppermute(rows, axis, [(i, i ^ offset) for i in range(count)])  25.2 us
    pallas_call x14, Pallas kernels, call(): pl.pallas_call(kernel, out_shape=outs, in_specs=[HBM_SPEC] * from_hbm + [...  9.75 us
  transfers between devices with their start and end apart: 42, of which 15 were waited for; matrix products, arithmetic and copies ran while one was open for 0% of the time, Pallas kernels for 10%

profile of v5, /device:TPU:0, one launch (start us, length us, event | category | flops | bytes accessed | tf_op | source)
XLA Modules:
  0.0 70.5 jit_solution(7250059547534637809)
XLA Ops:
  1.1 2.6 %collective-permute-start = (bf16[128,128]{1,0:T(8,128)(2,1)}, bf16[128,128]{1,0:T(8,128)(2,1)S(1)}, u32[]{:S(2)}, u32[]{:S(2)}) collective-permute-start(bf16[128,128]{1,0:T(8,128)(2,1)} %refs_1_.1), channel_id=1, source_target_pairs={{0,8},{4,12},{8,0},{12,4},{1,9},{5,13},{9,1},{13,5},{2,10},{6,14},... | collective-permute-start | bytes 98312 | tf_op jit(solution)/shard_map/ppermute | solution.py:167
  4.2 2.1 %shard_map.113 = (bf16[128,1024]{1,0:T(8,128)(2,1)S(1)}, bf16[128,128]{1,0:T(8,128)(2,1)S(1)}, bf16[128,128]{1,0:T(8,128)(2,1)S(1)}, f32[4,128]{1,0:T(4,128)S(1)...) custom-call(bf16[128,1024]{1,0:T(8,128)(2,1)} %refs_0_.2, ...), custom_call_target="tpu_custom_call" | custom-call | flops 5000000000 | bytes 1024 | tf_op jit(solution)/shard_map/pallas_call | solution.py:175
  6.3 1.7 %collective-permute-done.1.refs_12_ = bf16[128,128]{1,0:T(8,128)(2,1)S(1)} collective-permute-done((bf16[128,128]{1,0:T(8,128)(2,1)}, bf16[128,128]{1,0:T(8,128)(2,1)S(1)}, u32[]{:S(2)}, u32[]{:S(2)}) %collective-permute-start.1) | collective-permute-done | bytes 32800 | tf_op jit(solution)/shard_map/ppermute | solution.py:167
  9.6 1.8 %shard_map.115 = (bf16[128,1024]{1,0:T(8,128)(2,1)}, f32[32,2048]{1,0:T(8,128)S(1)}, bf16[32,2048]{1,0:T(8,128)(2,1)S(1)}, bf16[32,2048]{1,0:T(8,128)(2,1)S(1)}, bf16[32,2048]{1,0:T(8,128)(2,1)S(1)}) custom-call(bf16[1024,2048]{1,0:T(8,128)(2,1)S(1)} %copy-done.3, bf16[128,1024]{1,0:T(8,128)(2,1)S(1)} %get-tuple-element.73.q_ref.refs_1_, ...), custom_call_target="tpu_custom_call" | custom-call | flops 1024 | bytes 1024 | tf_op jit(solution)/shard_map/pallas_call | solution.py:175
  11.3 2.6 %collective-permute-start.9 = (bf16[32,2048]{1,0:T(8,128)(2,1)S(1)}, bf16[32,2048]{1,0:T(8,128)(2,1)S(1)}, u32[]{:S(2)}, u32[]{:S(2)}) collective-permute-start(bf16[32,2048]{1,0:T(8,128)(2,1)S(1)} %get-tuple-element.91), channel_id=1, source_target_pairs={{0,2},{1,3},{2,0},{3,1},{4,6},{5,7},{6,4},{7,5},{8,10},{9,11},{10,... | collective-permute-start | bytes 393224 | tf_op jit(solution)/shard_map/ppermute | solution.py:167
  13.9 1.3 %collective-permute-start.10 = (bf16[32,2048]{1,0:T(8,128)(2,1)S(1)}, bf16[32,2048]{1,0:T(8,128)(2,1)S(1)}, u32[]{:S(2)}, u32[]{:S(2)}) collective-permute-start(bf16[32,2048]{1,0:T(8,128)(2,1)S(1)} %get-tuple-element.92), channel_id=1, source_target_pairs={{0,3},{1,2},{2,1},{3,0},{4,7},{5,6},{6,5},{7,4},{8,11},{9,10},{10,... | collective-permute-start | bytes 393224 | tf_op jit(solution)/shard_map/ppermute | solution.py:167
  17.4 1.7 %collective-permute-done.7.refs_2_ = f32[1,128]{1,0:T(1,128)S(1)} collective-permute-done((f32[1,128]{1,0:T(1,128)S(1)}, f32[1,128]{1,0:T(1,128)S(1)}, u32[]{:S(2)}, u32[]{:S(2)}) %collective-permute-start.7) | collective-permute-done | bytes 544 | tf_op jit(solution)/shard_map/ppermute | solution.py:167
  19.6 4.6 %collective-permute-done.9.refs_5_ = bf16[32,2048]{1,0:T(8,128)(2,1)S(1)} collective-permute-done((bf16[32,2048]{1,0:T(8,128)(2,1)S(1)}, bf16[32,2048]{1,0:T(8,128)(2,1)S(1)}, u32[]{:S(2)}, u32[]{:S(2)}) %collective-permute-start.9) | collective-permute-done | bytes 131104 | tf_op jit(solution)/shard_map/ppermute | solution.py:167
  25.0 2.2 %collective-permute-start.13 = (bf16[32,2048]{1,0:T(8,128)(2,1)S(1)}, bf16[32,2048]{1,0:T(8,128)(2,1)S(1)}, u32[]{:S(2)}, u32[]{:S(2)}) collective-permute-start(bf16[32,2048]{1,0:T(8,128)(2,1)S(1)} %get-tuple-element.118.refs_0_), channel_id=1, source_target_pairs={{0,1},{1,0},{2,3},{3,2},{4,5},{5,4},{6,7},{7,6},{8,9},{9,8},{10,11... | collective-permute-start | bytes 393224 | tf_op jit(solution)/shard_map/ppermute | solution.py:167
  27.3 2.0 %collective-permute-start.15 = (bf16[32,2048]{1,0:T(8,128)(2,1)S(1)}, bf16[32,2048]{1,0:T(8,128)(2,1)S(1)}, u32[]{:S(2)}, u32[]{:S(2)}) collective-permute-start(bf16[32,2048]{1,0:T(8,128)(2,1)S(1)} %get-tuple-element.118.refs_0_), channel_id=1, source_target_pairs={{0,2},{1,3},{2,0},{3,1},{4,6},{5,7},{6,4},{7,5},{8,10},{9,11},{10,... | collective-permute-start | bytes 393224 | tf_op jit(solution)/shard_map/ppermute | solution.py:167
  29.8 4.0 %collective-permute-done.13.refs_0_ = bf16[32,2048]{1,0:T(8,128)(2,1)S(1)} collective-permute-done((bf16[32,2048]{1,0:T(8,128)(2,1)S(1)}, bf16[32,2048]{1,0:T(8,128)(2,1)S(1)}, u32[]{:S(2)}, u32[]{:S(2)}) %collective-permute-start.13) | collective-permute-done | bytes 131104 | tf_op jit(solution)/shard_map/ppermute | solution.py:167
  34.3 1.5 %collective-permute-start.19 = (bf16[32,2048]{1,0:T(8,128)(2,1)S(1)}, bf16[32,2048]{1,0:T(8,128)(2,1)S(1)}, u32[]{:S(2)}, u32[]{:S(2)}) collective-permute-start(bf16[32,2048]{1,0:T(8,128)(2,1)S(1)} %collective-permute-done.15.refs_4_), channel_id=1, source_target_pairs={{0,8},{4,12},{8,0},{12,4},{1,9},{5,13},{9,1},{13,5},{2,10},{6,14},... | collective-permute-start | bytes 393224 | tf_op jit(solution)/shard_map/ppermute | solution.py:167
  35.8 2.2 %collective-permute-start.21 = (bf16[32,2048]{1,0:T(8,128)(2,1)S(1)}, bf16[32,2048]{1,0:T(8,128)(2,1)S(1)}, u32[]{:S(2)}, u32[]{:S(2)}) collective-permute-start(bf16[32,2048]{1,0:T(8,128)(2,1)S(1)} %collective-permute-done.15.refs_4_), channel_id=1, source_target_pairs={{0,1},{1,0},{2,3},{3,2},{4,5},{5,4},{6,7},{7,6},{8,9},{9,8},{10,11... | collective-permute-start | bytes 393224 | tf_op jit(solution)/shard_map/ppermute | solution.py:167
  38.7 1.4 %collective-permute-done.19.refs_6_ = bf16[32,2048]{1,0:T(8,128)(2,1)S(1)} collective-permute-done((bf16[32,2048]{1,0:T(8,128)(2,1)S(1)}, bf16[32,2048]{1,0:T(8,128)(2,1)S(1)}, u32[]{:S(2)}, u32[]{:S(2)}) %collective-permute-start.19) | collective-permute-done | bytes 131104 | tf_op jit(solution)/shard_map/ppermute | solution.py:167
  40.9 1.5 %collective-permute-start.23 = (bf16[32,2048]{1,0:T(8,128)(2,1)S(1)}, bf16[32,2048]{1,0:T(8,128)(2,1)S(1)}, u32[]{:S(2)}, u32[]{:S(2)}) collective-permute-start(bf16[32,2048]{1,0:T(8,128)(2,1)S(1)} %collective-permute-done.21.refs_4_), channel_id=1, source_target_pairs={{0,8},{4,12},{8,0},{12,4},{1,9},{5,13},{9,1},{13,5},{2,10},{6,14},... | collective-permute-start | bytes 393224 | tf_op jit(solution)/shard_map/ppermute | solution.py:167
  42.4 1.9 %shard_map.117 = (f32[32,2048]{1,0:T(8,128)S(1)}, bf16[32,2048]{1,0:T(8,128)(2,1)S(1)}, f32[32,2048]{1,0:T(8,128)S(1)}, bf16[32,2048]{1,0:T(8,128)(2,1)S(1)}, f3...) custom-call(bf16[32,2048]{1,0:T(8,128)(2,1)S(1)} %collective-permute, ...), custom_call_target="tpu_custom_call" | custom-call | flops 1024 | bytes 1024 | tf_op jit(solution)/shard_map/pallas_call | solution.py:175
  44.4 1.7 %collective-permute-done.23.refs_6_ = bf16[32,2048]{1,0:T(8,128)(2,1)S(1)} collective-permute-done((bf16[32,2048]{1,0:T(8,128)(2,1)S(1)}, bf16[32,2048]{1,0:T(8,128)(2,1)S(1)}, u32[]{:S(2)}, u32[]{:S(2)}) %collective-permute-start.23) | collective-permute-done | bytes 131104 | tf_op jit(solution)/shard_map/ppermute | solution.py:167
  47.1 1.4 %collective-permute-start.30 = (bf16[32,2048]{1,0:T(8,128)(2,1)S(1)}, bf16[32,2048]{1,0:T(8,128)(2,1)S(1)}, u32[]{:S(2)}, u32[]{:S(2)}) collective-permute-start(bf16[32,2048]{1,0:T(8,128)(2,1)S(1)} %shard_map.118), channel_id=1, source_target_pairs={{0,8},{4,12},{8,0},{12,4},{1,9},{5,13},{9,1},{13,5},{2,10},{6,14},... | collective-permute-start | bytes 393224 | tf_op jit(solution)/shard_map/ppermute | solution.py:167
  48.5 1.9 %shard_map.119 = (f32[32,2048]{1,0:T(8,128)S(1)}, bf16[32,2048]{1,0:T(8,128)(2,1)S(1)}, f32[32,2048]{1,0:T(8,128)S(1)}, bf16[32,2048]{1,0:T(8,128)(2,1)S(1)}, f3...) custom-call(bf16[32,2048]{1,0:T(8,128)(2,1)S(1)} %get-tuple-element., ...), custom_call_target="tpu_custom_call" | custom-call | flops 1024 | bytes 1024 | tf_op jit(solution)/shard_map/pallas_call | solution.py:175
  52.7 1.4 %collective-permute-start.35 = (bf16[32,2048]{1,0:T(8,128)(2,1)S(1)}, bf16[32,2048]{1,0:T(8,128)(2,1)S(1)}, u32[]{:S(2)}, u32[]{:S(2)}) collective-permute-start(bf16[32,2048]{1,0:T(8,128)(2,1)S(1)} %shard_map.121), channel_id=1, source_target_pairs={{0,8},{4,12},{8,0},{12,4},{1,9},{5,13},{9,1},{13,5},{2,10},{6,14},... | collective-permute-start | bytes 393224 | tf_op jit(solution)/shard_map/ppermute | solution.py:167
  54.1 2.5 %collective-permute-start.36 = (bf16[32,2048]{1,0:T(8,128)(2,1)S(1)}, bf16[32,2048]{1,0:T(8,128)(2,1)S(1)}, u32[]{:S(2)}, u32[]{:S(2)}) collective-permute-start(bf16[32,2048]{1,0:T(8,128)(2,1)S(1)} %shard_map.120), channel_id=1, source_target_pairs={{0,2},{1,3},{2,0},{3,1},{4,6},{5,7},{6,4},{7,5},{8,10},{9,11},{10,... | collective-permute-start | bytes 393224 | tf_op jit(solution)/shard_map/ppermute | solution.py:167
  58.0 4.7 %collective-permute-start.38 = (bf16[32,2048]{1,0:T(8,128)(2,1)S(1)}, bf16[32,2048]{1,0:T(8,128)(2,1)S(1)}, u32[]{:S(2)}, u32[]{:S(2)}) collective-permute-start(bf16[32,2048]{1,0:T(8,128)(2,1)S(1)} %shard_map.123), channel_id=1, source_target_pairs={{0,3},{1,2},{2,1},{3,0},{4,7},{5,6},{6,5},{7,4},{8,11},{9,10},{10,... | collective-permute-start | bytes 393224 | tf_op jit(solution)/shard_map/ppermute | solution.py:167
  62.7 1.4 %collective-permute-done.36.refs_2_ = bf16[32,2048]{1,0:T(8,128)(2,1)S(1)} collective-permute-done((bf16[32,2048]{1,0:T(8,128)(2,1)S(1)}, bf16[32,2048]{1,0:T(8,128)(2,1)S(1)}, u32[]{:S(2)}, u32[]{:S(2)}) %collective-permute-start.36) | collective-permute-done | bytes 131104 | tf_op jit(solution)/shard_map/ppermute | solution.py:167
  65.4 4.3 %collective-permute-done.37.refs_1_ = bf16[32,2048]{1,0:T(8,128)(2,1)S(1)} collective-permute-done((bf16[32,2048]{1,0:T(8,128)(2,1)S(1)}, bf16[32,2048]{1,0:T(8,128)(2,1)S(1)}, u32[]{:S(2)}, u32[]{:S(2)}) %collective-permute-start.37) | collective-permute-done | bytes 131104 | tf_op jit(solution)/shard_map/ppermute | solution.py:167
  (84 shorter events, 15.3 us)
Async XLA Ops:
  0.6 8.8 %collective-permute-start.2 = (bf16[128,128]{1,0:T(8,128)(2,1)}, bf16[128,128]{1,0:T(8,128)(2,1)S(1)}, u32[]{:S(2)}, u32[]{:S(2)}) collective-permute-start(bf16[128,128]{1,0:T(8,128)(2,1)} %refs_1_.1), channel_id=1, source_target_pairs={{0,4},{4,0},{8,12},{12,8},{1,5},{5,1},{9,13},{13,9},{2,6},{6,2},{1... | collective-permute-start | bytes 98312 | tf_op jit(solution)/shard_map/ppermute | solution.py:167
  1.1 5.1 %collective-permute-start = (bf16[128,128]{1,0:T(8,128)(2,1)}, bf16[128,128]{1,0:T(8,128)(2,1)S(1)}, u32[]{:S(2)}, u32[]{:S(2)}) collective-permute-start(bf16[128,128]{1,0:T(8,128)(2,1)} %refs_1_.1), channel_id=1, source_target_pairs={{0,8},{4,12},{8,0},{12,4},{1,9},{5,13},{9,1},{13,5},{2,10},{6,14},... | collective-permute-start | bytes 98312 | tf_op jit(solution)/shard_map/ppermute | solution.py:167
  3.7 5.8 %collective-permute-start.4 = (bf16[128,128]{1,0:T(8,128)(2,1)}, bf16[128,128]{1,0:T(8,128)(2,1)S(1)}, u32[]{:S(2)}, u32[]{:S(2)}) collective-permute-start(bf16[128,128]{1,0:T(8,128)(2,1)} %refs_2_.1), channel_id=1, source_target_pairs={{0,4},{4,0},{8,12},{12,8},{1,5},{5,1},{9,13},{13,9},{2,6},{6,2},{1... | collective-permute-start | bytes 98312 | tf_op jit(solution)/shard_map/ppermute | solution.py:167
  11.3 12.9 %collective-permute-start.9 = (bf16[32,2048]{1,0:T(8,128)(2,1)S(1)}, bf16[32,2048]{1,0:T(8,128)(2,1)S(1)}, u32[]{:S(2)}, u32[]{:S(2)}) collective-permute-start(bf16[32,2048]{1,0:T(8,128)(2,1)S(1)} %get-tuple-element.91), channel_id=1, source_target_pairs={{0,2},{1,3},{2,0},{3,1},{4,6},{5,7},{6,4},{7,5},{8,10},{9,11},{10,... | collective-permute-start | bytes 393224 | tf_op jit(solution)/shard_map/ppermute | solution.py:167
  13.9 10.3 %collective-permute-start.10 = (bf16[32,2048]{1,0:T(8,128)(2,1)S(1)}, bf16[32,2048]{1,0:T(8,128)(2,1)S(1)}, u32[]{:S(2)}, u32[]{:S(2)}) collective-permute-start(bf16[32,2048]{1,0:T(8,128)(2,1)S(1)} %get-tuple-element.92), channel_id=1, source_target_pairs={{0,3},{1,2},{2,1},{3,0},{4,7},{5,6},{6,5},{7,4},{8,11},{9,10},{10,... | collective-permute-start | bytes 393224 | tf_op jit(solution)/shard_map/ppermute | solution.py:167
  15.3 9.6 %collective-permute-start.11 = (bf16[32,2048]{1,0:T(8,128)(2,1)S(1)}, bf16[32,2048]{1,0:T(8,128)(2,1)S(1)}, u32[]{:S(2)}, u32[]{:S(2)}) collective-permute-start(bf16[32,2048]{1,0:T(8,128)(2,1)S(1)} %get-tuple-element.93), channel_id=1, source_target_pairs={{0,1},{1,0},{2,3},{3,2},{4,5},{5,4},{6,7},{7,6},{8,9},{9,8},{10,11... | collective-permute-start | bytes 393224 | tf_op jit(solution)/shard_map/ppermute | solution.py:167
  25.0 8.7 %collective-permute-start.13 = (bf16[32,2048]{1,0:T(8,128)(2,1)S(1)}, bf16[32,2048]{1,0:T(8,128)(2,1)S(1)}, u32[]{:S(2)}, u32[]{:S(2)}) collective-permute-start(bf16[32,2048]{1,0:T(8,128)(2,1)S(1)} %get-tuple-element.118.refs_0_), channel_id=1, source_target_pairs={{0,1},{1,0},{2,3},{3,2},{4,5},{5,4},{6,7},{7,6},{8,9},{9,8},{10,11... | collective-permute-start | bytes 393224 | tf_op jit(solution)/shard_map/ppermute | solution.py:167
  27.3 7.0 %collective-permute-start.15 = (bf16[32,2048]{1,0:T(8,128)(2,1)S(1)}, bf16[32,2048]{1,0:T(8,128)(2,1)S(1)}, u32[]{:S(2)}, u32[]{:S(2)}) collective-permute-start(bf16[32,2048]{1,0:T(8,128)(2,1)S(1)} %get-tuple-element.118.refs_0_), channel_id=1, source_target_pairs={{0,2},{1,3},{2,0},{3,1},{4,6},{5,7},{6,4},{7,5},{8,10},{9,11},{10,... | collective-permute-start | bytes 393224 | tf_op jit(solution)/shard_map/ppermute | solution.py:167
  29.3 8.7 %collective-permute-start.12 = (bf16[32,2048]{1,0:T(8,128)(2,1)S(1)}, bf16[32,2048]{1,0:T(8,128)(2,1)S(1)}, u32[]{:S(2)}, u32[]{:S(2)}) collective-permute-start(bf16[32,2048]{1,0:T(8,128)(2,1)S(1)} %get-tuple-element.118.refs_0_), channel_id=1, source_target_pairs={{0,8},{4,12},{8,0},{12,4},{1,9},{5,13},{9,1},{13,5},{2,10},{6,14},... | collective-permute-start | bytes 393224 | tf_op jit(solution)/shard_map/ppermute | solution.py:167
  33.8 5.0 %collective-permute-start.14 = (bf16[32,2048]{1,0:T(8,128)(2,1)S(1)}, bf16[32,2048]{1,0:T(8,128)(2,1)S(1)}, u32[]{:S(2)}, u32[]{:S(2)}) collective-permute-start(bf16[32,2048]{1,0:T(8,128)(2,1)S(1)} %collective-permute-done.13.refs_0_), channel_id=1, source_target_pairs={{0,8},{4,12},{8,0},{12,4},{1,9},{5,13},{9,1},{13,5},{2,10},{6,14},... | collective-permute-start | bytes 393224 | tf_op jit(solution)/shard_map/ppermute | solution.py:167
  34.3 5.8 %collective-permute-start.19 = (bf16[32,2048]{1,0:T(8,128)(2,1)S(1)}, bf16[32,2048]{1,0:T(8,128)(2,1)S(1)}, u32[]{:S(2)}, u32[]{:S(2)}) collective-permute-start(bf16[32,2048]{1,0:T(8,128)(2,1)S(1)} %collective-permute-done.15.refs_4_), channel_id=1, source_target_pairs={{0,8},{4,12},{8,0},{12,4},{1,9},{5,13},{9,1},{13,5},{2,10},{6,14},... | collective-permute-start | bytes 393224 | tf_op jit(solution)/shard_map/ppermute | solution.py:167
  35.8 5.1 %collective-permute-start.21 = (bf16[32,2048]{1,0:T(8,128)(2,1)S(1)}, bf16[32,2048]{1,0:T(8,128)(2,1)S(1)}, u32[]{:S(2)}, u32[]{:S(2)}) collective-permute-start(bf16[32,2048]{1,0:T(8,128)(2,1)S(1)} %collective-permute-done.15.refs_4_), channel_id=1, source_target_pairs={{0,1},{1,0},{2,3},{3,2},{4,5},{5,4},{6,7},{7,6},{8,9},{9,8},{10,11... | collective-permute-start | bytes 393224 | tf_op jit(solution)/shard_map/ppermute | solution.py:167
  40.9 5.1 %collective-permute-start.23 = (bf16[32,2048]{1,0:T(8,128)(2,1)S(1)}, bf16[32,2048]{1,0:T(8,128)(2,1)S(1)}, u32[]{:S(2)}, u32[]{:S(2)}) collective-permute-start(bf16[32,2048]{1,0:T(8,128)(2,1)S(1)} %collective-permute-done.21.refs_4_), channel_id=1, source_target_pairs={{0,8},{4,12},{8,0},{12,4},{1,9},{5,13},{9,1},{13,5},{2,10},{6,14},... | collective-permute-start | bytes 393224 | tf_op jit(solution)/shard_map/ppermute | solution.py:167
  47.1 5.5 %collective-permute-start.30 = (bf16[32,2048]{1,0:T(8,128)(2,1)S(1)}, bf16[32,2048]{1,0:T(8,128)(2,1)S(1)}, u32[]{:S(2)}, u32[]{:S(2)}) collective-permute-start(bf16[32,2048]{1,0:T(8,128)(2,1)S(1)} %shard_map.118), channel_id=1, source_target_pairs={{0,8},{4,12},{8,0},{12,4},{1,9},{5,13},{9,1},{13,5},{2,10},{6,14},... | collective-permute-start | bytes 393224 | tf_op jit(solution)/shard_map/ppermute | solution.py:167
  51.0 5.6 %collective-permute-start.32 = (bf16[32,2048]{1,0:T(8,128)(2,1)S(1)}, bf16[32,2048]{1,0:T(8,128)(2,1)S(1)}, u32[]{:S(2)}, u32[]{:S(2)}) collective-permute-start(bf16[32,2048]{1,0:T(8,128)(2,1)S(1)} %get-tuple-element.133), channel_id=1, source_target_pairs={{0,4},{4,0},{8,12},{12,8},{1,5},{5,1},{9,13},{13,9},{2,6},{6,2},{1... | collective-permute-start | bytes 393224 | tf_op jit(solution)/shard_map/ppermute | solution.py:167
  51.0 6.3 %collective-permute-start.40 = (bf16[32,2048]{1,0:T(8,128)(2,1)S(1)}, bf16[32,2048]{1,0:T(8,128)(2,1)S(1)}, u32[]{:S(2)}, u32[]{:S(2)}) collective-permute-start(bf16[32,2048]{1,0:T(8,128)(2,1)S(1)} %get-tuple-element.142), channel_id=1, source_target_pairs={{0,4},{4,0},{8,12},{12,8},{1,5},{5,1},{9,13},{13,9},{2,6},{6,2},{1... | collective-permute-start | bytes 393224 | tf_op jit(solution)/shard_map/ppermute | solution.py:167
  52.7 5.1 %collective-permute-start.35 = (bf16[32,2048]{1,0:T(8,128)(2,1)S(1)}, bf16[32,2048]{1,0:T(8,128)(2,1)S(1)}, u32[]{:S(2)}, u32[]{:S(2)}) collective-permute-start(bf16[32,2048]{1,0:T(8,128)(2,1)S(1)} %shard_map.121), channel_id=1, source_target_pairs={{0,8},{4,12},{8,0},{12,4},{1,9},{5,13},{9,1},{13,5},{2,10},{6,14},... | collective-permute-start | bytes 393224 | tf_op jit(solution)/shard_map/ppermute | solution.py:167
  54.1 10.0 %collective-permute-start.36 = (bf16[32,2048]{1,0:T(8,128)(2,1)S(1)}, bf16[32,2048]{1,0:T(8,128)(2,1)S(1)}, u32[]{:S(2)}, u32[]{:S(2)}) collective-permute-start(bf16[32,2048]{1,0:T(8,128)(2,1)S(1)} %shard_map.120), channel_id=1, source_target_pairs={{0,2},{1,3},{2,0},{3,1},{4,6},{5,7},{6,4},{7,5},{8,10},{9,11},{10,... | collective-permute-start | bytes 393224 | tf_op jit(solution)/shard_map/ppermute | solution.py:167
  56.6 7.4 %collective-permute-start.33 = (bf16[32,2048]{1,0:T(8,128)(2,1)S(1)}, bf16[32,2048]{1,0:T(8,128)(2,1)S(1)}, u32[]{:S(2)}, u32[]{:S(2)}) collective-permute-start(bf16[32,2048]{1,0:T(8,128)(2,1)S(1)} %shard_map.122), channel_id=1, source_target_pairs={{0,8},{4,12},{8,0},{12,4},{1,9},{5,13},{9,1},{13,5},{2,10},{6,14},... | collective-permute-start | bytes 393224 | tf_op jit(solution)/shard_map/ppermute | solution.py:167
  57.3 6.8 %collective-permute-start.22 = (bf16[32,2048]{1,0:T(8,128)(2,1)S(1)}, bf16[32,2048]{1,0:T(8,128)(2,1)S(1)}, u32[]{:S(2)}, u32[]{:S(2)}) collective-permute-start(bf16[32,2048]{1,0:T(8,128)(2,1)S(1)} %get-tuple-element.108), channel_id=1, source_target_pairs={{0,4},{4,0},{8,12},{12,8},{1,5},{5,1},{9,13},{13,9},{2,6},{6,2},{1... | collective-permute-start | bytes 393224 | tf_op jit(solution)/shard_map/ppermute | solution.py:167
  57.8 7.6 %collective-permute-start.39 = (bf16[32,2048]{1,0:T(8,128)(2,1)S(1)}, bf16[32,2048]{1,0:T(8,128)(2,1)S(1)}, u32[]{:S(2)}, u32[]{:S(2)}) collective-permute-start(bf16[32,2048]{1,0:T(8,128)(2,1)S(1)} %get-tuple-element.139), channel_id=1, source_target_pairs={{0,4},{4,0},{8,12},{12,8},{1,5},{5,1},{9,13},{13,9},{2,6},{6,2},{1... | collective-permute-start | bytes 393224 | tf_op jit(solution)/shard_map/ppermute | solution.py:167
  58.0 11.8 %collective-permute-start.38 = (bf16[32,2048]{1,0:T(8,128)(2,1)S(1)}, bf16[32,2048]{1,0:T(8,128)(2,1)S(1)}, u32[]{:S(2)}, u32[]{:S(2)}) collective-permute-start(bf16[32,2048]{1,0:T(8,128)(2,1)S(1)} %shard_map.123), channel_id=1, source_target_pairs={{0,3},{1,2},{2,1},{3,0},{4,7},{5,6},{6,5},{7,4},{8,11},{9,10},{10,... | collective-permute-start | bytes 393224 | tf_op jit(solution)/shard_map/ppermute | solution.py:167
  64.1 5.6 %collective-permute-start.37 = (bf16[32,2048]{1,0:T(8,128)(2,1)S(1)}, bf16[32,2048]{1,0:T(8,128)(2,1)S(1)}, u32[]{:S(2)}, u32[]{:S(2)}) collective-permute-start(bf16[32,2048]{1,0:T(8,128)(2,1)S(1)} %shard_map.124), channel_id=1, source_target_pairs={{0,1},{1,0},{2,3},{3,2},{4,5},{5,4},{6,7},{7,6},{8,9},{9,8},{10,11... | collective-permute-start | bytes 393224 | tf_op jit(solution)/shard_map/ppermute | solution.py:167
  64.5 5.3 %collective-permute-start.41 = (bf16[32,2048]{1,0:T(8,128)(2,1)S(1)}, bf16[32,2048]{1,0:T(8,128)(2,1)S(1)}, u32[]{:S(2)}, u32[]{:S(2)}) collective-permute-start(bf16[32,2048]{1,0:T(8,128)(2,1)S(1)} %shard_map.125), channel_id=1, source_target_pairs={{0,8},{4,12},{8,0},{12,4},{1,9},{5,13},{9,1},{13,5},{2,10},{6,14},... | collective-permute-start | bytes 393224 | tf_op jit(solution)/shard_map/ppermute | solution.py:167
  (23 other events, 115.7 us)
